TPU v7x, 256 devices: a whole 4x4x8 slice. The times are simulated.
256 devices in a mesh: pair: 64 (over x, z, core), red: 4 (over y).
Axes of the slice: x: 4, y: 4, z: 8, core: 2. Of those that a mesh axis runs over, the one named last changes fastest.
Arguments:
- integrals: bfloat16 [2048, 64, 1536], P(('pair', 'red')), may hold values from -6 to 6
- coeffs: bfloat16 [6016, 512], replicated, may hold values from -0.078125 to 0.078125
- shell_pairs: int32 [2048, 2], replicated, may hold values from 0 to 93, as said below
- block_count: int32 [64, 4], P('pair', 'red'), may hold values from 1 to 8, as said below
Outputs:
- mo_ints: float32 [512, 24, 512], P('pair', None, 'red')
Inputs may be any that keep to these rules, and one draw needn't show every extreme that they name: `shell_pairs`: the 2048 rows are distinct shell pairs (row shell, column shell). `block_count`: some device has all 8 slots live.
All inputs are finite; a program needn't handle non-finite values.
Results may differ from a plain program's by a relative error of at most 0.0029.
Values may be sent and summed in bfloat16 or wider, within the bound.
No kernel may reach another device: no remote copies, remote signals or barrier semaphores. Data moves between devices by JAX's collectives and lax.ppermute only.
A program may use at most 128 MiB of HBM per device.

v0:
```python
import jax
import jax.numpy as jnp
from jax import lax
from jax.sharding import PartitionSpec as P


def on_device(integrals, coeffs, shell_pairs, block_count):
    slot_count = integrals.shape[0]
    shell_size = integrals.shape[1]
    ket_count = integrals.shape[2] // shell_size
    occ_count = coeffs.shape[1]
    shell_count = coeffs.shape[0] // shell_size
    pair_count = lax.axis_size("pair")
    red_count = lax.axis_size("red")
    pair_index = lax.axis_index("pair")
    red_index = lax.axis_index("red")
    owned_rows = occ_count // pair_count
    coef_table = coeffs.reshape(shell_count, shell_size, occ_count)
    first_slot = (pair_index * red_count + red_index) * slot_count
    own_pairs = lax.dynamic_slice_in_dim(shell_pairs, first_slot, slot_count, 0)
    live_mask = (jnp.arange(slot_count, dtype=jnp.int32) < block_count[0, 0]).astype(jnp.float32)
    left_panels = jnp.take(coef_table, own_pairs[:, 0], axis=0)
    half_done = jnp.einsum(
        "kmi,kmx->kix", left_panels, integrals, preferred_element_type=jnp.float32
    )
    half_done = (half_done * live_mask[:, None, None]).astype(jnp.bfloat16)
    right_panels = jnp.take(coef_table, own_pairs[:, 1], axis=0)
    whole_sum = jnp.einsum(
        "kpiqn,knrj->priqj",
        half_done.reshape(slot_count, pair_count, owned_rows, ket_count, shell_size),
        right_panels.reshape(slot_count, shell_size, red_count, occ_count // red_count),
        preferred_element_type=jnp.float32,
    )
    whole_sum = whole_sum.reshape(
        pair_count * red_count * owned_rows, ket_count, occ_count // red_count
    )
    return lax.psum_scatter(whole_sum, ("pair", "red"), scatter_dimension=0, tiled=True)


def solution(mesh):
    return jax.shard_map(
        on_device,
        mesh=mesh,
        in_specs=(P(("pair", "red"), None, None), P(), P(), P("pair", "red")),
        out_specs=P("pair", None, "red"),
        check_vma=False,
    )
```

profile of v0, /device:TPU:6, one launch (start us, length us, event | category | flops | bytes accessed | tf_op | source)
XLA Modules:
  0.0 564.4 jit_solution(9487662394370297582)
XLA Ops:
  6.5 0.0 copy-start
  6.5 0.0 reduce-scatter.2.cloned.1.call-start
  7.3 0.8 constant_dynamic-slice_fusion
  8.1 3.3 gather_fusion.1
  11.4 3.3 gather_fusion
  14.8 0.1 broadcast_select_fusion
  14.9 0.1 reshape.23
  15.0 0.0 copy-done
  15.0 6.8 %multiply_convert_fusion = bf16[8,512,1536]{2,1,0:T(8,128)(2,1)} fusion(bf16[8,64,1536]{2,1,0:T(8,128)(2,1)S(1)} %copy-done, f32[8]{0:T(128)S(1)} %compare_convert_fusion, bf16[8,64,512]{2,1,0:T(8,128)(2,1)S(1)} %gather_fusion.1, pred[8]{0:T(512)(128)(4,1)S(1)} %get-tuple-element.10), kind=kOutput, calls=%fused_computation.5 | convolution fusion | flops 818151424 | bytes 14680104 | tf_op jit(solution)/shard_map/kmi,kmx->kix/dot_general | solution.py:23
  21.8 31.0 %reshape.24 = bf16[8,64,8,24,64]{4,3,2,1,0:T(8,128)(2,1)} reshape(bf16[8,512,1536]{2,1,0:T(8,128)(2,1)} %multiply_convert_fusion) | data formatting | bytes 25165824 | tf_op jit(solution)/shard_map/reshape | solution.py:30
  52.8 27.4 %fusion.3 = f32[64,4,8,24,128]{4,0,3,2,1:T(8,128)S(1)} fusion(bf16[8,64,8,24,64]{4,3,2,1,0:T(8,128)(2,1)} %reshape.24, bf16[8,64,4,128,1,1]{3,2,1,0,5,4:T(4,128)(2,1)S(1)} %bitcast.23), kind=kOutput, calls=%fused_computation.6 | convolution fusion | flops 6442450944 | bytes 38273024 | tf_op jit(solution)/shard_map/kpiqn,knrj->priqj/dot_general | solution.py:28
  80.2 0.0 copy-start.1
  80.2 28.6 %copy.8 = f32[64,4,8,24,128]{4,3,2,1,0:T(8,128)} copy(f32[64,4,8,24,128]{4,0,3,2,1:T(8,128)S(1)} %fusion.3) | data formatting | bytes 50331648 | tf_op jit(solution)/shard_map/kpiqn,knrj->priqj/transpose | solution.py:28
  108.8 0.0 reduce-scatter.2.cloned.1.call-update
  108.8 448.8 %reduce-scatter.2.cloned.1.call-done = f32[8,24,128]{2,1,0:T(8,128)} async-done(((f32[2048,24,128]{2,1,0:T(8,128)}), f32[8,24,128]{2,1,0:T(8,128)}) %reduce-scatter.2.cloned.1.call-update) | async-done | bytes 98320 | tf_op jit(solution)/shard_map/reduce_scatter | solution.py:37
  557.6 0.0 copy-done.1
  (3 shorter events, 0.0 us)
Async XLA Ops:
  6.5 8.5 %copy-start = (bf16[8,64,1536]{2,1,0:T(8,128)(2,1)S(1)}, bf16[8,64,1536]{2,1,0:T(8,128)(2,1)}, u32[]{:S(2)}) copy-start(bf16[8,64,1536]{2,1,0:T(8,128)(2,1)} %param.6) | copy-start | bytes 4718596
  6.5 551.0 %reduce-scatter.2.cloned.1.call-start = ((), (), s32[]{:S(2)}) async-start(), calls=%async_computation.1 | async-start | bytes 25264128 | tf_op jit(solution)/shard_map/reduce_scatter | solution.py:37
  80.2 477.3 %copy-start.1 = (bf16[8,64,1536]{2,1,0:T(8,128)(2,1)S(1)}, bf16[8,64,1536]{2,1,0:T(8,128)(2,1)}, u32[]{:S(2)}) copy-start(bf16[8,64,1536]{2,1,0:T(8,128)(2,1)} %param.6) | copy-start | bytes 4718596
Sparse Core Ops, SparseCore 0:
  108.9 448.5 reduce-scatter.1
where the time goes:
time: 565 us; the launch traced here: 564 us
  waiting for transfers between devices  449 us (79%)
  local copies, waits for them, and re-layouts  67.1 us (12%)
  matrix products  34.2 us (6%)
  between operations  14.2 us (3%)
    reduce_scatter x1, waiting for transfers between devices, on_device(): lax.psum_scatter(whole_sum, ('pair', 'red'), scatter_dimension=0, tiled=T...  449 us
    reshape x1, local copies, waits for them, and re-layouts, on_device(): half_done.reshape(slot_count, pair_count, owned_rows, ket_count, shell_size)  31 us
    transpose x1, local copies, waits for them, and re-layouts, on_device(): jnp.einsum('kpiqn,knrj->priqj', half_done.reshape(slot_count, pair_count,...  28.6 us
    dot_general x1, matrix products, on_device(): jnp.einsum('kpiqn,knrj->priqj', half_done.reshape(slot_count, pair_count,...  27.4 us
  transfers between devices with their start and end apart: 1, of which 1 were waited for; matrix products, arithmetic and copies ran while one was open for 0% of the time, Pallas kernels for 0%

commit v1 on v0

v1 whole, which is shorter than its diff:
```python
import functools

import jax
import jax.numpy as jnp
from jax import lax
from jax.experimental import pallas as pl
from jax.experimental.pallas import tpu as pltpu
from jax.sharding import PartitionSpec as P

NX, NZ, NC, NY = 4, 8, 2, 4
SLOTS = 16
SH = 64
BF, F32 = jnp.bfloat16, jnp.float32


def pair_of(x, z, c):
    return (x * NZ + z) * NC + c


COORDS = [(x, z, c) for x in range(NX) for z in range(NZ) for c in range(NC)]


def move_x(a, d):
    return lax.ppermute(a, "pair", [(pair_of(x, z, c), pair_of((x + d) % NX, z, c)) for x, z, c in COORDS])


def move_z(a, d):
    return lax.ppermute(a, "pair", [(pair_of(x, z, c), pair_of(x, (z + d) % NZ, c)) for x, z, c in COORDS])


def move_y(a, d):
    return lax.ppermute(a, "red", [(y, (y + d) % NY) for y in range(NY)])


def swap_core(a):
    return lax.ppermute(a, "pair", [(pair_of(x, z, c), pair_of(x, z, 1 - c)) for x, z, c in COORDS])


def panel_kernel(idx, pos, coeffs, lt, r, lraw, lsem, rsem):
    x, z, c, y = pos[0], pos[1], pos[2], pos[3]
    copies_l, copies_r = [], []
    for k in range(SLOTS):
        row = pl.multiple_of(idx[0, k] * SH, SH)
        cp = pltpu.make_async_copy(coeffs.at[pl.ds(row, SH), :], lraw.at[pl.ds(k * SH, SH), :], lsem.at[k])
        cp.start()
        copies_l.append(cp)
    for k in range(SLOTS):
        row = pl.multiple_of(idx[1, k] * SH, SH)
        for yr in range(NY):
            col = pl.multiple_of(((y + yr) & (NY - 1)) * 128, 128)
            cp = pltpu.make_async_copy(
                coeffs.at[pl.ds(row, SH), pl.ds(col, 128)],
                r.at[pl.ds(k * SH, SH), pl.ds(yr * 128, 128)],
                rsem.at[k * NY + yr],
            )
            cp.start()
            copies_r.append(cp)
    ip = lax.broadcasted_iota(jnp.int32, (256, 512), 0)
    col = lax.broadcasted_iota(jnp.int32, (256, 512), 1)
    want = (((ip >> 6) + x) & 3) * 128 + ((((ip >> 3) & 7) + z) & 7) * 16 + c * 8 + (ip & 7)
    sel = jnp.where(col == want, 1.0, 0.0).astype(BF)
    for cp in copies_l:
        cp.wait()
    for g in range(4):
        lt[g] = lax.dot_general(
            sel, lraw[pl.ds(g * 256, 256), :], (((1,), (1,)), ((), ())), preferred_element_type=F32
        ).astype(BF)
    for cp in copies_r:
        cp.wait()


def panels(idx, pos, coeffs):
    return pl.pallas_call(
        panel_kernel,
        out_shape=(jax.ShapeDtypeStruct((4, 256, 256), BF), jax.ShapeDtypeStruct((1024, 512), BF)),
        in_specs=[
            pl.BlockSpec(memory_space=pltpu.SMEM),
            pl.BlockSpec(memory_space=pltpu.SMEM),
            pl.BlockSpec(memory_space=pl.ANY),
        ],
        out_specs=(pl.BlockSpec(memory_space=pltpu.VMEM), pl.BlockSpec(memory_space=pltpu.VMEM)),
        scratch_shapes=[
            pltpu.VMEM((1024, 512), BF),
            pltpu.SemaphoreType.DMA((SLOTS,)),
            pltpu.SemaphoreType.DMA((SLOTS * NY,)),
        ],
        cost_estimate=pl.CostEstimate(flops=300_000_000, bytes_accessed=4_000_000, transcendentals=0),
        name="panels",
    )(idx, pos, coeffs)


def block_kernel(by_x, acc_at, plain_at, cnt, lt_ref, r_ref, own_i, mate_i, far, plain, acc, own, lt, bd, half):
    step = pl.program_id(0)

    @pl.when(step == 0)
    def _():
        slot = lax.broadcasted_iota(jnp.int32, (256, 256), 1) >> 6
        for g in range(4):
            local = slot + 4 * (g % 2)
            keep = local < cnt[g // 2]
            lt[g] = jnp.where(keep, lt_ref[g].astype(F32), 0.0).astype(BF)
        bd[...] = jnp.zeros_like(bd)

    low = lax.broadcasted_iota(jnp.int32, (SH, 128), 1) < 64
    zero = jnp.zeros((SH, 128), F32)
    for k in range(SLOTS):
        src = (own_i if k < 8 else mate_i)[k % 8].astype(F32)
        swapped = pltpu.roll(src, 64, 1)
        g, kk = k // 4, k % 4
        for odd in range(2):
            piece = src if (kk % 2) == odd else swapped
            piece = jnp.where(low, zero, piece) if kk % 2 else jnp.where(low, piece, zero)
            bd[odd, g, pl.ds(kk * SH, SH), pl.ds((kk // 2) * 128, 128)] = piece.astype(BF)
    for odd in range(2):
        for g in range(4):
            half[pl.ds(odd * 256, 256), pl.ds(g * 256, 256)] = jnp.dot(
                lt[g], bd[odd, g], preferred_element_type=F32
            ).astype(BF)
    for odd in range(2):
        res = jnp.dot(half[pl.ds(odd * 256, 256), :], r_ref[...], preferred_element_type=F32)
        for at, ref in ((0, own), (2, far), (plain_at, plain), (acc_at, acc)):
            part = res[at * 64 : at * 64 + 64, :] if by_x else res[:, at * 128 : at * 128 + 128]
            ref[odd] = part.astype(ref.dtype)


def block(by_x, acc_at, plain_at, first_q, nq, cnt, lt, r, own_i, mate_i):
    rows, cols = (64, 512) if by_x else (256, 128)
    first = first_q // 2
    out = lambda dt: jax.ShapeDtypeStruct((nq, rows, cols), dt)
    spec = pl.BlockSpec((2, rows, cols), lambda s: (s, 0, 0))
    ints = pl.BlockSpec((8, SH, 128), lambda s: (0, 0, first + s))
    return pl.pallas_call(
        functools.partial(block_kernel, by_x, acc_at, plain_at),
        grid=(nq // 2,),
        out_shape=(out(BF), out(BF), out(F32), out(F32)),
        in_specs=[
            pl.BlockSpec(memory_space=pltpu.SMEM),
            pl.BlockSpec((4, 256, 256), lambda s: (0, 0, 0)),
            pl.BlockSpec((1024, 512), lambda s: (0, 0)),
            ints,
            ints,
        ],
        out_specs=(spec, spec, spec, spec),
        scratch_shapes=[
            pltpu.VMEM((4, 256, 256), BF),
            pltpu.VMEM((2, 4, 256, 256), BF),
            pltpu.VMEM((512, 1024), BF),
        ],
        compiler_params=pltpu.CompilerParams(vmem_limit_bytes=24 * 1024 * 1024),
        cost_estimate=pl.CostEstimate(flops=400_000_000 * nq, bytes_accessed=6_000_000, transcendentals=0),
        name="block_x" if by_x else "block_y",
    )(cnt, lt, r, own_i, mate_i)


def on_device(integrals, coeffs, shell_pairs, block_count):
    p = lax.axis_index("pair")
    y = lax.axis_index("red")
    x, z, c = p // (NZ * NC), (p // NC) % NZ, p % NC
    mate = p + 1 - 2 * c
    mate_i = swap_core(integrals)
    count = block_count[0, 0]
    mate_count = swap_core(block_count)[0, 0]
    own_sp = lax.dynamic_slice_in_dim(shell_pairs, (p * NY + y) * 8, 8, 0)
    mate_sp = lax.dynamic_slice_in_dim(shell_pairs, (mate * NY + y) * 8, 8, 0)
    idx = jnp.concatenate([own_sp, mate_sp], axis=0).T
    pos = jnp.stack([x, z, c, y]).astype(jnp.int32)
    cnt = jnp.stack([count, mate_count])
    lt, r = panels(idx, pos, coeffs)

    def parts(by_x, up, first_q):
        acc_at, plain_at = (1, 3) if up else (3, 1)
        return block(by_x, acc_at, plain_at, first_q, 6, cnt, lt, r, integrals, mate_i)

    def ring(by_x, up, made):
        far, plain, acc, own = made
        move = move_x if by_x else move_y
        d = 1 if up else -1
        got_far = move(far, d)
        got_plain = move(plain, -d)
        got_acc = move((acc + got_far.astype(F32)).astype(BF), d)
        return own + got_plain.astype(F32) + got_acc.astype(F32)

    made_xa = parts(True, True, 0)
    made_ya = parts(False, True, 12)
    made_xb = parts(True, False, 6)
    made_yb = parts(False, False, 18)
    sum_x = jnp.concatenate([ring(True, True, made_xa), ring(True, False, made_xb)], axis=0)
    sum_y = jnp.concatenate([ring(False, True, made_ya), ring(False, False, made_yb)], axis=0)

    tot_x, tot_y = sum_x[:, :, :128], sum_y[:, :64, :]
    for d in (1, 3, 2):
        tot_x = tot_x + move_y(sum_x[:, :, d * 128 : d * 128 + 128].astype(BF), d).astype(F32)
        tot_y = tot_y + move_x(sum_y[:, d * 64 : d * 64 + 64, :].astype(BF), d).astype(F32)
    tot = jnp.concatenate([tot_x, tot_y], axis=0).reshape(24, NZ, 8, 128)

    chunk = lambda d: tot[:, d % NZ]
    up, down = chunk(4), chunk(-3)
    for d in (3, 2, 1, 0):
        up = move_z(up, 1)
        if d:
            up = up + chunk(d)
            down = move_z(down, -1)
            if d > 1:
                down = down + chunk(1 - d)
    res = up + down + chunk(0)
    return jnp.transpose(res, (1, 0, 2))


def solution(mesh):
    return jax.shard_map(
        on_device,
        mesh=mesh,
        in_specs=(P(("pair", "red"), None, None), P(), P(), P("pair", "red")),
        out_specs=P("pair", None, "red"),
        check_vma=False,
    )
```

time: 565 us -> 117 us (0.21)
  waiting for transfers between devices: 449 us -> 54.9 us
  local copies, waits for them, and re-layouts: 67.1 us -> 3.39 us
  matrix products: 34.2 us -> 0 us
  starting transfers between devices: 0.01 us -> 31.1 us
  Pallas kernels: 0 us -> 21 us
  between operations: 14.2 us -> 1.01 us
    reduce_scatter x1 -> x0, waiting for transfers between devices: 449 us -> none  [on_device(): lax.psum_scatter(whole_sum, ('pair', 'red'), scatter_dimension=0, tiled=T...]
    ppermute x0 -> x27, waiting for transfers between devices: none -> 54.9 us  [the longest x9 31.9 us: move_y(): return lax.ppermute(a, 'red', [(y, (y + d) % NY) for y in range(NY)])]
    dot_general x2 -> x0, matrix products: 34.2 us -> none  [the longest x1 27.4 us: on_device(): jnp.einsum('kpiqn,knrj->priqj', half_done.reshape(slot_count, pair_count,...]
    ppermute x0 -> x27, starting transfers between devices: none -> 31.1 us  [the longest x7 12.9 us: move_z(): lax.ppermute(a, 'pair', [(pair_of(x, z, c), pair_of(x, (z + d) % NZ, c))...]
    reshape x2 -> x0, local copies, waits for them, and re-layouts: 31.1 us -> none  [the longest x1 31 us: on_device(): half_done.reshape(slot_count, pair_count, owned_rows, ket_count, shell_size)]
    transpose x1 -> x0, local copies, waits for them, and re-layouts: 28.6 us -> none  [on_device(): jnp.einsum('kpiqn,knrj->priqj', half_done.reshape(slot_count, pair_count,...]
    pallas_call x0 -> x5, Pallas kernels: none -> 21 us  [the longest x4 16.2 us: block(): pl.pallas_call(functools.partial(block_kernel, by_x, acc_at, plain_at), g...]
    gather x2 -> x0, local copies, waits for them, and re-layouts: 6.66 us -> none  [the longest x1 3.33 us: on_device(): left_panels = jnp.take(coef_table, own_pairs[:, 0], axis=0)]
  transfers between devices with their start and end apart: 1 -> 27, of which waited for: 1 -> 12; matrix products, arithmetic and copies ran while one was open for 0% -> 4% of each run, Pallas kernels for 0% -> 15%
where the time goes in v1:
time: 117 us; the launch traced here: 116 us
  waiting for transfers between devices  54.9 us (47%)
  starting transfers between devices  31.1 us (27%)
  Pallas kernels  21 us (18%)
  other arithmetic  4.25 us (4%)
  local copies, waits for them, and re-layouts  3.39 us (3%)
    ppermute x9, waiting for transfers between devices, move_y(): return lax.ppermute(a, 'red', [(y, (y + d) % NY) for y in range(NY)])  31.9 us
    pallas_call x4, Pallas kernels, block(): pl.pallas_call(functools.partial(block_kernel, by_x, acc_at, plain_at), g...  16.2 us
    ppermute x7, waiting for transfers between devices, move_z(): lax.ppermute(a, 'pair', [(pair_of(x, z, c), pair_of(x, (z + d) % NZ, c))...  13.6 us
    ppermute x7, starting transfers between devices, move_z(): lax.ppermute(a, 'pair', [(pair_of(x, z, c), pair_of(x, (z + d) % NZ, c))...  12.9 us
    ppermute x9, starting transfers between devices, move_x(): lax.ppermute(a, 'pair', [(pair_of(x, z, c), pair_of((x + d) % NX, z, c))...  10.2 us
    ppermute x9, waiting for transfers between devices, move_x(): lax.ppermute(a, 'pair', [(pair_of(x, z, c), pair_of((x + d) % NX, z, c))...  9.32 us
    ppermute x9, starting transfers between devices, move_y(): return lax.ppermute(a, 'red', [(y, (y + d) % NY) for y in range(NY)])  7.59 us
    pallas_call x1, Pallas kernels, panels(): pl.pallas_call(panel_kernel, out_shape=(jax.ShapeDtypeStruct((4, 256, 256...  4.86 us
  transfers between devices with their start and end apart: 27, of which 12 were waited for; matrix products, arithmetic and copies ran while one was open for 4% of the time, Pallas kernels for 15%

profile of v1, /device:TPU:6, one launch (start us, length us, event | category | flops | bytes accessed | tf_op | source)
XLA Modules:
  0.0 115.7 jit_solution(16672034775092961656)
XLA Ops:
  3.3 4.9 %panels.1 = (bf16[4,256,256]{2,1,0:T(8,128)(2,1)}, bf16[1024,512]{1,0:T(8,128)(2,1)}) custom-call(s32[2,16]{1,0:T(2,128)} %add_bitcast_fusion.idx, s32[4]{0:T(128)} %pad_add_fusion.1.pos, bf16[6016,512]{1,0:T(8,128)(2,1)} %coeffs.1), custom_call_target="tpu_custom_call" | custom-call | flops 300000000 | bytes 4000000 | tf_op jit(solution)/shard_map/panels/pallas_call | solution.py:73
  8.9 1.2 %copy-done.1 = bf16[1024,512]{1,0:T(8,128)(2,1)S(1)} copy-done((bf16[1024,512]{1,0:T(8,128)(2,1)S(1)}, bf16[1024,512]{1,0:T(8,128)(2,1)}, u32[]{:S(2)}) %copy-start.1) | copy-done | bytes 1048600
  10.2 1.0 copy-done.2
  11.2 4.0 %block_x.3 = (bf16[6,64,512]{2,1,0:T(8,128)(2,1)S(1)}, bf16[6,64,512]{2,1,0:T(8,128)(2,1)S(1)}, f32[6,64,512]{2,1,0:T(8,128)S(1)}, f32[6,64,512]{2,1,0:T(8,128)S(1)}) custom-call(s32[2]{0:T(128)S(1)} %pad_add_fusion.cnt, bf16[4,256,256]{2,1,0:T(8,128)(2,1)S(1)} %copy-done.2, bf16[1024,512]{1,0:T(8,128)(2,1)S(1)} %copy-done.1, ...), custom_call_target="tpu_custom_call" | custom-call | flops 2400000000 | bytes 6000000 | tf_op jit(solution)/shard_map/block_x/pallas_call | solution.py:132
  15.3 0.9 collective-permute-start.6
  16.2 2.4 %collective-permute-start.5 = (bf16[6,64,512]{2,1,0:T(8,128)(2,1)S(1)}, bf16[6,64,512]{2,1,0:T(8,128)(2,1)S(1)}, u32[]{:S(2)}, u32[]{:S(2)}) collective-permute-start(bf16[6,64,512]{2,1,0:T(8,128)(2,1)S(1)} %get-tuple-element.30), channel_id=1, source_target_pairs={{0,64},{4,68},{8,72},{12,76},{16,80},{20,84},{24,88},{28,92},{32,9... | collective-permute-start | bytes 1179656 | tf_op jit(solution)/shard_map/ppermute | solution.py:24
  18.6 4.0 %block_x.2 = (bf16[6,64,512]{2,1,0:T(8,128)(2,1)S(1)}, bf16[6,64,512]{2,1,0:T(8,128)(2,1)S(1)}, f32[6,64,512]{2,1,0:T(8,128)S(1)}, f32[6,64,512]{2,1,0:T(8,128)S(1)}) custom-call(s32[2]{0:T(128)S(1)} %pad_add_fusion.cnt, bf16[4,256,256]{2,1,0:T(8,128)(2,1)S(1)} %copy-done.2, bf16[1024,512]{1,0:T(8,128)(2,1)S(1)} %copy-done.1, ...), custom_call_target="tpu_custom_call" | custom-call | flops 2400000000 | bytes 6000000 | tf_op jit(solution)/shard_map/block_x/pallas_call | solution.py:132
  22.6 1.1 collective-permute-start.3
  23.7 1.0 collective-permute-start.2
  24.7 4.0 %block_y.3 = (bf16[6,256,128]{2,1,0:T(8,128)(2,1)S(1)}, bf16[6,256,128]{2,1,0:T(8,128)(2,1)S(1)}, f32[6,256,128]{2,1,0:T(8,128)S(1)}, f32[6,256,128]{2,1,0:T(8,128)S(1)}) custom-call(s32[2]{0:T(128)S(1)} %pad_add_fusion.cnt, bf16[4,256,256]{2,1,0:T(8,128)(2,1)S(1)} %copy-done.2, bf16[1024,512]{1,0:T(8,128)(2,1)S(1)} %copy-done.1, ...), custom_call_target="tpu_custom_call" | custom-call | flops 2400000000 | bytes 6000000 | tf_op jit(solution)/shard_map/block_y/pallas_call | solution.py:132
  28.8 3.1 %collective-permute-start.15 = (bf16[6,256,128]{2,1,0:T(8,128)(2,1)S(1)}, bf16[6,256,128]{2,1,0:T(8,128)(2,1)S(1)}, u32[]{:S(2)}, u32[]{:S(2)}) collective-permute-start(bf16[6,256,128]{2,1,0:T(8,128)(2,1)S(1)} %get-tuple-element.40), channel_id=1, source_target_pairs={{0,3},{1,0},{2,1},{3,2},{4,7},{5,4},{6,5},{7,6},{8,11},{9,8},{10,9... | collective-permute-start | bytes 1179656 | tf_op jit(solution)/shard_map/ppermute | solution.py:32
  31.9 4.0 %block_y.2 = (bf16[6,256,128]{2,1,0:T(8,128)(2,1)S(1)}, bf16[6,256,128]{2,1,0:T(8,128)(2,1)S(1)}, f32[6,256,128]{2,1,0:T(8,128)S(1)}, f32[6,256,128]{2,1,0:T(8,128)S(1)}) custom-call(s32[2]{0:T(128)S(1)} %pad_add_fusion.cnt, bf16[4,256,256]{2,1,0:T(8,128)(2,1)S(1)} %copy-done.2, bf16[1024,512]{1,0:T(8,128)(2,1)S(1)} %copy-done.1, ...), custom_call_target="tpu_custom_call" | custom-call | flops 2400000000 | bytes 6000000 | tf_op jit(solution)/shard_map/block_y/pallas_call | solution.py:132
  37.1 2.2 %collective-permute-done.15 = bf16[6,256,128]{2,1,0:T(8,128)(2,1)S(1)} collective-permute-done((bf16[6,256,128]{2,1,0:T(8,128)(2,1)S(1)}, bf16[6,256,128]{2,1,0:T(8,128)(2,1)S(1)}, u32[]{:S(2)}, u32[]{:S(2)}) %collective-permute-start.15) | collective-permute-done | bytes 393248 | tf_op jit(solution)/shard_map/ppermute | solution.py:32
  39.7 15.6 %collective-permute-done.12 = bf16[6,256,128]{2,1,0:T(8,128)(2,1)S(1)} collective-permute-done((bf16[6,256,128]{2,1,0:T(8,128)(2,1)S(1)}, bf16[6,256,128]{2,1,0:T(8,128)(2,1)S(1)}, u32[]{:S(2)}, u32[]{:S(2)}) %collective-permute-start.12) | collective-permute-done | bytes 393248 | tf_op jit(solution)/shard_map/ppermute | solution.py:32
  55.3 1.6 %collective-permute-start.4 = (bf16[6,64,512]{2,1,0:T(8,128)(2,1)S(1)}, bf16[6,64,512]{2,1,0:T(8,128)(2,1)S(1)}, u32[]{:S(2)}, u32[]{:S(2)}) collective-permute-start(bf16[6,64,512]{2,1,0:T(8,128)(2,1)S(1)} %add_convert_fusion.3), channel_id=1, source_target_pairs={{0,64},{4,68},{8,72},{12,76},{16,80},{20,84},{24,88},{28,92},{32,9... | collective-permute-start | bytes 1179656 | tf_op jit(solution)/shard_map/ppermute | solution.py:24
  57.3 2.1 %collective-permute-start.13 = (bf16[6,256,128]{2,1,0:T(8,128)(2,1)S(1)}, bf16[6,256,128]{2,1,0:T(8,128)(2,1)S(1)}, u32[]{:S(2)}, u32[]{:S(2)}) collective-permute-start(bf16[6,256,128]{2,1,0:T(8,128)(2,1)S(1)} %add_convert_fusion.1), channel_id=1, source_target_pairs={{0,1},{1,2},{2,3},{3,0},{4,5},{5,6},{6,7},{7,4},{8,9},{9,10},{10,1... | collective-permute-start | bytes 1179656 | tf_op jit(solution)/shard_map/ppermute | solution.py:32
  59.4 4.5 %collective-permute-done.4 = bf16[6,64,512]{2,1,0:T(8,128)(2,1)S(1)} collective-permute-done((bf16[6,64,512]{2,1,0:T(8,128)(2,1)S(1)}, bf16[6,64,512]{2,1,0:T(8,128)(2,1)S(1)}, u32[]{:S(2)}, u32[]{:S(2)}) %collective-permute-start.4) | collective-permute-done | bytes 393248 | tf_op jit(solution)/shard_map/ppermute | solution.py:24
  64.9 12.6 %collective-permute-done.16 = bf16[6,256,128]{2,1,0:T(8,128)(2,1)S(1)} collective-permute-done((bf16[6,256,128]{2,1,0:T(8,128)(2,1)S(1)}, bf16[6,256,128]{2,1,0:T(8,128)(2,1)S(1)}, u32[]{:S(2)}, u32[]{:S(2)}) %collective-permute-start.16) | collective-permute-done | bytes 393248 | tf_op jit(solution)/shard_map/ppermute | solution.py:32
  77.5 0.8 collective-permute-start.9
  78.8 2.0 %collective-permute-start.18 = (bf16[12,64,128]{2,1,0:T(8,128)(2,1)S(1)}, bf16[12,64,128]{2,1,0:T(8,128)(2,1)S(1)}, u32[]{:S(2)}, u32[]{:S(2)}) collective-permute-start(bf16[12,64,128]{2,1,0:T(8,128)(2,1)S(1)} %get-tuple-element.54), channel_id=1, source_target_pairs={{0,192},{4,196},{8,200},{12,204},{16,208},{20,212},{24,216},{28,22... | collective-permute-start | bytes 589832 | tf_op jit(solution)/shard_map/ppermute | solution.py:24
  81.6 1.5 %collective-permute-done.9 = bf16[12,64,128]{2,1,0:T(8,128)(2,1)S(1)} collective-permute-done((bf16[12,64,128]{2,1,0:T(8,128)(2,1)S(1)}, bf16[12,64,128]{2,1,0:T(8,128)(2,1)S(1)}, u32[]{:S(2)}, u32[]{:S(2)}) %collective-permute-start.9) | collective-permute-done | bytes 196640 | tf_op jit(solution)/shard_map/ppermute | solution.py:32
  83.3 1.2 %collective-permute-done.17 = bf16[12,64,128]{2,1,0:T(8,128)(2,1)S(1)} collective-permute-done((bf16[12,64,128]{2,1,0:T(8,128)(2,1)S(1)}, bf16[12,64,128]{2,1,0:T(8,128)(2,1)S(1)}, u32[]{:S(2)}, u32[]{:S(2)}) %collective-permute-start.17) | collective-permute-done | bytes 196640 | tf_op jit(solution)/shard_map/ppermute | solution.py:24
  84.5 1.3 %collective-permute-done.18 = bf16[12,64,128]{2,1,0:T(8,128)(2,1)S(1)} collective-permute-done((bf16[12,64,128]{2,1,0:T(8,128)(2,1)S(1)}, bf16[12,64,128]{2,1,0:T(8,128)(2,1)S(1)}, u32[]{:S(2)}, u32[]{:S(2)}) %collective-permute-start.18) | collective-permute-done | bytes 196640 | tf_op jit(solution)/shard_map/ppermute | solution.py:24
  85.8 2.2 %collective-permute-done.19 = bf16[12,64,128]{2,1,0:T(8,128)(2,1)S(1)} collective-permute-done((bf16[12,64,128]{2,1,0:T(8,128)(2,1)S(1)}, bf16[12,64,128]{2,1,0:T(8,128)(2,1)S(1)}, u32[]{:S(2)}, u32[]{:S(2)}) %collective-permute-start.19) | collective-permute-done | bytes 196640 | tf_op jit(solution)/shard_map/ppermute | solution.py:24
  88.3 2.0 %collective-permute-start.20 = (f32[24,8,128]{2,0,1:T(8,128)S(1)}, f32[24,8,128]{2,0,1:T(8,128)S(1)}, u32[]{:S(2)}, u32[]{:S(2)}) collective-permute-start(f32[24,8,128]{2,0,1:T(8,128)S(1)} %bitcast.46), channel_id=1, source_target_pairs={{0,8},{4,12},{8,16},{12,20},{16,24},{20,28},{24,32},{28,36},{32,40... | collective-permute-start | bytes 294920 | tf_op jit(solution)/shard_map/ppermute | solution.py:28
  90.3 4.0 %collective-permute-start.24 = (f32[24,8,128]{2,0,1:T(8,128)S(1)}, f32[24,8,128]{2,0,1:T(8,128)S(1)}, u32[]{:S(2)}, u32[]{:S(2)}) collective-permute-start(f32[24,8,128]{2,0,1:T(8,128)S(1)} %bitcast.45), channel_id=1, source_target_pairs={{0,56},{4,60},{8,0},{12,4},{16,8},{20,12},{24,16},{28,20},{32,24},... | collective-permute-start | bytes 294920 | tf_op jit(solution)/shard_map/ppermute | solution.py:28
  94.3 2.5 %collective-permute-done.20 = f32[24,8,128]{2,0,1:T(8,128)S(1)} collective-permute-done((f32[24,8,128]{2,0,1:T(8,128)S(1)}, f32[24,8,128]{2,0,1:T(8,128)S(1)}, u32[]{:S(2)}, u32[]{:S(2)}) %collective-permute-start.20) | collective-permute-done | bytes 98336 | tf_op jit(solution)/shard_map/ppermute | solution.py:28
  97.0 3.3 %collective-permute-start.25 = (f32[24,8,128]{2,0,1:T(8,128)S(1)}, f32[24,8,128]{2,0,1:T(8,128)S(1)}, u32[]{:S(2)}, u32[]{:S(2)}) collective-permute-start(f32[24,8,128]{2,0,1:T(8,128)S(1)} %fusion.13), channel_id=1, source_target_pairs={{0,56},{4,60},{8,0},{12,4},{16,8},{20,12},{24,16},{28,20},{32,24},... | collective-permute-start | bytes 294920 | tf_op jit(solution)/shard_map/ppermute | solution.py:28
  100.3 2.8 %collective-permute-done.21 = f32[24,8,128]{2,0,1:T(8,128)S(1)} collective-permute-done((f32[24,8,128]{2,0,1:T(8,128)S(1)}, f32[24,8,128]{2,0,1:T(8,128)S(1)}, u32[]{:S(2)}, u32[]{:S(2)}) %collective-permute-start.21) | collective-permute-done | bytes 98336 | tf_op jit(solution)/shard_map/ppermute | solution.py:28
  103.3 3.3 %collective-permute-start.26 = (f32[24,8,128]{2,0,1:T(8,128)S(1)}, f32[24,8,128]{2,0,1:T(8,128)S(1)}, u32[]{:S(2)}, u32[]{:S(2)}) collective-permute-start(f32[24,8,128]{2,0,1:T(8,128)S(1)} %fusion.12), channel_id=1, source_target_pairs={{0,56},{4,60},{8,0},{12,4},{16,8},{20,12},{24,16},{28,20},{32,24},... | collective-permute-start | bytes 294920 | tf_op jit(solution)/shard_map/ppermute | solution.py:28
  106.6 2.5 %collective-permute-done.22 = f32[24,8,128]{2,0,1:T(8,128)S(1)} collective-permute-done((f32[24,8,128]{2,0,1:T(8,128)S(1)}, f32[24,8,128]{2,0,1:T(8,128)S(1)}, u32[]{:S(2)}, u32[]{:S(2)}) %collective-permute-start.22) | collective-permute-done | bytes 98336 | tf_op jit(solution)/shard_map/ppermute | solution.py:28
  109.2 5.8 %collective-permute-done.23 = f32[24,8,128]{2,0,1:T(8,128)S(1)} collective-permute-done((f32[24,8,128]{2,0,1:T(8,128)S(1)}, f32[24,8,128]{2,0,1:T(8,128)S(1)}, u32[]{:S(2)}, u32[]{:S(2)}) %collective-permute-start.23) | collective-permute-done | bytes 98336 | tf_op jit(solution)/shard_map/ppermute | solution.py:28
  (61 shorter events, 8.9 us)
Async XLA Ops:
  0.0 8.9 %collective-permute-start.1 = (bf16[8,64,1536]{2,1,0:T(8,128)(2,1)}, bf16[8,64,1536]{2,1,0:T(8,128)(2,1)S(1)}, u32[]{:S(2)}, u32[]{:S(2)}) collective-permute-start(bf16[8,64,1536]{2,1,0:T(8,128)(2,1)} %own_i.7), channel_id=1, source_target_pairs={{0,4},{4,0},{8,12},{12,8},{16,20},{20,16},{24,28},{28,24},{32,36},... | collective-permute-start | bytes 4718600 | tf_op jit(solution)/shard_map/ppermute | solution.py:36
  0.0 8.2 %collective-permute-start = (s32[1,1]{1,0:T(1,128)}, s32[1,1]{1,0:T(1,128)}, u32[]{:S(2)}, u32[]{:S(2)}) collective-permute-start(s32[1,1]{1,0:T(1,128)} %param.7), channel_id=1, source_target_pairs={{0,4},{4,0},{8,12},{12,8},{16,20},{20,16},{24,28},{28,24},{32,36},... | collective-permute-start | bytes 20 | tf_op jit(solution)/shard_map/ppermute | solution.py:36
  3.3 5.6 %copy-start = (bf16[8,64,1536]{2,1,0:T(8,128)(2,1)S(1)}, bf16[8,64,1536]{2,1,0:T(8,128)(2,1)}, u32[]{:S(2)}) copy-start(bf16[8,64,1536]{2,1,0:T(8,128)(2,1)} %own_i.7) | copy-start | bytes 4718596
  8.9 1.2 %copy-start.1 = (bf16[1024,512]{1,0:T(8,128)(2,1)S(1)}, bf16[1024,512]{1,0:T(8,128)(2,1)}, u32[]{:S(2)}) copy-start(bf16[1024,512]{1,0:T(8,128)(2,1)} %get-tuple-element.24.r_ref) | copy-start | bytes 3145732
  10.2 1.0 copy-start.2
  15.3 20.7 %collective-permute-start.6 = (bf16[6,64,512]{2,1,0:T(8,128)(2,1)S(1)}, bf16[6,64,512]{2,1,0:T(8,128)(2,1)S(1)}, u32[]{:S(2)}, u32[]{:S(2)}) collective-permute-start(bf16[6,64,512]{2,1,0:T(8,128)(2,1)S(1)} %get-tuple-element.32), channel_id=1, source_target_pairs={{0,192},{4,196},{8,200},{12,204},{16,208},{20,212},{24,216},{28,22... | collective-permute-start | bytes 1179656 | tf_op jit(solution)/shard_map/ppermute | solution.py:24
  16.2 40.8 %collective-permute-start.5 = (bf16[6,64,512]{2,1,0:T(8,128)(2,1)S(1)}, bf16[6,64,512]{2,1,0:T(8,128)(2,1)S(1)}, u32[]{:S(2)}, u32[]{:S(2)}) collective-permute-start(bf16[6,64,512]{2,1,0:T(8,128)(2,1)S(1)} %get-tuple-element.30), channel_id=1, source_target_pairs={{0,64},{4,68},{8,72},{12,76},{16,80},{20,84},{24,88},{28,92},{32,9... | collective-permute-start | bytes 1179656 | tf_op jit(solution)/shard_map/ppermute | solution.py:24
  22.6 13.5 %collective-permute-start.3 = (bf16[6,64,512]{2,1,0:T(8,128)(2,1)S(1)}, bf16[6,64,512]{2,1,0:T(8,128)(2,1)S(1)}, u32[]{:S(2)}, u32[]{:S(2)}) collective-permute-start(bf16[6,64,512]{2,1,0:T(8,128)(2,1)S(1)} %get-tuple-element.28), channel_id=1, source_target_pairs={{0,64},{4,68},{8,72},{12,76},{16,80},{20,84},{24,88},{28,92},{32,9... | collective-permute-start | bytes 1179656 | tf_op jit(solution)/shard_map/ppermute | solution.py:24
  23.7 33.6 %collective-permute-start.2 = (bf16[6,64,512]{2,1,0:T(8,128)(2,1)S(1)}, bf16[6,64,512]{2,1,0:T(8,128)(2,1)S(1)}, u32[]{:S(2)}, u32[]{:S(2)}) collective-permute-start(bf16[6,64,512]{2,1,0:T(8,128)(2,1)S(1)} %get-tuple-element.26), channel_id=1, source_target_pairs={{0,192},{4,196},{8,200},{12,204},{16,208},{20,212},{24,216},{28,22... | collective-permute-start | bytes 1179656 | tf_op jit(solution)/shard_map/ppermute | solution.py:24
  28.8 10.5 %collective-permute-start.15 = (bf16[6,256,128]{2,1,0:T(8,128)(2,1)S(1)}, bf16[6,256,128]{2,1,0:T(8,128)(2,1)S(1)}, u32[]{:S(2)}, u32[]{:S(2)}) collective-permute-start(bf16[6,256,128]{2,1,0:T(8,128)(2,1)S(1)} %get-tuple-element.40), channel_id=1, source_target_pairs={{0,3},{1,0},{2,1},{3,2},{4,7},{5,4},{6,5},{7,6},{8,11},{9,8},{10,9... | collective-permute-start | bytes 1179656 | tf_op jit(solution)/shard_map/ppermute | solution.py:32
  35.9 28.6 %collective-permute-start.14 = (bf16[6,256,128]{2,1,0:T(8,128)(2,1)S(1)}, bf16[6,256,128]{2,1,0:T(8,128)(2,1)S(1)}, u32[]{:S(2)}, u32[]{:S(2)}) collective-permute-start(bf16[6,256,128]{2,1,0:T(8,128)(2,1)S(1)} %get-tuple-element.38), channel_id=1, source_target_pairs={{0,1},{1,2},{2,3},{3,0},{4,5},{5,6},{6,7},{7,4},{8,9},{9,10},{10,1... | collective-permute-start | bytes 1179656 | tf_op jit(solution)/shard_map/ppermute | solution.py:32
  36.2 19.1 %collective-permute-start.12 = (bf16[6,256,128]{2,1,0:T(8,128)(2,1)S(1)}, bf16[6,256,128]{2,1,0:T(8,128)(2,1)S(1)}, u32[]{:S(2)}, u32[]{:S(2)}) collective-permute-start(bf16[6,256,128]{2,1,0:T(8,128)(2,1)S(1)} %get-tuple-element.36), channel_id=1, source_target_pairs={{0,1},{1,2},{2,3},{3,0},{4,5},{5,6},{6,7},{7,4},{8,9},{9,10},{10,1... | collective-permute-start | bytes 1179656 | tf_op jit(solution)/shard_map/ppermute | solution.py:32
  39.3 17.7 %collective-permute-start.7 = (bf16[6,64,512]{2,1,0:T(8,128)(2,1)S(1)}, bf16[6,64,512]{2,1,0:T(8,128)(2,1)S(1)}, u32[]{:S(2)}, u32[]{:S(2)}) collective-permute-start(bf16[6,64,512]{2,1,0:T(8,128)(2,1)S(1)} %add_convert_fusion.2), channel_id=1, source_target_pairs={{0,192},{4,196},{8,200},{12,204},{16,208},{20,212},{24,216},{28,22... | collective-permute-start | bytes 1179656 | tf_op jit(solution)/shard_map/ppermute | solution.py:24
  55.3 8.7 %collective-permute-start.4 = (bf16[6,64,512]{2,1,0:T(8,128)(2,1)S(1)}, bf16[6,64,512]{2,1,0:T(8,128)(2,1)S(1)}, u32[]{:S(2)}, u32[]{:S(2)}) collective-permute-start(bf16[6,64,512]{2,1,0:T(8,128)(2,1)S(1)} %add_convert_fusion.3), channel_id=1, source_target_pairs={{0,64},{4,68},{8,72},{12,76},{16,80},{20,84},{24,88},{28,92},{32,9... | collective-permute-start | bytes 1179656 | tf_op jit(solution)/shard_map/ppermute | solution.py:24
  56.9 21.5 %collective-permute-start.11 = (bf16[6,256,128]{2,1,0:T(8,128)(2,1)S(1)}, bf16[6,256,128]{2,1,0:T(8,128)(2,1)S(1)}, u32[]{:S(2)}, u32[]{:S(2)}) collective-permute-start(bf16[6,256,128]{2,1,0:T(8,128)(2,1)S(1)} %get-tuple-element.34), channel_id=1, source_target_pairs={{0,3},{1,0},{2,1},{3,2},{4,7},{5,4},{6,5},{7,6},{8,11},{9,8},{10,9... | collective-permute-start | bytes 1179656 | tf_op jit(solution)/shard_map/ppermute | solution.py:32
  57.0 20.5 %collective-permute-start.16 = (bf16[6,256,128]{2,1,0:T(8,128)(2,1)S(1)}, bf16[6,256,128]{2,1,0:T(8,128)(2,1)S(1)}, u32[]{:S(2)}, u32[]{:S(2)}) collective-permute-start(bf16[6,256,128]{2,1,0:T(8,128)(2,1)S(1)} %add_convert_fusion), channel_id=1, source_target_pairs={{0,3},{1,0},{2,1},{3,2},{4,7},{5,4},{6,5},{7,6},{8,11},{9,8},{10,9... | collective-permute-start | bytes 1179656 | tf_op jit(solution)/shard_map/ppermute | solution.py:32
  57.3 21.1 %collective-permute-start.13 = (bf16[6,256,128]{2,1,0:T(8,128)(2,1)S(1)}, bf16[6,256,128]{2,1,0:T(8,128)(2,1)S(1)}, u32[]{:S(2)}, u32[]{:S(2)}) collective-permute-start(bf16[6,256,128]{2,1,0:T(8,128)(2,1)S(1)} %add_convert_fusion.1), channel_id=1, source_target_pairs={{0,1},{1,2},{2,3},{3,0},{4,5},{5,6},{6,7},{7,4},{8,9},{9,10},{10,1... | collective-permute-start | bytes 1179656 | tf_op jit(solution)/shard_map/ppermute | solution.py:32
  64.4 16.5 %collective-permute-start.10 = (bf16[12,64,128]{2,1,0:T(8,128)(2,1)S(1)}, bf16[12,64,128]{2,1,0:T(8,128)(2,1)S(1)}, u32[]{:S(2)}, u32[]{:S(2)}) collective-permute-start(bf16[12,64,128]{2,1,0:T(8,128)(2,1)S(1)} %get-tuple-element.50), channel_id=1, source_target_pairs={{0,2},{1,3},{2,0},{3,1},{4,6},{5,7},{6,4},{7,5},{8,10},{9,11},{10,... | collective-permute-start | bytes 589832 | tf_op jit(solution)/shard_map/ppermute | solution.py:32
  64.5 17.1 %collective-permute-start.8 = (bf16[12,64,128]{2,1,0:T(8,128)(2,1)S(1)}, bf16[12,64,128]{2,1,0:T(8,128)(2,1)S(1)}, u32[]{:S(2)}, u32[]{:S(2)}) collective-permute-start(bf16[12,64,128]{2,1,0:T(8,128)(2,1)S(1)} %get-tuple-element.49), channel_id=1, source_target_pairs={{0,1},{1,2},{2,3},{3,0},{4,5},{5,6},{6,7},{7,4},{8,9},{9,10},{10,1... | collective-permute-start | bytes 589832 | tf_op jit(solution)/shard_map/ppermute | solution.py:32
  77.5 5.7 %collective-permute-start.9 = (bf16[12,64,128]{2,1,0:T(8,128)(2,1)S(1)}, bf16[12,64,128]{2,1,0:T(8,128)(2,1)S(1)}, u32[]{:S(2)}, u32[]{:S(2)}) collective-permute-start(bf16[12,64,128]{2,1,0:T(8,128)(2,1)S(1)} %get-tuple-element.51), channel_id=1, source_target_pairs={{0,3},{1,0},{2,1},{3,2},{4,7},{5,4},{6,5},{7,6},{8,11},{9,8},{10,9... | collective-permute-start | bytes 589832 | tf_op jit(solution)/shard_map/ppermute | solution.py:32
  78.7 5.7 %collective-permute-start.17 = (bf16[12,64,128]{2,1,0:T(8,128)(2,1)S(1)}, bf16[12,64,128]{2,1,0:T(8,128)(2,1)S(1)}, u32[]{:S(2)}, u32[]{:S(2)}) collective-permute-start(bf16[12,64,128]{2,1,0:T(8,128)(2,1)S(1)} %get-tuple-element.52), channel_id=1, source_target_pairs={{0,64},{4,68},{8,72},{12,76},{16,80},{20,84},{24,88},{28,92},{32,9... | collective-permute-start | bytes 589832 | tf_op jit(solution)/shard_map/ppermute | solution.py:24
  78.8 7.0 %collective-permute-start.18 = (bf16[12,64,128]{2,1,0:T(8,128)(2,1)S(1)}, bf16[12,64,128]{2,1,0:T(8,128)(2,1)S(1)}, u32[]{:S(2)}, u32[]{:S(2)}) collective-permute-start(bf16[12,64,128]{2,1,0:T(8,128)(2,1)S(1)} %get-tuple-element.54), channel_id=1, source_target_pairs={{0,192},{4,196},{8,200},{12,204},{16,208},{20,212},{24,216},{28,22... | collective-permute-start | bytes 589832 | tf_op jit(solution)/shard_map/ppermute | solution.py:24
  80.8 7.2 %collective-permute-start.19 = (bf16[12,64,128]{2,1,0:T(8,128)(2,1)S(1)}, bf16[12,64,128]{2,1,0:T(8,128)(2,1)S(1)}, u32[]{:S(2)}, u32[]{:S(2)}) collective-permute-start(bf16[12,64,128]{2,1,0:T(8,128)(2,1)S(1)} %get-tuple-element.53), channel_id=1, source_target_pairs={{0,128},{4,132},{8,136},{12,140},{16,144},{20,148},{24,152},{28,15... | collective-permute-start | bytes 589832 | tf_op jit(solution)/shard_map/ppermute | solution.py:24
  88.3 8.5 %collective-permute-start.20 = (f32[24,8,128]{2,0,1:T(8,128)S(1)}, f32[24,8,128]{2,0,1:T(8,128)S(1)}, u32[]{:S(2)}, u32[]{:S(2)}) collective-permute-start(f32[24,8,128]{2,0,1:T(8,128)S(1)} %bitcast.46), channel_id=1, source_target_pairs={{0,8},{4,12},{8,16},{12,20},{16,24},{20,28},{24,32},{28,36},{32,40... | collective-permute-start | bytes 294920 | tf_op jit(solution)/shard_map/ppermute | solution.py:28
  90.3 6.6 %collective-permute-start.24 = (f32[24,8,128]{2,0,1:T(8,128)S(1)}, f32[24,8,128]{2,0,1:T(8,128)S(1)}, u32[]{:S(2)}, u32[]{:S(2)}) collective-permute-start(f32[24,8,128]{2,0,1:T(8,128)S(1)} %bitcast.45), channel_id=1, source_target_pairs={{0,56},{4,60},{8,0},{12,4},{16,8},{20,12},{24,16},{28,20},{32,24},... | collective-permute-start | bytes 294920 | tf_op jit(solution)/shard_map/ppermute | solution.py:28
  96.8 6.3 %collective-permute-start.21 = (f32[24,8,128]{2,0,1:T(8,128)S(1)}, f32[24,8,128]{2,0,1:T(8,128)S(1)}, u32[]{:S(2)}, u32[]{:S(2)}) collective-permute-start(f32[24,8,128]{2,0,1:T(8,128)S(1)} %fusion.16), channel_id=1, source_target_pairs={{0,8},{4,12},{8,16},{12,20},{16,24},{20,28},{24,32},{28,36},{32,40... | collective-permute-start | bytes 294920 | tf_op jit(solution)/shard_map/ppermute | solution.py:28
  97.0 6.3 %collective-permute-start.25 = (f32[24,8,128]{2,0,1:T(8,128)S(1)}, f32[24,8,128]{2,0,1:T(8,128)S(1)}, u32[]{:S(2)}, u32[]{:S(2)}) collective-permute-start(f32[24,8,128]{2,0,1:T(8,128)S(1)} %fusion.13), channel_id=1, source_target_pairs={{0,56},{4,60},{8,0},{12,4},{16,8},{20,12},{24,16},{28,20},{32,24},... | collective-permute-start | bytes 294920 | tf_op jit(solution)/shard_map/ppermute | solution.py:28
  103.1 5.9 %collective-permute-start.22 = (f32[24,8,128]{2,0,1:T(8,128)S(1)}, f32[24,8,128]{2,0,1:T(8,128)S(1)}, u32[]{:S(2)}, u32[]{:S(2)}) collective-permute-start(f32[24,8,128]{2,0,1:T(8,128)S(1)} %fusion.15), channel_id=1, source_target_pairs={{0,8},{4,12},{8,16},{12,20},{16,24},{20,28},{24,32},{28,36},{32,40... | collective-permute-start | bytes 294920 | tf_op jit(solution)/shard_map/ppermute | solution.py:28
  103.3 5.9 %collective-permute-start.26 = (f32[24,8,128]{2,0,1:T(8,128)S(1)}, f32[24,8,128]{2,0,1:T(8,128)S(1)}, u32[]{:S(2)}, u32[]{:S(2)}) collective-permute-start(f32[24,8,128]{2,0,1:T(8,128)S(1)} %fusion.12), channel_id=1, source_target_pairs={{0,56},{4,60},{8,0},{12,4},{16,8},{20,12},{24,16},{28,20},{32,24},... | collective-permute-start | bytes 294920 | tf_op jit(solution)/shard_map/ppermute | solution.py:28
  109.1 5.9 %collective-permute-start.23 = (f32[24,8,128]{2,0,1:T(8,128)S(1)}, f32[24,8,128]{2,0,1:T(8,128)S(1)}, u32[]{:S(2)}, u32[]{:S(2)}) collective-permute-start(f32[24,8,128]{2,0,1:T(8,128)S(1)} %fusion.14), channel_id=1, source_target_pairs={{0,8},{4,12},{8,16},{12,20},{16,24},{20,28},{24,32},{28,36},{32,40... | collective-permute-start | bytes 294920 | tf_op jit(solution)/shard_map/ppermute | solution.py:28

commit v2 on v1

v2 whole, which is shorter than its diff:
```python
import functools

import jax
import jax.numpy as jnp
from jax import lax
from jax.experimental import pallas as pl
from jax.experimental.pallas import tpu as pltpu
from jax.sharding import PartitionSpec as P

NX, NZ, NC, NY = 4, 8, 2, 4
SLOTS = 16
SH = 64
BF, F32 = jnp.bfloat16, jnp.float32
VMEM = 24 * 1024 * 1024
SIZES = (6, 6, 6, 6)


def pair_of(x, z, c):
    return (x * NZ + z) * NC + c


COORDS = [(x, z, c) for x in range(NX) for z in range(NZ) for c in range(NC)]


def move_x(a, d):
    return lax.ppermute(a, "pair", [(pair_of(x, z, c), pair_of((x + d) % NX, z, c)) for x, z, c in COORDS])


def trade_z(a):
    groups = [[pair_of(x, z, c) for z in range(NZ)] for x in range(NX) for c in range(NC)]
    return lax.all_to_all(a, "pair", 0, 0, tiled=True, axis_index_groups=groups)


def move_y(a, d):
    return lax.ppermute(a, "red", [(y, (y + d) % NY) for y in range(NY)])


def swap_core(a):
    return lax.ppermute(a, "pair", [(pair_of(x, z, c), pair_of(x, z, 1 - c)) for x, z, c in COORDS])


def panel_kernel(pairs, coeffs, lt, r, lraw, rraw, lsem, rsem):
    p, y = lax.axis_index("pair"), lax.axis_index("red")
    x, c = p >> 4, p & 1
    copies_l, copies_r = [], []
    for side, raw, sem, copies in ((0, lraw, lsem, copies_l), (1, rraw, rsem, copies_r)):
        for k in range(SLOTS):
            device = p if k < 8 else p + 1 - 2 * c
            row = pl.multiple_of(pairs[side, (device * NY + y) * 8 + k % 8] * SH, SH)
            cp = pltpu.make_async_copy(coeffs.at[pl.ds(row, SH), :], raw.at[pl.ds(k * SH, SH), :], sem.at[k])
            cp.start()
            copies.append(cp)
    ip = lax.broadcasted_iota(jnp.int32, (256, 512), 0)
    col = lax.broadcasted_iota(jnp.int32, (256, 512), 1)
    want = (((ip >> 6) + x) & 3) * 128 + ((ip >> 3) & 7) * 16 + c * 8 + (ip & 7)
    sel = jnp.where(col == want, 1.0, 0.0).astype(BF)
    for cp in copies_l:
        cp.wait()
    for g in range(4):
        lt[g] = lax.dot_general(
            sel, lraw[pl.ds(g * 256, 256), :], (((1,), (1,)), ((), ())), preferred_element_type=F32
        ).astype(BF)
    for cp in copies_r:
        cp.wait()
    for yr in range(NY):
        col = pl.multiple_of(((y + yr) & (NY - 1)) * 128, 128)
        r[:, pl.ds(yr * 128, 128)] = rraw[:, pl.ds(col, 128)]


def panels(pairs, coeffs):
    return pl.pallas_call(
        panel_kernel,
        out_shape=tuple(jax.ShapeDtypeStruct(dims, BF) for dims in ((4, 256, 256), (1024, 512))),
        in_specs=[pl.BlockSpec(memory_space=pltpu.SMEM), pl.BlockSpec(memory_space=pl.ANY)],
        out_specs=(pl.BlockSpec(memory_space=pltpu.VMEM),) * 2,
        scratch_shapes=[
            pltpu.VMEM((1024, 512), BF),
            pltpu.VMEM((1024, 512), BF),
            pltpu.SemaphoreType.DMA((SLOTS,)),
            pltpu.SemaphoreType.DMA((SLOTS,)),
        ],
        compiler_params=pltpu.CompilerParams(vmem_limit_bytes=2 * VMEM),
        cost_estimate=pl.CostEstimate(flops=300_000_000, bytes_accessed=4_000_000, transcendentals=0),
        name="panels",
    )(pairs, coeffs)


def block_kernel(by_x, acc_at, plain_at, own_n, mate_n, lt_ref, r_ref, own_i, mate_i, earlier, far, plain, acc, own, lt, bd, half):
    step = pl.program_id(0)

    @pl.when(step == 0)
    def _():
        slot = lax.broadcasted_iota(jnp.int32, (256, 256), 1) >> 6
        for g in range(4):
            local = slot + 4 * (g % 2)
            keep = local < (own_n if g < 2 else mate_n)[0, 0]
            lt[g] = jnp.where(keep, lt_ref[g].astype(F32), 0.0).astype(BF)
        bd[...] = jnp.zeros_like(bd)

    low = lax.broadcasted_iota(jnp.int32, (SH, 128), 1) < 64
    zero = jnp.zeros((SH, 128), F32)
    for k in range(SLOTS):
        src = (own_i if k < 8 else mate_i)[k % 8].astype(F32)
        swapped = pltpu.roll(src, 64, 1)
        g, kk = k // 4, k % 4
        for odd in range(2):
            piece = src if (kk % 2) == odd else swapped
            piece = jnp.where(low, zero, piece) if kk % 2 else jnp.where(low, piece, zero)
            bd[odd, g, pl.ds(kk * SH, SH), pl.ds((kk // 2) * 128, 128)] = piece.astype(BF)
    for odd in range(2):
        for g in range(4):
            half[pl.ds(odd * 256, 256), pl.ds(g * 256, 256)] = jnp.dot(
                lt[g], bd[odd, g], preferred_element_type=F32
            ).astype(BF)
    whole = jnp.dot(half[...], r_ref[...], preferred_element_type=F32)
    for odd in range(2):
        res = whole[odd * 256 : odd * 256 + 256]
        for at, ref in ((0, own), (2, far), (plain_at, plain), (acc_at, acc)):
            part = res[at * 64 : at * 64 + 64, :] if by_x else res[:, at * 128 : at * 128 + 128]
            ref[odd] = part.astype(ref.dtype)


def block(by_x, acc_at, plain_at, first_q, nq, earlier, own_n, mate_n, lt, r, own_i, mate_i):
    rows, cols = (64, 512) if by_x else (256, 128)
    first = first_q // 2
    out = lambda dt: jax.ShapeDtypeStruct((nq, rows, cols), dt)
    spec = pl.BlockSpec((2, rows, cols), lambda s: (s, 0, 0))
    ints = pl.BlockSpec((8, SH, 128), lambda s: (0, 0, first + s))
    return pl.pallas_call(
        functools.partial(block_kernel, by_x, acc_at, plain_at),
        grid=(nq // 2,),
        out_shape=(out(BF), out(BF), out(F32), out(F32)),
        in_specs=[
            pl.BlockSpec(memory_space=pltpu.SMEM),
            pl.BlockSpec(memory_space=pltpu.SMEM),
            pl.BlockSpec((4, 256, 256), lambda s: (0, 0, 0)),
            pl.BlockSpec((1024, 512), lambda s: (0, 0)),
            ints,
            ints,
            pl.BlockSpec(memory_space=pl.ANY),
        ],
        out_specs=(spec, spec, spec, spec),
        scratch_shapes=[
            pltpu.VMEM((4, 256, 256), BF),
            pltpu.VMEM((2, 4, 256, 256), BF),
            pltpu.VMEM((512, 1024), BF),
        ],
        compiler_params=pltpu.CompilerParams(vmem_limit_bytes=VMEM),
        cost_estimate=pl.CostEstimate(flops=1_000_000, bytes_accessed=10_000, transcendentals=0),
        name="block_x" if by_x else "block_y",
    )(own_n, mate_n, lt, r, own_i, mate_i, earlier)


def after(value, *earlier):
    return lax.optimization_barrier((value,) + earlier)[0]


def tie(*values):
    return lax.optimization_barrier(values)


def on_device(integrals, coeffs, shell_pairs, block_count):
    mate_i = swap_core(integrals)
    mate_n = swap_core(block_count)
    lt, r = panels(shell_pairs.T, coeffs)

    def parts(by_x, up, first_q, earlier, nq=6):
        acc_at, plain_at = (1, 3) if up else (3, 1)
        return block(by_x, acc_at, plain_at, first_q, nq, earlier, block_count, mate_n, lt, r, integrals, mate_i)

    def join(acc, far):
        return (acc + far.astype(F32)).astype(BF)

    def total(own, plain, acc):
        return own + plain.astype(F32) + acc.astype(F32)

    na, ma, nb, mb = SIZES
    far_xa, plain_xa, acc_xa, own_xa = parts(True, True, 0, lt, na)
    f_xa = move_x(far_xa, 1)
    p_xa = move_x(plain_xa, -1)
    far_ya, plain_ya, acc_ya, own_ya = parts(False, True, na + nb, own_xa, ma)
    f_ya = move_y(far_ya, 1)
    p_ya = move_y(plain_ya, -1)
    far_xb, plain_xb, acc_xb, own_xb = parts(True, False, na, own_ya, nb)
    far_xb, plain_xb, f_xa, p_xa, own_xb = tie(far_xb, plain_xb, f_xa, p_xa, own_xb)
    f_xb = move_x(far_xb, -1)
    p_xb = move_x(plain_xb, 1)
    far_yb, plain_yb, acc_yb, own_yb = parts(False, False, na + nb + ma, own_xb, mb)
    far_yb, plain_yb, f_ya, p_ya, own_yb = tie(far_yb, plain_yb, f_ya, p_ya, own_yb)
    f_yb = move_y(far_yb, -1)
    p_yb = move_y(plain_yb, 1)
    f_xa, f_xb, p_xb, own_yb = tie(f_xa, f_xb, p_xb, own_yb)
    a_xa = move_x(join(acc_xa, f_xa), 1)
    a_xb = move_x(join(acc_xb, f_xb), -1)
    f_ya, f_yb, p_yb = tie(f_ya, f_yb, p_yb)
    a_ya = move_y(join(acc_ya, f_ya), 1)
    a_yb = move_y(join(acc_yb, f_yb), -1)
    sum_x = jnp.concatenate([total(own_xa, p_xa, a_xa), total(own_xb, p_xb, a_xb)], axis=0)
    sum_y = jnp.concatenate([total(own_ya, p_ya, a_ya), total(own_yb, p_yb, a_yb)], axis=0)

    tot_x, tot_y = sum_x[:, :, :128], sum_y[:, :64, :]
    for d in (1, 3, 2):
        tot_x = tot_x + move_y(sum_x[:, :, d * 128 : d * 128 + 128].astype(BF), d).astype(F32)
        tot_y = tot_y + move_x(sum_y[:, d * 64 : d * 64 + 64, :].astype(BF), d).astype(F32)

    tot = jnp.concatenate([tot_x, tot_y], axis=0)
    send = jnp.transpose(tot.reshape(24, NZ, 8, 128), (1, 2, 0, 3))
    zi = (lax.axis_index("pair") // NC) % NZ
    own = lax.dynamic_index_in_dim(send, zi, 0, keepdims=False)
    got = trade_z(send.astype(BF))
    return jnp.where((jnp.arange(NZ) == zi)[:, None, None, None], own[None], got.astype(F32)).sum(0)


def solution(mesh):
    return jax.shard_map(
        on_device,
        mesh=mesh,
        in_specs=(P(("pair", "red"), None, None), P(), P(), P("pair", "red")),
        out_specs=P("pair", None, "red"),
        check_vma=False,
    )
```

time: 117 us -> 91.1 us (0.78)
  waiting for transfers between devices: 54.9 us -> 33.7 us
  other arithmetic: 4.25 us -> 2.4 us
  local copies, waits for them, and re-layouts: 3.39 us -> 1.59 us
    ppermute x9, waiting for transfers between devices: 31.9 us -> 13.7 us  [move_y(): return lax.ppermute(a, 'red', [(y, (y + d) % NY) for y in range(NY)])]
    ppermute x7 -> x0, waiting for transfers between devices: 13.6 us -> none  [move_z(): lax.ppermute(a, 'pair', [(pair_of(x, z, c), pair_of(x, (z + d) % NZ, c))...]
    ppermute x7 -> x0, starting transfers between devices: 12.9 us -> none  [move_z(): lax.ppermute(a, 'pair', [(pair_of(x, z, c), pair_of(x, (z + d) % NZ, c))...]
    all_to_all x0 -> x1, waiting for transfers between devices: none -> 11.8 us  [trade_z(): return lax.all_to_all(a, 'pair', 0, 0, tiled=True, axis_index_groups=groups)]
    all_to_all x0 -> x1, starting transfers between devices: none -> 8.47 us  [trade_z(): return lax.all_to_all(a, 'pair', 0, 0, tiled=True, axis_index_groups=groups)]
    ppermute x9, starting transfers between devices: 7.59 us -> 10.9 us  [move_y(): return lax.ppermute(a, 'red', [(y, (y + d) % NY) for y in range(NY)])]
    ppermute x9, starting transfers between devices: 10.2 us -> 12 us  [move_x(): lax.ppermute(a, 'pair', [(pair_of(x, z, c), pair_of((x + d) % NX, z, c))...]
    unnamed x8 -> x4, local copies, waits for them, and re-layouts: 2.31 us -> 0.71 us
  transfers between devices with their start and end apart: 27 -> 21, of which waited for: 12 -> 11; matrix products, arithmetic and copies ran while one was open for 4% -> 2% of each run, Pallas kernels for 15% -> 18%
where the time goes in v2:
time: 91.1 us; the launch traced here: 90.8 us
  waiting for transfers between devices  33.7 us (37%)
  starting transfers between devices  31.9 us (35%)
  Pallas kernels  20.3 us (22%)
  other arithmetic  2.4 us (3%)
  local copies, waits for them, and re-layouts  1.59 us (2%)
    pallas_call x4, Pallas kernels, block(): pl.pallas_call(functools.partial(block_kernel, by_x, acc_at, plain_at), g...  17 us
    ppermute x9, waiting for transfers between devices, move_y(): return lax.ppermute(a, 'red', [(y, (y + d) % NY) for y in range(NY)])  13.7 us
    ppermute x9, starting transfers between devices, move_x(): lax.ppermute(a, 'pair', [(pair_of(x, z, c), pair_of((x + d) % NX, z, c))...  12 us
    all_to_all x1, waiting for transfers between devices, trade_z(): return lax.all_to_all(a, 'pair', 0, 0, tiled=True, axis_index_groups=groups)  11.8 us
    ppermute x9, starting transfers between devices, move_y(): return lax.ppermute(a, 'red', [(y, (y + d) % NY) for y in range(NY)])  10.9 us
    all_to_all x1, starting transfers between devices, trade_z(): return lax.all_to_all(a, 'pair', 0, 0, tiled=True, axis_index_groups=groups)  8.47 us
    ppermute x9, waiting for transfers between devices, move_x(): lax.ppermute(a, 'pair', [(pair_of(x, z, c), pair_of((x + d) % NX, z, c))...  8.22 us
    pallas_call x1, Pallas kernels, panels(): pl.pallas_call(panel_kernel, out_shape=tuple((jax.ShapeDtypeStruct(dims,...  3.33 us
  transfers between devices with their start and end apart: 21, of which 11 were waited for; matrix products, arithmetic and copies ran while one was open for 2% of the time, Pallas kernels for 18%

profile of v2, /device:TPU:6, one launch (start us, length us, event | category | flops | bytes accessed | tf_op | source)
XLA Modules:
  0.0 90.8 jit_solution(8897147761181967693)
XLA Ops:
  0.0 0.5 collective-permute-start
  1.2 0.7 copy-done.1
  1.9 3.3 %panels.1 = (bf16[4,256,256]{2,1,0:T(8,128)(2,1)S(1)}, bf16[1024,512]{1,0:T(8,128)(2,1)S(1)}) custom-call(s32[2,2048]{1,0:T(2,128)S(1)} %bitcast.10, bf16[6016,512]{1,0:T(8,128)(2,1)} %coeffs.1), custom_call_target="tpu_custom_call" | custom-call | flops 300000000 | bytes 4000000 | tf_op jit(solution)/shard_map/panels/pallas_call | solution.py:71
  5.3 4.2 %block_x.2 = (bf16[6,64,512]{2,1,0:T(8,128)(2,1)S(1)}, bf16[6,64,512]{2,1,0:T(8,128)(2,1)S(1)}, f32[6,64,512]{2,1,0:T(8,128)S(1)}, f32[6,64,512]{2,1,0:T(8,128)S(1)}) custom-call(s32[1,1]{1,0:T(1,128)S(6)} %copy.12.own_n, s32[1,1]{1,0:T(1,128)} %collective-permute-done.mate_n, bf16[4,256,256]{2,1,0:T(8,128)(2,1)S(1)} %get-tuple-element.40.lt_ref.earlier, ...), custom_call_target="tpu_custom_call" | custom-call | flops 1000000 | bytes 10000 | tf_op jit(solution)/shard_map/block_x/pallas_call | solution.py:129
  9.5 2.3 %collective-permute-start.2 = (bf16[6,64,512]{2,1,0:T(8,128)(2,1)S(1)}, bf16[6,64,512]{2,1,0:T(8,128)(2,1)S(1)}, u32[]{:S(2)}, u32[]{:S(2)}) collective-permute-start(bf16[6,64,512]{2,1,0:T(8,128)(2,1)S(1)} %get-tuple-element.46), channel_id=1, source_target_pairs={{0,64},{4,68},{8,72},{12,76},{16,80},{20,84},{24,88},{28,92},{32,9... | collective-permute-start | bytes 1179656 | tf_op jit(solution)/shard_map/ppermute | solution.py:26
  11.8 4.2 %block_y.2 = (bf16[6,256,128]{2,1,0:T(8,128)(2,1)S(1)}, bf16[6,256,128]{2,1,0:T(8,128)(2,1)S(1)}, f32[6,256,128]{2,1,0:T(8,128)S(1)}, f32[6,256,128]{2,1,0:T(8,128)S(1)}) custom-call(s32[1,1]{1,0:T(1,128)S(6)} %copy.12.own_n, s32[1,1]{1,0:T(1,128)} %collective-permute-done.mate_n, bf16[4,256,256]{2,1,0:T(8,128)(2,1)S(1)} %get-tuple-element.40.lt_ref.earlier, ...), custom_call_target="tpu_custom_call" | custom-call | flops 1000000 | bytes 10000 | tf_op jit(solution)/shard_map/block_y/pallas_call | solution.py:129
  16.0 1.5 %collective-permute-start.6 = (bf16[6,256,128]{2,1,0:T(8,128)(2,1)S(1)}, bf16[6,256,128]{2,1,0:T(8,128)(2,1)S(1)}, u32[]{:S(2)}, u32[]{:S(2)}) collective-permute-start(bf16[6,256,128]{2,1,0:T(8,128)(2,1)S(1)} %get-tuple-element.57), channel_id=1, source_target_pairs={{0,1},{1,2},{2,3},{3,0},{4,5},{5,6},{6,7},{7,4},{8,9},{9,10},{10,1... | collective-permute-start | bytes 1179656 | tf_op jit(solution)/shard_map/ppermute | solution.py:35
  17.5 1.8 %collective-permute-start.7 = (bf16[6,256,128]{2,1,0:T(8,128)(2,1)S(1)}, bf16[6,256,128]{2,1,0:T(8,128)(2,1)S(1)}, u32[]{:S(2)}, u32[]{:S(2)}) collective-permute-start(bf16[6,256,128]{2,1,0:T(8,128)(2,1)S(1)} %get-tuple-element.58), channel_id=1, source_target_pairs={{0,3},{1,0},{2,1},{3,2},{4,7},{5,4},{6,5},{7,6},{8,11},{9,8},{10,9... | collective-permute-start | bytes 1179656 | tf_op jit(solution)/shard_map/ppermute | solution.py:35
  19.4 4.2 %block_x.3 = (bf16[6,64,512]{2,1,0:T(8,128)(2,1)S(1)}, bf16[6,64,512]{2,1,0:T(8,128)(2,1)S(1)}, f32[6,64,512]{2,1,0:T(8,128)S(1)}, f32[6,64,512]{2,1,0:T(8,128)S(1)}) custom-call(s32[1,1]{1,0:T(1,128)S(6)} %copy.12.own_n, s32[1,1]{1,0:T(1,128)} %collective-permute-done.mate_n, bf16[4,256,256]{2,1,0:T(8,128)(2,1)S(1)} %get-tuple-element.40.lt_ref.earlier, ...), custom_call_target="tpu_custom_call" | custom-call | flops 1000000 | bytes 10000 | tf_op jit(solution)/shard_map/block_x/pallas_call | solution.py:129
  23.7 0.6 collective-permute-start.4
  24.3 2.7 %collective-permute-start.5 = (bf16[6,64,512]{2,1,0:T(8,128)(2,1)S(1)}, bf16[6,64,512]{2,1,0:T(8,128)(2,1)S(1)}, u32[]{:S(2)}, u32[]{:S(2)}) collective-permute-start(bf16[6,64,512]{2,1,0:T(8,128)(2,1)S(1)} %get-tuple-element.53), channel_id=1, source_target_pairs={{0,64},{4,68},{8,72},{12,76},{16,80},{20,84},{24,88},{28,92},{32,9... | collective-permute-start | bytes 1179656 | tf_op jit(solution)/shard_map/ppermute | solution.py:26
  27.0 4.2 %block_y.3 = (bf16[6,256,128]{2,1,0:T(8,128)(2,1)S(1)}, bf16[6,256,128]{2,1,0:T(8,128)(2,1)S(1)}, f32[6,256,128]{2,1,0:T(8,128)S(1)}, f32[6,256,128]{2,1,0:T(8,128)S(1)}) custom-call(s32[1,1]{1,0:T(1,128)S(6)} %copy.12.own_n, s32[1,1]{1,0:T(1,128)} %collective-permute-done.mate_n, bf16[4,256,256]{2,1,0:T(8,128)(2,1)S(1)} %get-tuple-element.40.lt_ref.earlier, ...), custom_call_target="tpu_custom_call" | custom-call | flops 1000000 | bytes 10000 | tf_op jit(solution)/shard_map/block_y/pallas_call | solution.py:129
  31.3 1.6 %collective-permute-start.13 = (bf16[6,256,128]{2,1,0:T(8,128)(2,1)S(1)}, bf16[6,256,128]{2,1,0:T(8,128)(2,1)S(1)}, u32[]{:S(2)}, u32[]{:S(2)}) collective-permute-start(bf16[6,256,128]{2,1,0:T(8,128)(2,1)S(1)} %get-tuple-element.68), channel_id=1, source_target_pairs={{0,3},{1,0},{2,1},{3,2},{4,7},{5,4},{6,5},{7,6},{8,11},{9,8},{10,9... | collective-permute-start | bytes 1179656 | tf_op jit(solution)/shard_map/ppermute | solution.py:35
  33.4 1.7 %collective-permute-done.4 = bf16[6,64,512]{2,1,0:T(8,128)(2,1)S(1)} collective-permute-done((bf16[6,64,512]{2,1,0:T(8,128)(2,1)S(1)}, bf16[6,64,512]{2,1,0:T(8,128)(2,1)S(1)}, u32[]{:S(2)}, u32[]{:S(2)}) %collective-permute-start.4) | collective-permute-done | bytes 393248 | tf_op jit(solution)/shard_map/ppermute | solution.py:26
  35.2 1.2 %collective-permute-start.9 = (bf16[6,64,512]{2,1,0:T(8,128)(2,1)S(1)}, bf16[6,64,512]{2,1,0:T(8,128)(2,1)S(1)}, u32[]{:S(2)}, u32[]{:S(2)}) collective-permute-start(bf16[6,64,512]{2,1,0:T(8,128)(2,1)S(1)} %add_convert_fusion.2), channel_id=1, source_target_pairs={{0,192},{4,196},{8,200},{12,204},{16,208},{20,212},{24,216},{28,22... | collective-permute-start | bytes 1179656 | tf_op jit(solution)/shard_map/ppermute | solution.py:26
  36.6 2.2 %collective-permute-start.8 = (bf16[6,64,512]{2,1,0:T(8,128)(2,1)S(1)}, bf16[6,64,512]{2,1,0:T(8,128)(2,1)S(1)}, u32[]{:S(2)}, u32[]{:S(2)}) collective-permute-start(bf16[6,64,512]{2,1,0:T(8,128)(2,1)S(1)} %add_convert_fusion.3), channel_id=1, source_target_pairs={{0,64},{4,68},{8,72},{12,76},{16,80},{20,84},{24,88},{28,92},{32,9... | collective-permute-start | bytes 1179656 | tf_op jit(solution)/shard_map/ppermute | solution.py:26
  38.7 2.2 %collective-permute-done.13 = bf16[6,256,128]{2,1,0:T(8,128)(2,1)S(1)} collective-permute-done((bf16[6,256,128]{2,1,0:T(8,128)(2,1)S(1)}, bf16[6,256,128]{2,1,0:T(8,128)(2,1)S(1)}, u32[]{:S(2)}, u32[]{:S(2)}) %collective-permute-start.13) | collective-permute-done | bytes 393248 | tf_op jit(solution)/shard_map/ppermute | solution.py:35
  41.0 2.2 %collective-permute-done.14 = bf16[6,256,128]{2,1,0:T(8,128)(2,1)S(1)} collective-permute-done((bf16[6,256,128]{2,1,0:T(8,128)(2,1)S(1)}, bf16[6,256,128]{2,1,0:T(8,128)(2,1)S(1)}, u32[]{:S(2)}, u32[]{:S(2)}) %collective-permute-start.14) | collective-permute-done | bytes 393248 | tf_op jit(solution)/shard_map/ppermute | solution.py:35
  43.7 1.8 %collective-permute-start.15 = (bf16[6,256,128]{2,1,0:T(8,128)(2,1)S(1)}, bf16[6,256,128]{2,1,0:T(8,128)(2,1)S(1)}, u32[]{:S(2)}, u32[]{:S(2)}) collective-permute-start(bf16[6,256,128]{2,1,0:T(8,128)(2,1)S(1)} %add_convert_fusion.1), channel_id=1, source_target_pairs={{0,1},{1,2},{2,3},{3,0},{4,5},{5,6},{6,7},{7,4},{8,9},{9,10},{10,1... | collective-permute-start | bytes 1179656 | tf_op jit(solution)/shard_map/ppermute | solution.py:35
  46.5 3.2 %collective-permute-start.11 = (bf16[12,64,128]{2,1,0:T(8,128)(2,1)S(1)}, bf16[12,64,128]{2,1,0:T(8,128)(2,1)S(1)}, u32[]{:S(2)}, u32[]{:S(2)}) collective-permute-start(bf16[12,64,128]{2,1,0:T(8,128)(2,1)S(1)} %get-tuple-element.77), channel_id=1, source_target_pairs={{0,3},{1,0},{2,1},{3,2},{4,7},{5,4},{6,5},{7,6},{8,11},{9,8},{10,9... | collective-permute-start | bytes 589832 | tf_op jit(solution)/shard_map/ppermute | solution.py:35
  49.7 7.6 %collective-permute-done.15 = bf16[6,256,128]{2,1,0:T(8,128)(2,1)S(1)} collective-permute-done((bf16[6,256,128]{2,1,0:T(8,128)(2,1)S(1)}, bf16[6,256,128]{2,1,0:T(8,128)(2,1)S(1)}, u32[]{:S(2)}, u32[]{:S(2)}) %collective-permute-start.15) | collective-permute-done | bytes 393248 | tf_op jit(solution)/shard_map/ppermute | solution.py:35
  57.7 1.1 %collective-permute-start.17 = (bf16[12,64,128]{2,1,0:T(8,128)(2,1)S(1)}, bf16[12,64,128]{2,1,0:T(8,128)(2,1)S(1)}, u32[]{:S(2)}, u32[]{:S(2)}) collective-permute-start(bf16[12,64,128]{2,1,0:T(8,128)(2,1)S(1)} %get-tuple-element.78), channel_id=1, source_target_pairs={{0,64},{4,68},{8,72},{12,76},{16,80},{20,84},{24,88},{28,92},{32,9... | collective-permute-start | bytes 589832 | tf_op jit(solution)/shard_map/ppermute | solution.py:26
  58.8 1.1 %collective-permute-start.18 = (bf16[12,64,128]{2,1,0:T(8,128)(2,1)S(1)}, bf16[12,64,128]{2,1,0:T(8,128)(2,1)S(1)}, u32[]{:S(2)}, u32[]{:S(2)}) collective-permute-start(bf16[12,64,128]{2,1,0:T(8,128)(2,1)S(1)} %get-tuple-element.80), channel_id=1, source_target_pairs={{0,192},{4,196},{8,200},{12,204},{16,208},{20,212},{24,216},{28,22... | collective-permute-start | bytes 589832 | tf_op jit(solution)/shard_map/ppermute | solution.py:26
  59.8 1.7 %collective-permute-done.10 = bf16[12,64,128]{2,1,0:T(8,128)(2,1)S(1)} collective-permute-done((bf16[12,64,128]{2,1,0:T(8,128)(2,1)S(1)}, bf16[12,64,128]{2,1,0:T(8,128)(2,1)S(1)}, u32[]{:S(2)}, u32[]{:S(2)}) %collective-permute-start.10) | collective-permute-done | bytes 196640 | tf_op jit(solution)/shard_map/ppermute | solution.py:35
  61.5 0.9 collective-permute-start.19
  62.5 0.9 %collective-permute-done.17 = bf16[12,64,128]{2,1,0:T(8,128)(2,1)S(1)} collective-permute-done((bf16[12,64,128]{2,1,0:T(8,128)(2,1)S(1)}, bf16[12,64,128]{2,1,0:T(8,128)(2,1)S(1)}, u32[]{:S(2)}, u32[]{:S(2)}) %collective-permute-start.17) | collective-permute-done | bytes 196640 | tf_op jit(solution)/shard_map/ppermute | solution.py:26
  63.5 2.2 %collective-permute-done.18 = bf16[12,64,128]{2,1,0:T(8,128)(2,1)S(1)} collective-permute-done((bf16[12,64,128]{2,1,0:T(8,128)(2,1)S(1)}, bf16[12,64,128]{2,1,0:T(8,128)(2,1)S(1)}, u32[]{:S(2)}, u32[]{:S(2)}) %collective-permute-start.18) | collective-permute-done | bytes 196640 | tf_op jit(solution)/shard_map/ppermute | solution.py:26
  65.6 3.1 %collective-permute-done.19 = bf16[12,64,128]{2,1,0:T(8,128)(2,1)S(1)} collective-permute-done((bf16[12,64,128]{2,1,0:T(8,128)(2,1)S(1)}, bf16[12,64,128]{2,1,0:T(8,128)(2,1)S(1)}, u32[]{:S(2)}, u32[]{:S(2)}) %collective-permute-start.19) | collective-permute-done | bytes 196640 | tf_op jit(solution)/shard_map/ppermute | solution.py:26
  68.8 0.8 fusion.2
  69.6 8.5 %all-to-all-start = ((bf16[8,8,24,128]{3,1,2,0:T(8,128)(2,1)}), bf16[8,8,24,128]{3,1,2,0:T(8,128)(2,1)S(1)}, u32[]{:S(2)}, u32[]{:S(2)}) async-start(bf16[8,8,24,128]{3,1,2,0:T(8,128)(2,1)} %fusion.2), calls=%async_computation | async-start | bytes 786432 | tf_op jit(solution)/shard_map/all_to_all | solution.py:31
  78.2 11.8 %all-to-all-done = bf16[8,8,24,128]{3,1,2,0:T(8,128)(2,1)S(1)} async-done(((bf16[8,8,24,128]{3,1,2,0:T(8,128)(2,1)}), bf16[8,8,24,128]{3,1,2,0:T(8,128)(2,1)S(1)}, u32[]{:S(2)}, u32[]{:S(2)}) %all-to-all-start) | async-done | bytes 393248 | tf_op jit(solution)/shard_map/all_to_all | solution.py:31
  90.1 0.7 copy.7
  (39 shorter events, 3.2 us)
Async XLA Ops:
  0.0 5.2 %collective-permute-start.1 = (bf16[8,64,1536]{2,1,0:T(8,128)(2,1)}, bf16[8,64,1536]{2,1,0:T(8,128)(2,1)S(1)}, u32[]{:S(2)}, u32[]{:S(2)}) collective-permute-start(bf16[8,64,1536]{2,1,0:T(8,128)(2,1)} %own_i.7), channel_id=1, source_target_pairs={{0,4},{4,0},{8,12},{12,8},{16,20},{20,16},{24,28},{28,24},{32,36},... | collective-permute-start | bytes 4718600 | tf_op jit(solution)/shard_map/ppermute | solution.py:39
  0.0 5.2 %collective-permute-start = (s32[1,1]{1,0:T(1,128)}, s32[1,1]{1,0:T(1,128)}, u32[]{:S(2)}, u32[]{:S(2)}) collective-permute-start(s32[1,1]{1,0:T(1,128)} %param.7), channel_id=1, source_target_pairs={{0,4},{4,0},{8,12},{12,8},{16,20},{20,16},{24,28},{28,24},{32,36},... | collective-permute-start | bytes 20 | tf_op jit(solution)/shard_map/ppermute | solution.py:39
  1.2 0.7 copy-start.1
  1.9 3.4 %copy-start = (bf16[8,64,1536]{2,1,0:T(8,128)(2,1)S(1)}, bf16[8,64,1536]{2,1,0:T(8,128)(2,1)}, u32[]{:S(2)}) copy-start(bf16[8,64,1536]{2,1,0:T(8,128)(2,1)} %own_i.7) | copy-start | bytes 4718596
  9.5 14.1 %collective-permute-start.2 = (bf16[6,64,512]{2,1,0:T(8,128)(2,1)S(1)}, bf16[6,64,512]{2,1,0:T(8,128)(2,1)S(1)}, u32[]{:S(2)}, u32[]{:S(2)}) collective-permute-start(bf16[6,64,512]{2,1,0:T(8,128)(2,1)S(1)} %get-tuple-element.46), channel_id=1, source_target_pairs={{0,64},{4,68},{8,72},{12,76},{16,80},{20,84},{24,88},{28,92},{32,9... | collective-permute-start | bytes 1179656 | tf_op jit(solution)/shard_map/ppermute | solution.py:26
  11.8 12.0 %collective-permute-start.3 = (bf16[6,64,512]{2,1,0:T(8,128)(2,1)S(1)}, bf16[6,64,512]{2,1,0:T(8,128)(2,1)S(1)}, u32[]{:S(2)}, u32[]{:S(2)}) collective-permute-start(bf16[6,64,512]{2,1,0:T(8,128)(2,1)S(1)} %get-tuple-element.47), channel_id=1, source_target_pairs={{0,192},{4,196},{8,200},{12,204},{16,208},{20,212},{24,216},{28,22... | collective-permute-start | bytes 1179656 | tf_op jit(solution)/shard_map/ppermute | solution.py:26
  16.0 15.2 %collective-permute-start.6 = (bf16[6,256,128]{2,1,0:T(8,128)(2,1)S(1)}, bf16[6,256,128]{2,1,0:T(8,128)(2,1)S(1)}, u32[]{:S(2)}, u32[]{:S(2)}) collective-permute-start(bf16[6,256,128]{2,1,0:T(8,128)(2,1)S(1)} %get-tuple-element.57), channel_id=1, source_target_pairs={{0,1},{1,2},{2,3},{3,0},{4,5},{5,6},{6,7},{7,4},{8,9},{9,10},{10,1... | collective-permute-start | bytes 1179656 | tf_op jit(solution)/shard_map/ppermute | solution.py:35
  17.5 13.8 %collective-permute-start.7 = (bf16[6,256,128]{2,1,0:T(8,128)(2,1)S(1)}, bf16[6,256,128]{2,1,0:T(8,128)(2,1)S(1)}, u32[]{:S(2)}, u32[]{:S(2)}) collective-permute-start(bf16[6,256,128]{2,1,0:T(8,128)(2,1)S(1)} %get-tuple-element.58), channel_id=1, source_target_pairs={{0,3},{1,0},{2,1},{3,2},{4,7},{5,4},{6,5},{7,6},{8,11},{9,8},{10,9... | collective-permute-start | bytes 1179656 | tf_op jit(solution)/shard_map/ppermute | solution.py:35
  23.7 11.3 %collective-permute-start.4 = (bf16[6,64,512]{2,1,0:T(8,128)(2,1)S(1)}, bf16[6,64,512]{2,1,0:T(8,128)(2,1)S(1)}, u32[]{:S(2)}, u32[]{:S(2)}) collective-permute-start(bf16[6,64,512]{2,1,0:T(8,128)(2,1)S(1)} %get-tuple-element.52), channel_id=1, source_target_pairs={{0,192},{4,196},{8,200},{12,204},{16,208},{20,212},{24,216},{28,22... | collective-permute-start | bytes 1179656 | tf_op jit(solution)/shard_map/ppermute | solution.py:26
  24.3 10.8 %collective-permute-start.5 = (bf16[6,64,512]{2,1,0:T(8,128)(2,1)S(1)}, bf16[6,64,512]{2,1,0:T(8,128)(2,1)S(1)}, u32[]{:S(2)}, u32[]{:S(2)}) collective-permute-start(bf16[6,64,512]{2,1,0:T(8,128)(2,1)S(1)} %get-tuple-element.53), channel_id=1, source_target_pairs={{0,64},{4,68},{8,72},{12,76},{16,80},{20,84},{24,88},{28,92},{32,9... | collective-permute-start | bytes 1179656 | tf_op jit(solution)/shard_map/ppermute | solution.py:26
  31.3 9.7 %collective-permute-start.13 = (bf16[6,256,128]{2,1,0:T(8,128)(2,1)S(1)}, bf16[6,256,128]{2,1,0:T(8,128)(2,1)S(1)}, u32[]{:S(2)}, u32[]{:S(2)}) collective-permute-start(bf16[6,256,128]{2,1,0:T(8,128)(2,1)S(1)} %get-tuple-element.68), channel_id=1, source_target_pairs={{0,3},{1,0},{2,1},{3,2},{4,7},{5,4},{6,5},{7,6},{8,11},{9,8},{10,9... | collective-permute-start | bytes 1179656 | tf_op jit(solution)/shard_map/ppermute | solution.py:35
  32.9 10.2 %collective-permute-start.14 = (bf16[6,256,128]{2,1,0:T(8,128)(2,1)S(1)}, bf16[6,256,128]{2,1,0:T(8,128)(2,1)S(1)}, u32[]{:S(2)}, u32[]{:S(2)}) collective-permute-start(bf16[6,256,128]{2,1,0:T(8,128)(2,1)S(1)} %get-tuple-element.69), channel_id=1, source_target_pairs={{0,1},{1,2},{2,3},{3,0},{4,5},{5,6},{6,7},{7,4},{8,9},{9,10},{10,1... | collective-permute-start | bytes 1179656 | tf_op jit(solution)/shard_map/ppermute | solution.py:35
  35.2 10.5 %collective-permute-start.9 = (bf16[6,64,512]{2,1,0:T(8,128)(2,1)S(1)}, bf16[6,64,512]{2,1,0:T(8,128)(2,1)S(1)}, u32[]{:S(2)}, u32[]{:S(2)}) collective-permute-start(bf16[6,64,512]{2,1,0:T(8,128)(2,1)S(1)} %add_convert_fusion.2), channel_id=1, source_target_pairs={{0,192},{4,196},{8,200},{12,204},{16,208},{20,212},{24,216},{28,22... | collective-permute-start | bytes 1179656 | tf_op jit(solution)/shard_map/ppermute | solution.py:26
  36.6 9.3 %collective-permute-start.8 = (bf16[6,64,512]{2,1,0:T(8,128)(2,1)S(1)}, bf16[6,64,512]{2,1,0:T(8,128)(2,1)S(1)}, u32[]{:S(2)}, u32[]{:S(2)}) collective-permute-start(bf16[6,64,512]{2,1,0:T(8,128)(2,1)S(1)} %add_convert_fusion.3), channel_id=1, source_target_pairs={{0,64},{4,68},{8,72},{12,76},{16,80},{20,84},{24,88},{28,92},{32,9... | collective-permute-start | bytes 1179656 | tf_op jit(solution)/shard_map/ppermute | solution.py:26
  43.2 14.2 %collective-permute-start.16 = (bf16[6,256,128]{2,1,0:T(8,128)(2,1)S(1)}, bf16[6,256,128]{2,1,0:T(8,128)(2,1)S(1)}, u32[]{:S(2)}, u32[]{:S(2)}) collective-permute-start(bf16[6,256,128]{2,1,0:T(8,128)(2,1)S(1)} %add_convert_fusion), channel_id=1, source_target_pairs={{0,3},{1,0},{2,1},{3,2},{4,7},{5,4},{6,5},{7,6},{8,11},{9,8},{10,9... | collective-permute-start | bytes 1179656 | tf_op jit(solution)/shard_map/ppermute | solution.py:35
  43.7 13.6 %collective-permute-start.15 = (bf16[6,256,128]{2,1,0:T(8,128)(2,1)S(1)}, bf16[6,256,128]{2,1,0:T(8,128)(2,1)S(1)}, u32[]{:S(2)}, u32[]{:S(2)}) collective-permute-start(bf16[6,256,128]{2,1,0:T(8,128)(2,1)S(1)} %add_convert_fusion.1), channel_id=1, source_target_pairs={{0,1},{1,2},{2,3},{3,0},{4,5},{5,6},{6,7},{7,4},{8,9},{9,10},{10,1... | collective-permute-start | bytes 1179656 | tf_op jit(solution)/shard_map/ppermute | solution.py:35
  46.4 15.1 %collective-permute-start.10 = (bf16[12,64,128]{2,1,0:T(8,128)(2,1)S(1)}, bf16[12,64,128]{2,1,0:T(8,128)(2,1)S(1)}, u32[]{:S(2)}, u32[]{:S(2)}) collective-permute-start(bf16[12,64,128]{2,1,0:T(8,128)(2,1)S(1)} %get-tuple-element.75), channel_id=1, source_target_pairs={{0,1},{1,2},{2,3},{3,0},{4,5},{5,6},{6,7},{7,4},{8,9},{9,10},{10,1... | collective-permute-start | bytes 589832 | tf_op jit(solution)/shard_map/ppermute | solution.py:35
  46.5 16.0 %collective-permute-start.11 = (bf16[12,64,128]{2,1,0:T(8,128)(2,1)S(1)}, bf16[12,64,128]{2,1,0:T(8,128)(2,1)S(1)}, u32[]{:S(2)}, u32[]{:S(2)}) collective-permute-start(bf16[12,64,128]{2,1,0:T(8,128)(2,1)S(1)} %get-tuple-element.77), channel_id=1, source_target_pairs={{0,3},{1,0},{2,1},{3,2},{4,7},{5,4},{6,5},{7,6},{8,11},{9,8},{10,9... | collective-permute-start | bytes 589832 | tf_op jit(solution)/shard_map/ppermute | solution.py:35
  49.7 12.7 %collective-permute-start.12 = (bf16[12,64,128]{2,1,0:T(8,128)(2,1)S(1)}, bf16[12,64,128]{2,1,0:T(8,128)(2,1)S(1)}, u32[]{:S(2)}, u32[]{:S(2)}) collective-permute-start(bf16[12,64,128]{2,1,0:T(8,128)(2,1)S(1)} %get-tuple-element.76), channel_id=1, source_target_pairs={{0,2},{1,3},{2,0},{3,1},{4,6},{5,7},{6,4},{7,5},{8,10},{9,11},{10,... | collective-permute-start | bytes 589832 | tf_op jit(solution)/shard_map/ppermute | solution.py:35
  57.7 5.7 %collective-permute-start.17 = (bf16[12,64,128]{2,1,0:T(8,128)(2,1)S(1)}, bf16[12,64,128]{2,1,0:T(8,128)(2,1)S(1)}, u32[]{:S(2)}, u32[]{:S(2)}) collective-permute-start(bf16[12,64,128]{2,1,0:T(8,128)(2,1)S(1)} %get-tuple-element.78), channel_id=1, source_target_pairs={{0,64},{4,68},{8,72},{12,76},{16,80},{20,84},{24,88},{28,92},{32,9... | collective-permute-start | bytes 589832 | tf_op jit(solution)/shard_map/ppermute | solution.py:26
  58.8 6.9 %collective-permute-start.18 = (bf16[12,64,128]{2,1,0:T(8,128)(2,1)S(1)}, bf16[12,64,128]{2,1,0:T(8,128)(2,1)S(1)}, u32[]{:S(2)}, u32[]{:S(2)}) collective-permute-start(bf16[12,64,128]{2,1,0:T(8,128)(2,1)S(1)} %get-tuple-element.80), channel_id=1, source_target_pairs={{0,192},{4,196},{8,200},{12,204},{16,208},{20,212},{24,216},{28,22... | collective-permute-start | bytes 589832 | tf_op jit(solution)/shard_map/ppermute | solution.py:26
  61.5 7.2 %collective-permute-start.19 = (bf16[12,64,128]{2,1,0:T(8,128)(2,1)S(1)}, bf16[12,64,128]{2,1,0:T(8,128)(2,1)S(1)}, u32[]{:S(2)}, u32[]{:S(2)}) collective-permute-start(bf16[12,64,128]{2,1,0:T(8,128)(2,1)S(1)} %get-tuple-element.79), channel_id=1, source_target_pairs={{0,128},{4,132},{8,136},{12,140},{16,144},{20,148},{24,152},{28,15... | collective-permute-start | bytes 589832 | tf_op jit(solution)/shard_map/ppermute | solution.py:26
  69.6 20.4 %all-to-all-start = ((bf16[8,8,24,128]{3,1,2,0:T(8,128)(2,1)}), bf16[8,8,24,128]{3,1,2,0:T(8,128)(2,1)S(1)}, u32[]{:S(2)}, u32[]{:S(2)}) async-start(bf16[8,8,24,128]{3,1,2,0:T(8,128)(2,1)} %fusion.2), calls=%async_computation | async-start | bytes 786432 | tf_op jit(solution)/shard_map/all_to_all | solution.py:31

commit v3 on v2

--- a/solution.py
+++ b/solution.py
@@ -85,74 +85,59 @@
     )(pairs, coeffs)
 
 
-def block_kernel(by_x, acc_at, plain_at, own_n, mate_n, lt_ref, r_ref, own_i, mate_i, earlier, far, plain, acc, own, lt, bd, half):
-    step = pl.program_id(0)
-
-    @pl.when(step == 0)
-    def _():
-        slot = lax.broadcasted_iota(jnp.int32, (256, 256), 1) >> 6
-        for g in range(4):
-            local = slot + 4 * (g % 2)
-            keep = local < (own_n if g < 2 else mate_n)[0, 0]
-            lt[g] = jnp.where(keep, lt_ref[g].astype(F32), 0.0).astype(BF)
-        bd[...] = jnp.zeros_like(bd)
+def block_kernel(by_x, acc_at, plain_at, first_q, nq, own_n, mate_n, lt_ref, r, own_i, mate_i, earlier, far, plain, acc, own, lt, bd, half):
+    slot = lax.broadcasted_iota(jnp.int32, (256, 256), 1) >> 6
+    for g in range(4):
+        keep = slot + 4 * (g % 2) < (own_n if g < 2 else mate_n)[0, 0]
+        lt[g] = jnp.where(keep, lt_ref[g].astype(F32), 0.0).astype(BF)
 
     low = lax.broadcasted_iota(jnp.int32, (SH, 128), 1) < 64
     zero = jnp.zeros((SH, 128), F32)
-    for k in range(SLOTS):
-        src = (own_i if k < 8 else mate_i)[k % 8].astype(F32)
-        swapped = pltpu.roll(src, 64, 1)
-        g, kk = k // 4, k % 4
-        for odd in range(2):
-            piece = src if (kk % 2) == odd else swapped
-            piece = jnp.where(low, zero, piece) if kk % 2 else jnp.where(low, piece, zero)
-            bd[odd, g, pl.ds(kk * SH, SH), pl.ds((kk // 2) * 128, 128)] = piece.astype(BF)
-    for odd in range(2):
+    blank = jnp.zeros((SH, 128), BF)
+    for two in range(nq // 2):
+        for k in range(SLOTS):
+            src = (own_i if k < 8 else mate_i)[k % 8, :, pl.ds((first_q + 2 * two) * 64, 128)].astype(F32)
+            swapped = pltpu.roll(src, 64, 1)
+            g, kk = k // 4, k % 4
+            rows = pl.ds(kk * SH, SH)
+            for odd in range(2):
+                piece = src if (kk % 2) == odd else swapped
+                piece = jnp.where(low, zero, piece) if kk % 2 else jnp.where(low, piece, zero)
+                bd[2 * two + odd, g, rows, pl.ds((kk // 2) * 128, 128)] = piece.astype(BF)
+                bd[2 * two + odd, g, rows, pl.ds((1 - kk // 2) * 128, 128)] = blank
+    for q in range(nq):
         for g in range(4):
-            half[pl.ds(odd * 256, 256), pl.ds(g * 256, 256)] = jnp.dot(
-                lt[g], bd[odd, g], preferred_element_type=F32
+            half[pl.ds(q * 256, 256), pl.ds(g * 256, 256)] = jnp.dot(
+                lt[g], bd[q, g], preferred_element_type=F32
             ).astype(BF)
-    whole = jnp.dot(half[...], r_ref[...], preferred_element_type=F32)
-    for odd in range(2):
-        res = whole[odd * 256 : odd * 256 + 256]
+    res = jnp.dot(half[...], r[...], preferred_element_type=F32)
+    for q in range(nq):
         for at, ref in ((0, own), (2, far), (plain_at, plain), (acc_at, acc)):
-            part = res[at * 64 : at * 64 + 64, :] if by_x else res[:, at * 128 : at * 128 + 128]
-            ref[odd] = part.astype(ref.dtype)
+            if by_x:
+                part = res[q * 256 + at * 64 : q * 256 + at * 64 + 64, :]
+            else:
+                part = res[q * 256 : q * 256 + 256, at * 128 : at * 128 + 128]
+            ref[q] = part.astype(ref.dtype)
 
 
 def block(by_x, acc_at, plain_at, first_q, nq, earlier, own_n, mate_n, lt, r, own_i, mate_i):
     rows, cols = (64, 512) if by_x else (256, 128)
-    first = first_q // 2
     out = lambda dt: jax.ShapeDtypeStruct((nq, rows, cols), dt)
-    spec = pl.BlockSpec((2, rows, cols), lambda s: (s, 0, 0))
-    ints = pl.BlockSpec((8, SH, 128), lambda s: (0, 0, first + s))
+    smem, vmem = pl.BlockSpec(memory_space=pltpu.SMEM), pl.BlockSpec(memory_space=pltpu.VMEM)
     return pl.pallas_call(
-        functools.partial(block_kernel, by_x, acc_at, plain_at),
-        grid=(nq // 2,),
+        functools.partial(block_kernel, by_x, acc_at, plain_at, first_q, nq),
         out_shape=(out(BF), out(BF), out(F32), out(F32)),
-        in_specs=[
-            pl.BlockSpec(memory_space=pltpu.SMEM),
-            pl.BlockSpec(memory_space=pltpu.SMEM),
-            pl.BlockSpec((4, 256, 256), lambda s: (0, 0, 0)),
-            pl.BlockSpec((1024, 512), lambda s: (0, 0)),
-            ints,
-            ints,
-            pl.BlockSpec(memory_space=pl.ANY),
-        ],
-        out_specs=(spec, spec, spec, spec),
+        in_specs=[smem, smem, vmem, vmem, vmem, vmem, pl.BlockSpec(memory_space=pl.ANY)],
+        out_specs=(vmem,) * 4,
         scratch_shapes=[
             pltpu.VMEM((4, 256, 256), BF),
-            pltpu.VMEM((2, 4, 256, 256), BF),
-            pltpu.VMEM((512, 1024), BF),
+            pltpu.VMEM((nq, 4, 256, 256), BF),
+            pltpu.VMEM((nq * 256, 1024), BF),
         ],
         compiler_params=pltpu.CompilerParams(vmem_limit_bytes=VMEM),
         cost_estimate=pl.CostEstimate(flops=1_000_000, bytes_accessed=10_000, transcendentals=0),
         name="block_x" if by_x else "block_y",
     )(own_n, mate_n, lt, r, own_i, mate_i, earlier)
-
-
-def after(value, *earlier):
-    return lax.optimization_barrier((value,) + earlier)[0]
 
 
 def tie(*values):
@@ -189,15 +174,15 @@
     far_yb, plain_yb, f_ya, p_ya, own_yb = tie(far_yb, plain_yb, f_ya, p_ya, own_yb)
     f_yb = move_y(far_yb, -1)
     p_yb = move_y(plain_yb, 1)
-    f_xa, f_xb, p_xb, own_yb = tie(f_xa, f_xb, p_xb, own_yb)
+    f_xa, f_xb, p_xb, own_yb, f_ya = tie(f_xa, f_xb, p_xb, own_yb, f_ya)
     a_xa = move_x(join(acc_xa, f_xa), 1)
     a_xb = move_x(join(acc_xb, f_xb), -1)
-    f_ya, f_yb, p_yb = tie(f_ya, f_yb, p_yb)
     a_ya = move_y(join(acc_ya, f_ya), 1)
     a_yb = move_y(join(acc_yb, f_yb), -1)
     sum_x = jnp.concatenate([total(own_xa, p_xa, a_xa), total(own_xb, p_xb, a_xb)], axis=0)
     sum_y = jnp.concatenate([total(own_ya, p_ya, a_ya), total(own_yb, p_yb, a_yb)], axis=0)
 
+    sum_x, sum_y = tie(sum_x, sum_y)
     tot_x, tot_y = sum_x[:, :, :128], sum_y[:, :64, :]
     for d in (1, 3, 2):
         tot_x = tot_x + move_y(sum_x[:, :, d * 128 : d * 128 + 128].astype(BF), d).astype(F32)

time: 91.1 us -> 88.9 us (0.976)
  Pallas kernels: 20.3 us -> 17.7 us
    pallas_call x4, Pallas kernels: 17 us -> 14.4 us  [block(): pl.pallas_call(functools.partial(block_kernel, by_x, acc_at, plain_at, fi...]
    ppermute x9, waiting for transfers between devices: 8.22 us -> 9.21 us  [move_x(): lax.ppermute(a, 'pair', [(pair_of(x, z, c), pair_of((x + d) % NX, z, c))...]
  transfers between devices with their start and end apart: 21 -> 21, of which waited for: 11 -> 10; matrix products, arithmetic and copies ran while one was open for 2% -> 2% of each run, Pallas kernels for 18% -> 16%
where the time goes in v3:
time: 88.9 us; the launch traced here: 88.6 us
  waiting for transfers between devices  33.9 us (38%)
  starting transfers between devices  31.8 us (36%)
  Pallas kernels  17.7 us (20%)
  other arithmetic  2.65 us (3%)
  local copies, waits for them, and re-layouts  1.54 us (2%)
  between operations  0.92 us (1%)
    pallas_call x4, Pallas kernels, block(): pl.pallas_call(functools.partial(block_kernel, by_x, acc_at, plain_at, fi...  14.4 us
    ppermute x9, waiting for transfers between devices, move_y(): return lax.ppermute(a, 'red', [(y, (y + d) % NY) for y in range(NY)])  12.9 us
    ppermute x9, starting transfers between devices, move_x(): lax.ppermute(a, 'pair', [(pair_of(x, z, c), pair_of((x + d) % NX, z, c))...  12.7 us
    all_to_all x1, waiting for transfers between devices, trade_z(): return lax.all_to_all(a, 'pair', 0, 0, tiled=True, axis_index_groups=groups)  11.8 us
    ppermute x9, starting transfers between devices, move_y(): return lax.ppermute(a, 'red', [(y, (y + d) % NY) for y in range(NY)])  10.1 us
    ppermute x9, waiting for transfers between devices, move_x(): lax.ppermute(a, 'pair', [(pair_of(x, z, c), pair_of((x + d) % NX, z, c))...  9.21 us
    all_to_all x1, starting transfers between devices, trade_z(): return lax.all_to_all(a, 'pair', 0, 0, tiled=True, axis_index_groups=groups)  8.47 us
    pallas_call x1, Pallas kernels, panels(): pl.pallas_call(panel_kernel, out_shape=tuple((jax.ShapeDtypeStruct(dims,...  3.33 us
  transfers between devices with their start and end apart: 21, of which 10 were waited for; matrix products, arithmetic and copies ran while one was open for 2% of the time, Pallas kernels for 16%

profile of v3, /device:TPU:6, one launch (start us, length us, event | category | flops | bytes accessed | tf_op | source)
XLA Modules:
  0.0 88.6 jit_solution(2403858226551687614)
XLA Ops:
  0.0 0.5 collective-permute-start
  1.2 0.7 copy-done.1
  1.9 3.3 %panels.1 = (bf16[4,256,256]{2,1,0:T(8,128)(2,1)S(1)}, bf16[1024,512]{1,0:T(8,128)(2,1)S(1)}) custom-call(s32[2,2048]{1,0:T(2,128)S(1)} %bitcast.10, bf16[6016,512]{1,0:T(8,128)(2,1)} %coeffs.1), custom_call_target="tpu_custom_call" | custom-call | flops 300000000 | bytes 4000000 | tf_op jit(solution)/shard_map/panels/pallas_call | solution.py:71
  5.3 3.6 %block_x.2 = (bf16[6,64,512]{2,1,0:T(8,128)(2,1)S(1)}, bf16[6,64,512]{2,1,0:T(8,128)(2,1)S(1)}, f32[6,64,512]{2,1,0:T(8,128)S(1)}, f32[6,64,512]{2,1,0:T(8,128)S(1)}) custom-call(s32[1,1]{1,0:T(1,128)S(6)} %copy.12.own_n, s32[1,1]{1,0:T(1,128)} %collective-permute-done.mate_n, bf16[4,256,256]{2,1,0:T(8,128)(2,1)S(1)} %get-tuple-element.40.lt_ref.earlier, ...), custom_call_target="tpu_custom_call" | custom-call | flops 1000000 | bytes 10000 | tf_op jit(solution)/shard_map/block_x/pallas_call | solution.py:127
  8.8 2.3 %collective-permute-start.2 = (bf16[6,64,512]{2,1,0:T(8,128)(2,1)S(1)}, bf16[6,64,512]{2,1,0:T(8,128)(2,1)S(1)}, u32[]{:S(2)}, u32[]{:S(2)}) collective-permute-start(bf16[6,64,512]{2,1,0:T(8,128)(2,1)S(1)} %get-tuple-element.46), channel_id=1, source_target_pairs={{0,64},{4,68},{8,72},{12,76},{16,80},{20,84},{24,88},{28,92},{32,9... | collective-permute-start | bytes 1179656 | tf_op jit(solution)/shard_map/ppermute | solution.py:26
  11.1 3.6 %block_y.2 = (bf16[6,256,128]{2,1,0:T(8,128)(2,1)S(1)}, bf16[6,256,128]{2,1,0:T(8,128)(2,1)S(1)}, f32[6,256,128]{2,1,0:T(8,128)S(1)}, f32[6,256,128]{2,1,0:T(8,128)S(1)}) custom-call(s32[1,1]{1,0:T(1,128)S(6)} %copy.12.own_n, s32[1,1]{1,0:T(1,128)} %collective-permute-done.mate_n, bf16[4,256,256]{2,1,0:T(8,128)(2,1)S(1)} %get-tuple-element.40.lt_ref.earlier, ...), custom_call_target="tpu_custom_call" | custom-call | flops 1000000 | bytes 10000 | tf_op jit(solution)/shard_map/block_y/pallas_call | solution.py:127
  14.7 1.5 %collective-permute-start.6 = (bf16[6,256,128]{2,1,0:T(8,128)(2,1)S(1)}, bf16[6,256,128]{2,1,0:T(8,128)(2,1)S(1)}, u32[]{:S(2)}, u32[]{:S(2)}) collective-permute-start(bf16[6,256,128]{2,1,0:T(8,128)(2,1)S(1)} %get-tuple-element.57), channel_id=1, source_target_pairs={{0,1},{1,2},{2,3},{3,0},{4,5},{5,6},{6,7},{7,4},{8,9},{9,10},{10,1... | collective-permute-start | bytes 1179656 | tf_op jit(solution)/shard_map/ppermute | solution.py:35
  16.2 1.9 %collective-permute-start.7 = (bf16[6,256,128]{2,1,0:T(8,128)(2,1)S(1)}, bf16[6,256,128]{2,1,0:T(8,128)(2,1)S(1)}, u32[]{:S(2)}, u32[]{:S(2)}) collective-permute-start(bf16[6,256,128]{2,1,0:T(8,128)(2,1)S(1)} %get-tuple-element.58), channel_id=1, source_target_pairs={{0,3},{1,0},{2,1},{3,2},{4,7},{5,4},{6,5},{7,6},{8,11},{9,8},{10,9... | collective-permute-start | bytes 1179656 | tf_op jit(solution)/shard_map/ppermute | solution.py:35
  18.1 3.6 %block_x.3 = (bf16[6,64,512]{2,1,0:T(8,128)(2,1)S(1)}, bf16[6,64,512]{2,1,0:T(8,128)(2,1)S(1)}, f32[6,64,512]{2,1,0:T(8,128)S(1)}, f32[6,64,512]{2,1,0:T(8,128)S(1)}) custom-call(s32[1,1]{1,0:T(1,128)S(6)} %copy.12.own_n, s32[1,1]{1,0:T(1,128)} %collective-permute-done.mate_n, bf16[4,256,256]{2,1,0:T(8,128)(2,1)S(1)} %get-tuple-element.40.lt_ref.earlier, ...), custom_call_target="tpu_custom_call" | custom-call | flops 1000000 | bytes 10000 | tf_op jit(solution)/shard_map/block_x/pallas_call | solution.py:127
  21.7 1.4 %collective-permute-done.3 = bf16[6,64,512]{2,1,0:T(8,128)(2,1)S(1)} collective-permute-done((bf16[6,64,512]{2,1,0:T(8,128)(2,1)S(1)}, bf16[6,64,512]{2,1,0:T(8,128)(2,1)S(1)}, u32[]{:S(2)}, u32[]{:S(2)}) %collective-permute-start.3) | collective-permute-done | bytes 393248 | tf_op jit(solution)/shard_map/ppermute | solution.py:26
  23.1 3.2 %collective-permute-start.5 = (bf16[6,64,512]{2,1,0:T(8,128)(2,1)S(1)}, bf16[6,64,512]{2,1,0:T(8,128)(2,1)S(1)}, u32[]{:S(2)}, u32[]{:S(2)}) collective-permute-start(bf16[6,64,512]{2,1,0:T(8,128)(2,1)S(1)} %get-tuple-element.53), channel_id=1, source_target_pairs={{0,64},{4,68},{8,72},{12,76},{16,80},{20,84},{24,88},{28,92},{32,9... | collective-permute-start | bytes 1179656 | tf_op jit(solution)/shard_map/ppermute | solution.py:26
  26.3 3.6 %block_y.3 = (bf16[6,256,128]{2,1,0:T(8,128)(2,1)S(1)}, bf16[6,256,128]{2,1,0:T(8,128)(2,1)S(1)}, f32[6,256,128]{2,1,0:T(8,128)S(1)}, f32[6,256,128]{2,1,0:T(8,128)S(1)}) custom-call(s32[1,1]{1,0:T(1,128)S(6)} %copy.12.own_n, s32[1,1]{1,0:T(1,128)} %collective-permute-done.mate_n, bf16[4,256,256]{2,1,0:T(8,128)(2,1)S(1)} %get-tuple-element.40.lt_ref.earlier, ...), custom_call_target="tpu_custom_call" | custom-call | flops 1000000 | bytes 10000 | tf_op jit(solution)/shard_map/block_y/pallas_call | solution.py:127
  30.0 1.4 %collective-permute-start.12 = (bf16[6,256,128]{2,1,0:T(8,128)(2,1)S(1)}, bf16[6,256,128]{2,1,0:T(8,128)(2,1)S(1)}, u32[]{:S(2)}, u32[]{:S(2)}) collective-permute-start(bf16[6,256,128]{2,1,0:T(8,128)(2,1)S(1)} %get-tuple-element.72), channel_id=1, source_target_pairs={{0,3},{1,0},{2,1},{3,2},{4,7},{5,4},{6,5},{7,6},{8,11},{9,8},{10,9... | collective-permute-start | bytes 1179656 | tf_op jit(solution)/shard_map/ppermute | solution.py:35
  31.3 0.7 collective-permute-start.11
  32.1 2.1 %collective-permute-done.4 = bf16[6,64,512]{2,1,0:T(8,128)(2,1)S(1)} collective-permute-done((bf16[6,64,512]{2,1,0:T(8,128)(2,1)S(1)}, bf16[6,64,512]{2,1,0:T(8,128)(2,1)S(1)}, u32[]{:S(2)}, u32[]{:S(2)}) %collective-permute-start.4) | collective-permute-done | bytes 393248 | tf_op jit(solution)/shard_map/ppermute | solution.py:26
  34.6 3.2 %collective-permute-start.8 = (bf16[6,64,512]{2,1,0:T(8,128)(2,1)S(1)}, bf16[6,64,512]{2,1,0:T(8,128)(2,1)S(1)}, u32[]{:S(2)}, u32[]{:S(2)}) collective-permute-start(bf16[6,64,512]{2,1,0:T(8,128)(2,1)S(1)} %add_convert_fusion.3), channel_id=1, source_target_pairs={{0,64},{4,68},{8,72},{12,76},{16,80},{20,84},{24,88},{28,92},{32,9... | collective-permute-start | bytes 1179656 | tf_op jit(solution)/shard_map/ppermute | solution.py:26
  37.8 1.5 %collective-permute-done.12 = bf16[6,256,128]{2,1,0:T(8,128)(2,1)S(1)} collective-permute-done((bf16[6,256,128]{2,1,0:T(8,128)(2,1)S(1)}, bf16[6,256,128]{2,1,0:T(8,128)(2,1)S(1)}, u32[]{:S(2)}, u32[]{:S(2)}) %collective-permute-start.12) | collective-permute-done | bytes 393248 | tf_op jit(solution)/shard_map/ppermute | solution.py:35
  39.4 2.6 %collective-permute-start.13 = (bf16[6,256,128]{2,1,0:T(8,128)(2,1)S(1)}, bf16[6,256,128]{2,1,0:T(8,128)(2,1)S(1)}, u32[]{:S(2)}, u32[]{:S(2)}) collective-permute-start(bf16[6,256,128]{2,1,0:T(8,128)(2,1)S(1)} %add_convert_fusion), channel_id=1, source_target_pairs={{0,3},{1,0},{2,1},{3,2},{4,7},{5,4},{6,5},{7,6},{8,11},{9,8},{10,9... | collective-permute-start | bytes 1179656 | tf_op jit(solution)/shard_map/ppermute | solution.py:35
  42.4 2.1 %collective-permute-done.9 = bf16[6,64,512]{2,1,0:T(8,128)(2,1)S(1)} collective-permute-done((bf16[6,64,512]{2,1,0:T(8,128)(2,1)S(1)}, bf16[6,64,512]{2,1,0:T(8,128)(2,1)S(1)}, u32[]{:S(2)}, u32[]{:S(2)}) %collective-permute-start.9) | collective-permute-done | bytes 393248 | tf_op jit(solution)/shard_map/ppermute | solution.py:26
  45.0 6.6 %collective-permute-done.10 = bf16[6,256,128]{2,1,0:T(8,128)(2,1)S(1)} collective-permute-done((bf16[6,256,128]{2,1,0:T(8,128)(2,1)S(1)}, bf16[6,256,128]{2,1,0:T(8,128)(2,1)S(1)}, u32[]{:S(2)}, u32[]{:S(2)}) %collective-permute-start.10) | collective-permute-done | bytes 393248 | tf_op jit(solution)/shard_map/ppermute | solution.py:35
  52.2 0.5 collective-permute-start.19
  52.8 1.7 %collective-permute-start.18 = (bf16[12,64,128]{2,1,0:T(8,128)(2,1)S(1)}, bf16[12,64,128]{2,1,0:T(8,128)(2,1)S(1)}, u32[]{:S(2)}, u32[]{:S(2)}) collective-permute-start(bf16[12,64,128]{2,1,0:T(8,128)(2,1)S(1)} %get-tuple-element.80), channel_id=1, source_target_pairs={{0,192},{4,196},{8,200},{12,204},{16,208},{20,212},{24,216},{28,22... | collective-permute-start | bytes 589832 | tf_op jit(solution)/shard_map/ppermute | solution.py:26
  54.5 1.5 %collective-permute-start.17 = (bf16[12,64,128]{2,1,0:T(8,128)(2,1)S(1)}, bf16[12,64,128]{2,1,0:T(8,128)(2,1)S(1)}, u32[]{:S(2)}, u32[]{:S(2)}) collective-permute-start(bf16[12,64,128]{2,1,0:T(8,128)(2,1)S(1)} %get-tuple-element.78), channel_id=1, source_target_pairs={{0,64},{4,68},{8,72},{12,76},{16,80},{20,84},{24,88},{28,92},{32,9... | collective-permute-start | bytes 589832 | tf_op jit(solution)/shard_map/ppermute | solution.py:26
  56.3 1.7 %collective-permute-start.15 = (bf16[12,64,128]{2,1,0:T(8,128)(2,1)S(1)}, bf16[12,64,128]{2,1,0:T(8,128)(2,1)S(1)}, u32[]{:S(2)}, u32[]{:S(2)}) collective-permute-start(bf16[12,64,128]{2,1,0:T(8,128)(2,1)S(1)} %get-tuple-element.77), channel_id=1, source_target_pairs={{0,3},{1,0},{2,1},{3,2},{4,7},{5,4},{6,5},{7,6},{8,11},{9,8},{10,9... | collective-permute-start | bytes 589832 | tf_op jit(solution)/shard_map/ppermute | solution.py:35
  58.0 1.5 %collective-permute-done.19 = bf16[12,64,128]{2,1,0:T(8,128)(2,1)S(1)} collective-permute-done((bf16[12,64,128]{2,1,0:T(8,128)(2,1)S(1)}, bf16[12,64,128]{2,1,0:T(8,128)(2,1)S(1)}, u32[]{:S(2)}, u32[]{:S(2)}) %collective-permute-start.19) | collective-permute-done | bytes 196640 | tf_op jit(solution)/shard_map/ppermute | solution.py:26
  59.6 2.0 %collective-permute-done.18 = bf16[12,64,128]{2,1,0:T(8,128)(2,1)S(1)} collective-permute-done((bf16[12,64,128]{2,1,0:T(8,128)(2,1)S(1)}, bf16[12,64,128]{2,1,0:T(8,128)(2,1)S(1)}, u32[]{:S(2)}, u32[]{:S(2)}) %collective-permute-start.18) | collective-permute-done | bytes 196640 | tf_op jit(solution)/shard_map/ppermute | solution.py:26
  61.7 1.8 %collective-permute-done.16 = bf16[12,64,128]{2,1,0:T(8,128)(2,1)S(1)} collective-permute-done((bf16[12,64,128]{2,1,0:T(8,128)(2,1)S(1)}, bf16[12,64,128]{2,1,0:T(8,128)(2,1)S(1)}, u32[]{:S(2)}, u32[]{:S(2)}) %collective-permute-start.16) | collective-permute-done | bytes 196640 | tf_op jit(solution)/shard_map/ppermute | solution.py:35
  63.5 3.0 %collective-permute-done.14 = bf16[12,64,128]{2,1,0:T(8,128)(2,1)S(1)} collective-permute-done((bf16[12,64,128]{2,1,0:T(8,128)(2,1)S(1)}, bf16[12,64,128]{2,1,0:T(8,128)(2,1)S(1)}, u32[]{:S(2)}, u32[]{:S(2)}) %collective-permute-start.14) | collective-permute-done | bytes 196640 | tf_op jit(solution)/shard_map/ppermute | solution.py:35
  66.6 0.8 fusion
  67.4 8.5 %all-to-all-start = ((bf16[8,8,24,128]{3,1,2,0:T(8,128)(2,1)}), bf16[8,8,24,128]{3,1,2,0:T(8,128)(2,1)S(1)}, u32[]{:S(2)}, u32[]{:S(2)}) async-start(bf16[8,8,24,128]{3,1,2,0:T(8,128)(2,1)} %fusion), calls=%async_computation | async-start | bytes 786432 | tf_op jit(solution)/shard_map/all_to_all | solution.py:31
  76.0 11.8 %all-to-all-done = bf16[8,8,24,128]{3,1,2,0:T(8,128)(2,1)S(1)} async-done(((bf16[8,8,24,128]{3,1,2,0:T(8,128)(2,1)}), bf16[8,8,24,128]{3,1,2,0:T(8,128)(2,1)S(1)}, u32[]{:S(2)}, u32[]{:S(2)}) %all-to-all-start) | async-done | bytes 393248 | tf_op jit(solution)/shard_map/all_to_all | solution.py:31
  87.9 0.7 copy.7
  (41 shorter events, 2.7 us)
Async XLA Ops:
  0.0 5.2 %collective-permute-start.1 = (bf16[8,64,1536]{2,1,0:T(8,128)(2,1)}, bf16[8,64,1536]{2,1,0:T(8,128)(2,1)S(1)}, u32[]{:S(2)}, u32[]{:S(2)}) collective-permute-start(bf16[8,64,1536]{2,1,0:T(8,128)(2,1)} %own_i.7), channel_id=1, source_target_pairs={{0,4},{4,0},{8,12},{12,8},{16,20},{20,16},{24,28},{28,24},{32,36},... | collective-permute-start | bytes 4718600 | tf_op jit(solution)/shard_map/ppermute | solution.py:39
  0.0 5.2 %collective-permute-start = (s32[1,1]{1,0:T(1,128)}, s32[1,1]{1,0:T(1,128)}, u32[]{:S(2)}, u32[]{:S(2)}) collective-permute-start(s32[1,1]{1,0:T(1,128)} %param.7), channel_id=1, source_target_pairs={{0,4},{4,0},{8,12},{12,8},{16,20},{20,16},{24,28},{28,24},{32,36},... | collective-permute-start | bytes 20 | tf_op jit(solution)/shard_map/ppermute | solution.py:39
  1.2 0.7 copy-start.1
  1.9 3.4 %copy-start = (bf16[8,64,1536]{2,1,0:T(8,128)(2,1)S(1)}, bf16[8,64,1536]{2,1,0:T(8,128)(2,1)}, u32[]{:S(2)}) copy-start(bf16[8,64,1536]{2,1,0:T(8,128)(2,1)} %own_i.7) | copy-start | bytes 4718596
  8.8 12.8 %collective-permute-start.2 = (bf16[6,64,512]{2,1,0:T(8,128)(2,1)S(1)}, bf16[6,64,512]{2,1,0:T(8,128)(2,1)S(1)}, u32[]{:S(2)}, u32[]{:S(2)}) collective-permute-start(bf16[6,64,512]{2,1,0:T(8,128)(2,1)S(1)} %get-tuple-element.46), channel_id=1, source_target_pairs={{0,64},{4,68},{8,72},{12,76},{16,80},{20,84},{24,88},{28,92},{32,9... | collective-permute-start | bytes 1179656 | tf_op jit(solution)/shard_map/ppermute | solution.py:26
  11.1 12.0 %collective-permute-start.3 = (bf16[6,64,512]{2,1,0:T(8,128)(2,1)S(1)}, bf16[6,64,512]{2,1,0:T(8,128)(2,1)S(1)}, u32[]{:S(2)}, u32[]{:S(2)}) collective-permute-start(bf16[6,64,512]{2,1,0:T(8,128)(2,1)S(1)} %get-tuple-element.47), channel_id=1, source_target_pairs={{0,192},{4,196},{8,200},{12,204},{16,208},{20,212},{24,216},{28,22... | collective-permute-start | bytes 1179656 | tf_op jit(solution)/shard_map/ppermute | solution.py:26
  14.7 15.2 %collective-permute-start.6 = (bf16[6,256,128]{2,1,0:T(8,128)(2,1)S(1)}, bf16[6,256,128]{2,1,0:T(8,128)(2,1)S(1)}, u32[]{:S(2)}, u32[]{:S(2)}) collective-permute-start(bf16[6,256,128]{2,1,0:T(8,128)(2,1)S(1)} %get-tuple-element.57), channel_id=1, source_target_pairs={{0,1},{1,2},{2,3},{3,0},{4,5},{5,6},{6,7},{7,4},{8,9},{9,10},{10,1... | collective-permute-start | bytes 1179656 | tf_op jit(solution)/shard_map/ppermute | solution.py:35
  16.2 13.7 %collective-permute-start.7 = (bf16[6,256,128]{2,1,0:T(8,128)(2,1)S(1)}, bf16[6,256,128]{2,1,0:T(8,128)(2,1)S(1)}, u32[]{:S(2)}, u32[]{:S(2)}) collective-permute-start(bf16[6,256,128]{2,1,0:T(8,128)(2,1)S(1)} %get-tuple-element.58), channel_id=1, source_target_pairs={{0,3},{1,0},{2,1},{3,2},{4,7},{5,4},{6,5},{7,6},{8,11},{9,8},{10,9... | collective-permute-start | bytes 1179656 | tf_op jit(solution)/shard_map/ppermute | solution.py:35
  23.1 11.1 %collective-permute-start.4 = (bf16[6,64,512]{2,1,0:T(8,128)(2,1)S(1)}, bf16[6,64,512]{2,1,0:T(8,128)(2,1)S(1)}, u32[]{:S(2)}, u32[]{:S(2)}) collective-permute-start(bf16[6,64,512]{2,1,0:T(8,128)(2,1)S(1)} %get-tuple-element.52), channel_id=1, source_target_pairs={{0,192},{4,196},{8,200},{12,204},{16,208},{20,212},{24,216},{28,22... | collective-permute-start | bytes 1179656 | tf_op jit(solution)/shard_map/ppermute | solution.py:26
  23.1 11.1 %collective-permute-start.5 = (bf16[6,64,512]{2,1,0:T(8,128)(2,1)S(1)}, bf16[6,64,512]{2,1,0:T(8,128)(2,1)S(1)}, u32[]{:S(2)}, u32[]{:S(2)}) collective-permute-start(bf16[6,64,512]{2,1,0:T(8,128)(2,1)S(1)} %get-tuple-element.53), channel_id=1, source_target_pairs={{0,64},{4,68},{8,72},{12,76},{16,80},{20,84},{24,88},{28,92},{32,9... | collective-permute-start | bytes 1179656 | tf_op jit(solution)/shard_map/ppermute | solution.py:26
  30.0 9.4 %collective-permute-start.12 = (bf16[6,256,128]{2,1,0:T(8,128)(2,1)S(1)}, bf16[6,256,128]{2,1,0:T(8,128)(2,1)S(1)}, u32[]{:S(2)}, u32[]{:S(2)}) collective-permute-start(bf16[6,256,128]{2,1,0:T(8,128)(2,1)S(1)} %get-tuple-element.72), channel_id=1, source_target_pairs={{0,3},{1,0},{2,1},{3,2},{4,7},{5,4},{6,5},{7,6},{8,11},{9,8},{10,9... | collective-permute-start | bytes 1179656 | tf_op jit(solution)/shard_map/ppermute | solution.py:35
  31.3 20.5 %collective-permute-start.11 = (bf16[6,256,128]{2,1,0:T(8,128)(2,1)S(1)}, bf16[6,256,128]{2,1,0:T(8,128)(2,1)S(1)}, u32[]{:S(2)}, u32[]{:S(2)}) collective-permute-start(bf16[6,256,128]{2,1,0:T(8,128)(2,1)S(1)} %get-tuple-element.70), channel_id=1, source_target_pairs={{0,1},{1,2},{2,3},{3,0},{4,5},{5,6},{6,7},{7,4},{8,9},{9,10},{10,1... | collective-permute-start | bytes 1179656 | tf_op jit(solution)/shard_map/ppermute | solution.py:35
  34.3 10.2 %collective-permute-start.9 = (bf16[6,64,512]{2,1,0:T(8,128)(2,1)S(1)}, bf16[6,64,512]{2,1,0:T(8,128)(2,1)S(1)}, u32[]{:S(2)}, u32[]{:S(2)}) collective-permute-start(bf16[6,64,512]{2,1,0:T(8,128)(2,1)S(1)} %add_convert_fusion.2), channel_id=1, source_target_pairs={{0,192},{4,196},{8,200},{12,204},{16,208},{20,212},{24,216},{28,22... | collective-permute-start | bytes 1179656 | tf_op jit(solution)/shard_map/ppermute | solution.py:26
  34.6 10.1 %collective-permute-start.8 = (bf16[6,64,512]{2,1,0:T(8,128)(2,1)S(1)}, bf16[6,64,512]{2,1,0:T(8,128)(2,1)S(1)}, u32[]{:S(2)}, u32[]{:S(2)}) collective-permute-start(bf16[6,64,512]{2,1,0:T(8,128)(2,1)S(1)} %add_convert_fusion.3), channel_id=1, source_target_pairs={{0,64},{4,68},{8,72},{12,76},{16,80},{20,84},{24,88},{28,92},{32,9... | collective-permute-start | bytes 1179656 | tf_op jit(solution)/shard_map/ppermute | solution.py:26
  39.4 12.4 %collective-permute-start.13 = (bf16[6,256,128]{2,1,0:T(8,128)(2,1)S(1)}, bf16[6,256,128]{2,1,0:T(8,128)(2,1)S(1)}, u32[]{:S(2)}, u32[]{:S(2)}) collective-permute-start(bf16[6,256,128]{2,1,0:T(8,128)(2,1)S(1)} %add_convert_fusion), channel_id=1, source_target_pairs={{0,3},{1,0},{2,1},{3,2},{4,7},{5,4},{6,5},{7,6},{8,11},{9,8},{10,9... | collective-permute-start | bytes 1179656 | tf_op jit(solution)/shard_map/ppermute | solution.py:35
  42.1 9.6 %collective-permute-start.10 = (bf16[6,256,128]{2,1,0:T(8,128)(2,1)S(1)}, bf16[6,256,128]{2,1,0:T(8,128)(2,1)S(1)}, u32[]{:S(2)}, u32[]{:S(2)}) collective-permute-start(bf16[6,256,128]{2,1,0:T(8,128)(2,1)S(1)} %add_convert_fusion.1), channel_id=1, source_target_pairs={{0,1},{1,2},{2,3},{3,0},{4,5},{5,6},{6,7},{7,4},{8,9},{9,10},{10,1... | collective-permute-start | bytes 1179656 | tf_op jit(solution)/shard_map/ppermute | solution.py:35
  52.2 7.4 %collective-permute-start.19 = (bf16[12,64,128]{2,1,0:T(8,128)(2,1)S(1)}, bf16[12,64,128]{2,1,0:T(8,128)(2,1)S(1)}, u32[]{:S(2)}, u32[]{:S(2)}) collective-permute-start(bf16[12,64,128]{2,1,0:T(8,128)(2,1)S(1)} %get-tuple-element.79), channel_id=1, source_target_pairs={{0,128},{4,132},{8,136},{12,140},{16,144},{20,148},{24,152},{28,15... | collective-permute-start | bytes 589832 | tf_op jit(solution)/shard_map/ppermute | solution.py:26
  52.8 8.8 %collective-permute-start.18 = (bf16[12,64,128]{2,1,0:T(8,128)(2,1)S(1)}, bf16[12,64,128]{2,1,0:T(8,128)(2,1)S(1)}, u32[]{:S(2)}, u32[]{:S(2)}) collective-permute-start(bf16[12,64,128]{2,1,0:T(8,128)(2,1)S(1)} %get-tuple-element.80), channel_id=1, source_target_pairs={{0,192},{4,196},{8,200},{12,204},{16,208},{20,212},{24,216},{28,22... | collective-permute-start | bytes 589832 | tf_op jit(solution)/shard_map/ppermute | solution.py:26
  54.5 7.1 %collective-permute-start.17 = (bf16[12,64,128]{2,1,0:T(8,128)(2,1)S(1)}, bf16[12,64,128]{2,1,0:T(8,128)(2,1)S(1)}, u32[]{:S(2)}, u32[]{:S(2)}) collective-permute-start(bf16[12,64,128]{2,1,0:T(8,128)(2,1)S(1)} %get-tuple-element.78), channel_id=1, source_target_pairs={{0,64},{4,68},{8,72},{12,76},{16,80},{20,84},{24,88},{28,92},{32,9... | collective-permute-start | bytes 589832 | tf_op jit(solution)/shard_map/ppermute | solution.py:26
  56.2 7.3 %collective-permute-start.16 = (bf16[12,64,128]{2,1,0:T(8,128)(2,1)S(1)}, bf16[12,64,128]{2,1,0:T(8,128)(2,1)S(1)}, u32[]{:S(2)}, u32[]{:S(2)}) collective-permute-start(bf16[12,64,128]{2,1,0:T(8,128)(2,1)S(1)} %get-tuple-element.76), channel_id=1, source_target_pairs={{0,2},{1,3},{2,0},{3,1},{4,6},{5,7},{6,4},{7,5},{8,10},{9,11},{10,... | collective-permute-start | bytes 589832 | tf_op jit(solution)/shard_map/ppermute | solution.py:35
  56.3 7.2 %collective-permute-start.15 = (bf16[12,64,128]{2,1,0:T(8,128)(2,1)S(1)}, bf16[12,64,128]{2,1,0:T(8,128)(2,1)S(1)}, u32[]{:S(2)}, u32[]{:S(2)}) collective-permute-start(bf16[12,64,128]{2,1,0:T(8,128)(2,1)S(1)} %get-tuple-element.77), channel_id=1, source_target_pairs={{0,3},{1,0},{2,1},{3,2},{4,7},{5,4},{6,5},{7,6},{8,11},{9,8},{10,9... | collective-permute-start | bytes 589832 | tf_op jit(solution)/shard_map/ppermute | solution.py:35
  59.6 6.9 %collective-permute-start.14 = (bf16[12,64,128]{2,1,0:T(8,128)(2,1)S(1)}, bf16[12,64,128]{2,1,0:T(8,128)(2,1)S(1)}, u32[]{:S(2)}, u32[]{:S(2)}) collective-permute-start(bf16[12,64,128]{2,1,0:T(8,128)(2,1)S(1)} %get-tuple-element.75), channel_id=1, source_target_pairs={{0,1},{1,2},{2,3},{3,0},{4,5},{5,6},{6,7},{7,4},{8,9},{9,10},{10,1... | collective-permute-start | bytes 589832 | tf_op jit(solution)/shard_map/ppermute | solution.py:35
  67.4 20.4 %all-to-all-start = ((bf16[8,8,24,128]{3,1,2,0:T(8,128)(2,1)}), bf16[8,8,24,128]{3,1,2,0:T(8,128)(2,1)S(1)}, u32[]{:S(2)}, u32[]{:S(2)}) async-start(bf16[8,8,24,128]{3,1,2,0:T(8,128)(2,1)} %fusion), calls=%async_computation | async-start | bytes 786432 | tf_op jit(solution)/shard_map/all_to_all | solution.py:31

commit v4 on v3

--- a/solution.py
+++ b/solution.py
@@ -167,14 +167,14 @@
     f_ya = move_y(far_ya, 1)
     p_ya = move_y(plain_ya, -1)
     far_xb, plain_xb, acc_xb, own_xb = parts(True, False, na, own_ya, nb)
-    far_xb, plain_xb, f_xa, p_xa, own_xb = tie(far_xb, plain_xb, f_xa, p_xa, own_xb)
+    plain_xb, f_xa, p_xa, own_xb = tie(plain_xb, f_xa, p_xa, own_xb)
     f_xb = move_x(far_xb, -1)
     p_xb = move_x(plain_xb, 1)
     far_yb, plain_yb, acc_yb, own_yb = parts(False, False, na + nb + ma, own_xb, mb)
     far_yb, plain_yb, f_ya, p_ya, own_yb = tie(far_yb, plain_yb, f_ya, p_ya, own_yb)
     f_yb = move_y(far_yb, -1)
     p_yb = move_y(plain_yb, 1)
-    f_xa, f_xb, p_xb, own_yb, f_ya = tie(f_xa, f_xb, p_xb, own_yb, f_ya)
+    f_xa, f_xb, p_xb, own_yb = tie(f_xa, f_xb, p_xb, own_yb)
     a_xa = move_x(join(acc_xa, f_xa), 1)
     a_xb = move_x(join(acc_xb, f_xb), -1)
     a_ya = move_y(join(acc_ya, f_ya), 1)

time: 88.9 us -> 87.1 us (0.980)
  waiting for transfers between devices: 33.9 us -> 31.2 us
  starting transfers between devices: 31.8 us -> 32.8 us
    ppermute x9, waiting for transfers between devices: 9.21 us -> 5.22 us  [move_x(): lax.ppermute(a, 'pair', [(pair_of(x, z, c), pair_of((x + d) % NX, z, c))...]
    ppermute x9, waiting for transfers between devices: 12.9 us -> 14.2 us  [move_y(): return lax.ppermute(a, 'red', [(y, (y + d) % NY) for y in range(NY)])]
where the time goes in v4:
time: 87.1 us; the launch traced here: 86.8 us
  starting transfers between devices  32.8 us (38%)
  waiting for transfers between devices  31.2 us (36%)
  Pallas kernels  17.7 us (20%)
  other arithmetic  2.7 us (3%)
  local copies, waits for them, and re-layouts  1.54 us (2%)
  between operations  0.9 us (1%)
    pallas_call x4, Pallas kernels, block(): pl.pallas_call(functools.partial(block_kernel, by_x, acc_at, plain_at, fi...  14.4 us
    ppermute x9, waiting for transfers between devices, move_y(): return lax.ppermute(a, 'red', [(y, (y + d) % NY) for y in range(NY)])  14.2 us
    ppermute x9, starting transfers between devices, move_x(): lax.ppermute(a, 'pair', [(pair_of(x, z, c), pair_of((x + d) % NX, z, c))...  12.9 us
    all_to_all x1, waiting for transfers between devices, trade_z(): return lax.all_to_all(a, 'pair', 0, 0, tiled=True, axis_index_groups=groups)  11.8 us
    ppermute x9, starting transfers between devices, move_y(): return lax.ppermute(a, 'red', [(y, (y + d) % NY) for y in range(NY)])  10.8 us
    all_to_all x1, starting transfers between devices, trade_z(): return lax.all_to_all(a, 'pair', 0, 0, tiled=True, axis_index_groups=groups)  8.49 us
    ppermute x9, waiting for transfers between devices, move_x(): lax.ppermute(a, 'pair', [(pair_of(x, z, c), pair_of((x + d) % NX, z, c))...  5.22 us
    pallas_call x1, Pallas kernels, panels(): pl.pallas_call(panel_kernel, out_shape=tuple((jax.ShapeDtypeStruct(dims,...  3.33 us
  transfers between devices with their start and end apart: 21, of which 10 were waited for; matrix products, arithmetic and copies ran while one was open for 2% of the time, Pallas kernels for 16%

profile of v4, /device:TPU:6, one launch (start us, length us, event | category | flops | bytes accessed | tf_op | source)
XLA Modules:
  0.0 86.8 jit_solution(8444636090073604669)
XLA Ops:
  0.0 0.5 collective-permute-start
  1.2 0.7 copy-done.1
  1.9 3.3 %panels.1 = (bf16[4,256,256]{2,1,0:T(8,128)(2,1)S(1)}, bf16[1024,512]{1,0:T(8,128)(2,1)S(1)}) custom-call(s32[2,2048]{1,0:T(2,128)S(1)} %bitcast.10, bf16[6016,512]{1,0:T(8,128)(2,1)} %coeffs.1), custom_call_target="tpu_custom_call" | custom-call | flops 300000000 | bytes 4000000 | tf_op jit(solution)/shard_map/panels/pallas_call | solution.py:71
  5.3 3.6 %block_x.2 = (bf16[6,64,512]{2,1,0:T(8,128)(2,1)S(1)}, bf16[6,64,512]{2,1,0:T(8,128)(2,1)S(1)}, f32[6,64,512]{2,1,0:T(8,128)S(1)}, f32[6,64,512]{2,1,0:T(8,128)S(1)}) custom-call(s32[1,1]{1,0:T(1,128)S(6)} %copy.12.own_n, s32[1,1]{1,0:T(1,128)} %collective-permute-done.mate_n, bf16[4,256,256]{2,1,0:T(8,128)(2,1)S(1)} %get-tuple-element.38.lt_ref.earlier, ...), custom_call_target="tpu_custom_call" | custom-call | flops 1000000 | bytes 10000 | tf_op jit(solution)/shard_map/block_x/pallas_call | solution.py:127
  8.8 2.3 %collective-permute-start.2 = (bf16[6,64,512]{2,1,0:T(8,128)(2,1)S(1)}, bf16[6,64,512]{2,1,0:T(8,128)(2,1)S(1)}, u32[]{:S(2)}, u32[]{:S(2)}) collective-permute-start(bf16[6,64,512]{2,1,0:T(8,128)(2,1)S(1)} %get-tuple-element.43), channel_id=1, source_target_pairs={{0,64},{4,68},{8,72},{12,76},{16,80},{20,84},{24,88},{28,92},{32,9... | collective-permute-start | bytes 1179656 | tf_op jit(solution)/shard_map/ppermute | solution.py:26
  11.1 3.6 %block_y.2 = (bf16[6,256,128]{2,1,0:T(8,128)(2,1)S(1)}, bf16[6,256,128]{2,1,0:T(8,128)(2,1)S(1)}, f32[6,256,128]{2,1,0:T(8,128)S(1)}, f32[6,256,128]{2,1,0:T(8,128)S(1)}) custom-call(s32[1,1]{1,0:T(1,128)S(6)} %copy.12.own_n, s32[1,1]{1,0:T(1,128)} %collective-permute-done.mate_n, bf16[4,256,256]{2,1,0:T(8,128)(2,1)S(1)} %get-tuple-element.38.lt_ref.earlier, ...), custom_call_target="tpu_custom_call" | custom-call | flops 1000000 | bytes 10000 | tf_op jit(solution)/shard_map/block_y/pallas_call | solution.py:127
  14.7 1.5 %collective-permute-start.6 = (bf16[6,256,128]{2,1,0:T(8,128)(2,1)S(1)}, bf16[6,256,128]{2,1,0:T(8,128)(2,1)S(1)}, u32[]{:S(2)}, u32[]{:S(2)}) collective-permute-start(bf16[6,256,128]{2,1,0:T(8,128)(2,1)S(1)} %get-tuple-element.54), channel_id=1, source_target_pairs={{0,1},{1,2},{2,3},{3,0},{4,5},{5,6},{6,7},{7,4},{8,9},{9,10},{10,1... | collective-permute-start | bytes 1179656 | tf_op jit(solution)/shard_map/ppermute | solution.py:35
  16.2 1.9 %collective-permute-start.7 = (bf16[6,256,128]{2,1,0:T(8,128)(2,1)S(1)}, bf16[6,256,128]{2,1,0:T(8,128)(2,1)S(1)}, u32[]{:S(2)}, u32[]{:S(2)}) collective-permute-start(bf16[6,256,128]{2,1,0:T(8,128)(2,1)S(1)} %get-tuple-element.55), channel_id=1, source_target_pairs={{0,3},{1,0},{2,1},{3,2},{4,7},{5,4},{6,5},{7,6},{8,11},{9,8},{10,9... | collective-permute-start | bytes 1179656 | tf_op jit(solution)/shard_map/ppermute | solution.py:35
  18.1 3.6 %block_x.3 = (bf16[6,64,512]{2,1,0:T(8,128)(2,1)S(1)}, bf16[6,64,512]{2,1,0:T(8,128)(2,1)S(1)}, f32[6,64,512]{2,1,0:T(8,128)S(1)}, f32[6,64,512]{2,1,0:T(8,128)S(1)}) custom-call(s32[1,1]{1,0:T(1,128)S(6)} %copy.12.own_n, s32[1,1]{1,0:T(1,128)} %collective-permute-done.mate_n, bf16[4,256,256]{2,1,0:T(8,128)(2,1)S(1)} %get-tuple-element.38.lt_ref.earlier, ...), custom_call_target="tpu_custom_call" | custom-call | flops 1000000 | bytes 10000 | tf_op jit(solution)/shard_map/block_x/pallas_call | solution.py:127
  21.7 0.8 collective-permute-start.4
  22.4 0.7 collective-permute-done.3
  23.1 2.0 %collective-permute-start.5 = (bf16[6,64,512]{2,1,0:T(8,128)(2,1)S(1)}, bf16[6,64,512]{2,1,0:T(8,128)(2,1)S(1)}, u32[]{:S(2)}, u32[]{:S(2)}) collective-permute-start(bf16[6,64,512]{2,1,0:T(8,128)(2,1)S(1)} %get-tuple-element.50), channel_id=1, source_target_pairs={{0,64},{4,68},{8,72},{12,76},{16,80},{20,84},{24,88},{28,92},{32,9... | collective-permute-start | bytes 1179656 | tf_op jit(solution)/shard_map/ppermute | solution.py:26
  25.1 3.6 %block_y.3 = (bf16[6,256,128]{2,1,0:T(8,128)(2,1)S(1)}, bf16[6,256,128]{2,1,0:T(8,128)(2,1)S(1)}, f32[6,256,128]{2,1,0:T(8,128)S(1)}, f32[6,256,128]{2,1,0:T(8,128)S(1)}) custom-call(s32[1,1]{1,0:T(1,128)S(6)} %copy.12.own_n, s32[1,1]{1,0:T(1,128)} %collective-permute-done.mate_n, bf16[4,256,256]{2,1,0:T(8,128)(2,1)S(1)} %get-tuple-element.38.lt_ref.earlier, ...), custom_call_target="tpu_custom_call" | custom-call | flops 1000000 | bytes 10000 | tf_op jit(solution)/shard_map/block_y/pallas_call | solution.py:127
  28.7 1.6 %collective-permute-start.12 = (bf16[6,256,128]{2,1,0:T(8,128)(2,1)S(1)}, bf16[6,256,128]{2,1,0:T(8,128)(2,1)S(1)}, u32[]{:S(2)}, u32[]{:S(2)}) collective-permute-start(bf16[6,256,128]{2,1,0:T(8,128)(2,1)S(1)} %get-tuple-element.68), channel_id=1, source_target_pairs={{0,3},{1,0},{2,1},{3,2},{4,7},{5,4},{6,5},{7,6},{8,11},{9,8},{10,9... | collective-permute-start | bytes 1179656 | tf_op jit(solution)/shard_map/ppermute | solution.py:35
  31.1 2.1 %collective-permute-done.4 = bf16[6,64,512]{2,1,0:T(8,128)(2,1)S(1)} collective-permute-done((bf16[6,64,512]{2,1,0:T(8,128)(2,1)S(1)}, bf16[6,64,512]{2,1,0:T(8,128)(2,1)S(1)}, u32[]{:S(2)}, u32[]{:S(2)}) %collective-permute-start.4) | collective-permute-done | bytes 393248 | tf_op jit(solution)/shard_map/ppermute | solution.py:26
  33.3 1.2 %collective-permute-start.9 = (bf16[6,64,512]{2,1,0:T(8,128)(2,1)S(1)}, bf16[6,64,512]{2,1,0:T(8,128)(2,1)S(1)}, u32[]{:S(2)}, u32[]{:S(2)}) collective-permute-start(bf16[6,64,512]{2,1,0:T(8,128)(2,1)S(1)} %add_convert_fusion.2), channel_id=1, source_target_pairs={{0,192},{4,196},{8,200},{12,204},{16,208},{20,212},{24,216},{28,22... | collective-permute-start | bytes 1179656 | tf_op jit(solution)/shard_map/ppermute | solution.py:26
  34.6 2.2 %collective-permute-start.8 = (bf16[6,64,512]{2,1,0:T(8,128)(2,1)S(1)}, bf16[6,64,512]{2,1,0:T(8,128)(2,1)S(1)}, u32[]{:S(2)}, u32[]{:S(2)}) collective-permute-start(bf16[6,64,512]{2,1,0:T(8,128)(2,1)S(1)} %add_convert_fusion.3), channel_id=1, source_target_pairs={{0,64},{4,68},{8,72},{12,76},{16,80},{20,84},{24,88},{28,92},{32,9... | collective-permute-start | bytes 1179656 | tf_op jit(solution)/shard_map/ppermute | solution.py:26
  36.8 1.6 %collective-permute-done.12 = bf16[6,256,128]{2,1,0:T(8,128)(2,1)S(1)} collective-permute-done((bf16[6,256,128]{2,1,0:T(8,128)(2,1)S(1)}, bf16[6,256,128]{2,1,0:T(8,128)(2,1)S(1)}, u32[]{:S(2)}, u32[]{:S(2)}) %collective-permute-start.12) | collective-permute-done | bytes 393248 | tf_op jit(solution)/shard_map/ppermute | solution.py:35
  38.5 2.7 %collective-permute-start.13 = (bf16[6,256,128]{2,1,0:T(8,128)(2,1)S(1)}, bf16[6,256,128]{2,1,0:T(8,128)(2,1)S(1)}, u32[]{:S(2)}, u32[]{:S(2)}) collective-permute-start(bf16[6,256,128]{2,1,0:T(8,128)(2,1)S(1)} %add_convert_fusion), channel_id=1, source_target_pairs={{0,3},{1,0},{2,1},{3,2},{4,7},{5,4},{6,5},{7,6},{8,11},{9,8},{10,9... | collective-permute-start | bytes 1179656 | tf_op jit(solution)/shard_map/ppermute | solution.py:35
  41.3 7.7 %collective-permute-done.10 = bf16[6,256,128]{2,1,0:T(8,128)(2,1)S(1)} collective-permute-done((bf16[6,256,128]{2,1,0:T(8,128)(2,1)S(1)}, bf16[6,256,128]{2,1,0:T(8,128)(2,1)S(1)}, u32[]{:S(2)}, u32[]{:S(2)}) %collective-permute-start.10) | collective-permute-done | bytes 393248 | tf_op jit(solution)/shard_map/ppermute | solution.py:35
  50.1 1.3 %collective-permute-start.19 = (bf16[12,64,128]{2,1,0:T(8,128)(2,1)S(1)}, bf16[12,64,128]{2,1,0:T(8,128)(2,1)S(1)}, u32[]{:S(2)}, u32[]{:S(2)}) collective-permute-start(bf16[12,64,128]{2,1,0:T(8,128)(2,1)S(1)} %get-tuple-element.75), channel_id=1, source_target_pairs={{0,128},{4,132},{8,136},{12,140},{16,144},{20,148},{24,152},{28,15... | collective-permute-start | bytes 589832 | tf_op jit(solution)/shard_map/ppermute | solution.py:26
  51.4 2.0 %collective-permute-start.18 = (bf16[12,64,128]{2,1,0:T(8,128)(2,1)S(1)}, bf16[12,64,128]{2,1,0:T(8,128)(2,1)S(1)}, u32[]{:S(2)}, u32[]{:S(2)}) collective-permute-start(bf16[12,64,128]{2,1,0:T(8,128)(2,1)S(1)} %get-tuple-element.76), channel_id=1, source_target_pairs={{0,192},{4,196},{8,200},{12,204},{16,208},{20,212},{24,216},{28,22... | collective-permute-start | bytes 589832 | tf_op jit(solution)/shard_map/ppermute | solution.py:26
  53.4 1.2 %collective-permute-start.17 = (bf16[12,64,128]{2,1,0:T(8,128)(2,1)S(1)}, bf16[12,64,128]{2,1,0:T(8,128)(2,1)S(1)}, u32[]{:S(2)}, u32[]{:S(2)}) collective-permute-start(bf16[12,64,128]{2,1,0:T(8,128)(2,1)S(1)} %get-tuple-element.74), channel_id=1, source_target_pairs={{0,64},{4,68},{8,72},{12,76},{16,80},{20,84},{24,88},{28,92},{32,9... | collective-permute-start | bytes 589832 | tf_op jit(solution)/shard_map/ppermute | solution.py:26
  55.0 2.3 %collective-permute-start.15 = (bf16[12,64,128]{2,1,0:T(8,128)(2,1)S(1)}, bf16[12,64,128]{2,1,0:T(8,128)(2,1)S(1)}, u32[]{:S(2)}, u32[]{:S(2)}) collective-permute-start(bf16[12,64,128]{2,1,0:T(8,128)(2,1)S(1)} %get-tuple-element.73), channel_id=1, source_target_pairs={{0,3},{1,0},{2,1},{3,2},{4,7},{5,4},{6,5},{7,6},{8,11},{9,8},{10,9... | collective-permute-start | bytes 589832 | tf_op jit(solution)/shard_map/ppermute | solution.py:35
  57.8 2.0 %collective-permute-done.18 = bf16[12,64,128]{2,1,0:T(8,128)(2,1)S(1)} collective-permute-done((bf16[12,64,128]{2,1,0:T(8,128)(2,1)S(1)}, bf16[12,64,128]{2,1,0:T(8,128)(2,1)S(1)}, u32[]{:S(2)}, u32[]{:S(2)}) %collective-permute-start.18) | collective-permute-done | bytes 196640 | tf_op jit(solution)/shard_map/ppermute | solution.py:26
  59.9 2.2 %collective-permute-done.16 = bf16[12,64,128]{2,1,0:T(8,128)(2,1)S(1)} collective-permute-done((bf16[12,64,128]{2,1,0:T(8,128)(2,1)S(1)}, bf16[12,64,128]{2,1,0:T(8,128)(2,1)S(1)}, u32[]{:S(2)}, u32[]{:S(2)}) %collective-permute-start.16) | collective-permute-done | bytes 196640 | tf_op jit(solution)/shard_map/ppermute | solution.py:35
  62.1 0.8 collective-permute-done.15
  62.9 1.8 %collective-permute-done.14 = bf16[12,64,128]{2,1,0:T(8,128)(2,1)S(1)} collective-permute-done((bf16[12,64,128]{2,1,0:T(8,128)(2,1)S(1)}, bf16[12,64,128]{2,1,0:T(8,128)(2,1)S(1)}, u32[]{:S(2)}, u32[]{:S(2)}) %collective-permute-start.14) | collective-permute-done | bytes 196640 | tf_op jit(solution)/shard_map/ppermute | solution.py:35
  64.8 0.8 fusion
  65.6 8.5 %all-to-all-start = ((bf16[8,8,24,128]{3,1,2,0:T(8,128)(2,1)}), bf16[8,8,24,128]{3,1,2,0:T(8,128)(2,1)S(1)}, u32[]{:S(2)}, u32[]{:S(2)}) async-start(bf16[8,8,24,128]{3,1,2,0:T(8,128)(2,1)} %fusion), calls=%async_computation | async-start | bytes 786432 | tf_op jit(solution)/shard_map/all_to_all | solution.py:31
  74.2 11.8 %all-to-all-done = bf16[8,8,24,128]{3,1,2,0:T(8,128)(2,1)S(1)} async-done(((bf16[8,8,24,128]{3,1,2,0:T(8,128)(2,1)}), bf16[8,8,24,128]{3,1,2,0:T(8,128)(2,1)S(1)}, u32[]{:S(2)}, u32[]{:S(2)}) %all-to-all-start) | async-done | bytes 393248 | tf_op jit(solution)/shard_map/all_to_all | solution.py:31
  86.1 0.7 copy.7
  (41 shorter events, 3.4 us)
Async XLA Ops:
  0.0 5.2 %collective-permute-start.1 = (bf16[8,64,1536]{2,1,0:T(8,128)(2,1)}, bf16[8,64,1536]{2,1,0:T(8,128)(2,1)S(1)}, u32[]{:S(2)}, u32[]{:S(2)}) collective-permute-start(bf16[8,64,1536]{2,1,0:T(8,128)(2,1)} %own_i.7), channel_id=1, source_target_pairs={{0,4},{4,0},{8,12},{12,8},{16,20},{20,16},{24,28},{28,24},{32,36},... | collective-permute-start | bytes 4718600 | tf_op jit(solution)/shard_map/ppermute | solution.py:39
  0.0 5.2 %collective-permute-start = (s32[1,1]{1,0:T(1,128)}, s32[1,1]{1,0:T(1,128)}, u32[]{:S(2)}, u32[]{:S(2)}) collective-permute-start(s32[1,1]{1,0:T(1,128)} %param.7), channel_id=1, source_target_pairs={{0,4},{4,0},{8,12},{12,8},{16,20},{20,16},{24,28},{28,24},{32,36},... | collective-permute-start | bytes 20 | tf_op jit(solution)/shard_map/ppermute | solution.py:39
  1.2 0.7 copy-start.1
  1.9 3.4 %copy-start = (bf16[8,64,1536]{2,1,0:T(8,128)(2,1)S(1)}, bf16[8,64,1536]{2,1,0:T(8,128)(2,1)}, u32[]{:S(2)}) copy-start(bf16[8,64,1536]{2,1,0:T(8,128)(2,1)} %own_i.7) | copy-start | bytes 4718596
  8.8 13.6 %collective-permute-start.2 = (bf16[6,64,512]{2,1,0:T(8,128)(2,1)S(1)}, bf16[6,64,512]{2,1,0:T(8,128)(2,1)S(1)}, u32[]{:S(2)}, u32[]{:S(2)}) collective-permute-start(bf16[6,64,512]{2,1,0:T(8,128)(2,1)S(1)} %get-tuple-element.43), channel_id=1, source_target_pairs={{0,64},{4,68},{8,72},{12,76},{16,80},{20,84},{24,88},{28,92},{32,9... | collective-permute-start | bytes 1179656 | tf_op jit(solution)/shard_map/ppermute | solution.py:26
  11.1 12.0 %collective-permute-start.3 = (bf16[6,64,512]{2,1,0:T(8,128)(2,1)S(1)}, bf16[6,64,512]{2,1,0:T(8,128)(2,1)S(1)}, u32[]{:S(2)}, u32[]{:S(2)}) collective-permute-start(bf16[6,64,512]{2,1,0:T(8,128)(2,1)S(1)} %get-tuple-element.44), channel_id=1, source_target_pairs={{0,192},{4,196},{8,200},{12,204},{16,208},{20,212},{24,216},{28,22... | collective-permute-start | bytes 1179656 | tf_op jit(solution)/shard_map/ppermute | solution.py:26
  14.7 13.9 %collective-permute-start.6 = (bf16[6,256,128]{2,1,0:T(8,128)(2,1)S(1)}, bf16[6,256,128]{2,1,0:T(8,128)(2,1)S(1)}, u32[]{:S(2)}, u32[]{:S(2)}) collective-permute-start(bf16[6,256,128]{2,1,0:T(8,128)(2,1)S(1)} %get-tuple-element.54), channel_id=1, source_target_pairs={{0,1},{1,2},{2,3},{3,0},{4,5},{5,6},{6,7},{7,4},{8,9},{9,10},{10,1... | collective-permute-start | bytes 1179656 | tf_op jit(solution)/shard_map/ppermute | solution.py:35
  16.2 12.5 %collective-permute-start.7 = (bf16[6,256,128]{2,1,0:T(8,128)(2,1)S(1)}, bf16[6,256,128]{2,1,0:T(8,128)(2,1)S(1)}, u32[]{:S(2)}, u32[]{:S(2)}) collective-permute-start(bf16[6,256,128]{2,1,0:T(8,128)(2,1)S(1)} %get-tuple-element.55), channel_id=1, source_target_pairs={{0,3},{1,0},{2,1},{3,2},{4,7},{5,4},{6,5},{7,6},{8,11},{9,8},{10,9... | collective-permute-start | bytes 1179656 | tf_op jit(solution)/shard_map/ppermute | solution.py:35
  21.7 11.5 %collective-permute-start.4 = (bf16[6,64,512]{2,1,0:T(8,128)(2,1)S(1)}, bf16[6,64,512]{2,1,0:T(8,128)(2,1)S(1)}, u32[]{:S(2)}, u32[]{:S(2)}) collective-permute-start(bf16[6,64,512]{2,1,0:T(8,128)(2,1)S(1)} %get-tuple-element.49), channel_id=1, source_target_pairs={{0,192},{4,196},{8,200},{12,204},{16,208},{20,212},{24,216},{28,22... | collective-permute-start | bytes 1179656 | tf_op jit(solution)/shard_map/ppermute | solution.py:26
  23.1 10.0 %collective-permute-start.5 = (bf16[6,64,512]{2,1,0:T(8,128)(2,1)S(1)}, bf16[6,64,512]{2,1,0:T(8,128)(2,1)S(1)}, u32[]{:S(2)}, u32[]{:S(2)}) collective-permute-start(bf16[6,64,512]{2,1,0:T(8,128)(2,1)S(1)} %get-tuple-element.50), channel_id=1, source_target_pairs={{0,64},{4,68},{8,72},{12,76},{16,80},{20,84},{24,88},{28,92},{32,9... | collective-permute-start | bytes 1179656 | tf_op jit(solution)/shard_map/ppermute | solution.py:26
  28.7 9.7 %collective-permute-start.12 = (bf16[6,256,128]{2,1,0:T(8,128)(2,1)S(1)}, bf16[6,256,128]{2,1,0:T(8,128)(2,1)S(1)}, u32[]{:S(2)}, u32[]{:S(2)}) collective-permute-start(bf16[6,256,128]{2,1,0:T(8,128)(2,1)S(1)} %get-tuple-element.68), channel_id=1, source_target_pairs={{0,3},{1,0},{2,1},{3,2},{4,7},{5,4},{6,5},{7,6},{8,11},{9,8},{10,9... | collective-permute-start | bytes 1179656 | tf_op jit(solution)/shard_map/ppermute | solution.py:35
  30.3 19.4 %collective-permute-start.11 = (bf16[6,256,128]{2,1,0:T(8,128)(2,1)S(1)}, bf16[6,256,128]{2,1,0:T(8,128)(2,1)S(1)}, u32[]{:S(2)}, u32[]{:S(2)}) collective-permute-start(bf16[6,256,128]{2,1,0:T(8,128)(2,1)S(1)} %get-tuple-element.66), channel_id=1, source_target_pairs={{0,1},{1,2},{2,3},{3,0},{4,5},{5,6},{6,7},{7,4},{8,9},{9,10},{10,1... | collective-permute-start | bytes 1179656 | tf_op jit(solution)/shard_map/ppermute | solution.py:35
  30.9 18.1 %collective-permute-start.10 = (bf16[6,256,128]{2,1,0:T(8,128)(2,1)S(1)}, bf16[6,256,128]{2,1,0:T(8,128)(2,1)S(1)}, u32[]{:S(2)}, u32[]{:S(2)}) collective-permute-start(bf16[6,256,128]{2,1,0:T(8,128)(2,1)S(1)} %add_convert_fusion.1), channel_id=1, source_target_pairs={{0,1},{1,2},{2,3},{3,0},{4,5},{5,6},{6,7},{7,4},{8,9},{9,10},{10,1... | collective-permute-start | bytes 1179656 | tf_op jit(solution)/shard_map/ppermute | solution.py:35
  33.3 15.9 %collective-permute-start.9 = (bf16[6,64,512]{2,1,0:T(8,128)(2,1)S(1)}, bf16[6,64,512]{2,1,0:T(8,128)(2,1)S(1)}, u32[]{:S(2)}, u32[]{:S(2)}) collective-permute-start(bf16[6,64,512]{2,1,0:T(8,128)(2,1)S(1)} %add_convert_fusion.2), channel_id=1, source_target_pairs={{0,192},{4,196},{8,200},{12,204},{16,208},{20,212},{24,216},{28,22... | collective-permute-start | bytes 1179656 | tf_op jit(solution)/shard_map/ppermute | solution.py:26
  34.6 14.7 %collective-permute-start.8 = (bf16[6,64,512]{2,1,0:T(8,128)(2,1)S(1)}, bf16[6,64,512]{2,1,0:T(8,128)(2,1)S(1)}, u32[]{:S(2)}, u32[]{:S(2)}) collective-permute-start(bf16[6,64,512]{2,1,0:T(8,128)(2,1)S(1)} %add_convert_fusion.3), channel_id=1, source_target_pairs={{0,64},{4,68},{8,72},{12,76},{16,80},{20,84},{24,88},{28,92},{32,9... | collective-permute-start | bytes 1179656 | tf_op jit(solution)/shard_map/ppermute | solution.py:26
  38.5 11.2 %collective-permute-start.13 = (bf16[6,256,128]{2,1,0:T(8,128)(2,1)S(1)}, bf16[6,256,128]{2,1,0:T(8,128)(2,1)S(1)}, u32[]{:S(2)}, u32[]{:S(2)}) collective-permute-start(bf16[6,256,128]{2,1,0:T(8,128)(2,1)S(1)} %add_convert_fusion), channel_id=1, source_target_pairs={{0,3},{1,0},{2,1},{3,2},{4,7},{5,4},{6,5},{7,6},{8,11},{9,8},{10,9... | collective-permute-start | bytes 1179656 | tf_op jit(solution)/shard_map/ppermute | solution.py:35
  50.1 7.7 %collective-permute-start.19 = (bf16[12,64,128]{2,1,0:T(8,128)(2,1)S(1)}, bf16[12,64,128]{2,1,0:T(8,128)(2,1)S(1)}, u32[]{:S(2)}, u32[]{:S(2)}) collective-permute-start(bf16[12,64,128]{2,1,0:T(8,128)(2,1)S(1)} %get-tuple-element.75), channel_id=1, source_target_pairs={{0,128},{4,132},{8,136},{12,140},{16,144},{20,148},{24,152},{28,15... | collective-permute-start | bytes 589832 | tf_op jit(solution)/shard_map/ppermute | solution.py:26
  51.4 8.5 %collective-permute-start.18 = (bf16[12,64,128]{2,1,0:T(8,128)(2,1)S(1)}, bf16[12,64,128]{2,1,0:T(8,128)(2,1)S(1)}, u32[]{:S(2)}, u32[]{:S(2)}) collective-permute-start(bf16[12,64,128]{2,1,0:T(8,128)(2,1)S(1)} %get-tuple-element.76), channel_id=1, source_target_pairs={{0,192},{4,196},{8,200},{12,204},{16,208},{20,212},{24,216},{28,22... | collective-permute-start | bytes 589832 | tf_op jit(solution)/shard_map/ppermute | solution.py:26
  53.4 6.5 %collective-permute-start.17 = (bf16[12,64,128]{2,1,0:T(8,128)(2,1)S(1)}, bf16[12,64,128]{2,1,0:T(8,128)(2,1)S(1)}, u32[]{:S(2)}, u32[]{:S(2)}) collective-permute-start(bf16[12,64,128]{2,1,0:T(8,128)(2,1)S(1)} %get-tuple-element.74), channel_id=1, source_target_pairs={{0,64},{4,68},{8,72},{12,76},{16,80},{20,84},{24,88},{28,92},{32,9... | collective-permute-start | bytes 589832 | tf_op jit(solution)/shard_map/ppermute | solution.py:26
  54.8 7.3 %collective-permute-start.16 = (bf16[12,64,128]{2,1,0:T(8,128)(2,1)S(1)}, bf16[12,64,128]{2,1,0:T(8,128)(2,1)S(1)}, u32[]{:S(2)}, u32[]{:S(2)}) collective-permute-start(bf16[12,64,128]{2,1,0:T(8,128)(2,1)S(1)} %get-tuple-element.72), channel_id=1, source_target_pairs={{0,2},{1,3},{2,0},{3,1},{4,6},{5,7},{6,4},{7,5},{8,10},{9,11},{10,... | collective-permute-start | bytes 589832 | tf_op jit(solution)/shard_map/ppermute | solution.py:35
  55.0 7.9 %collective-permute-start.15 = (bf16[12,64,128]{2,1,0:T(8,128)(2,1)S(1)}, bf16[12,64,128]{2,1,0:T(8,128)(2,1)S(1)}, u32[]{:S(2)}, u32[]{:S(2)}) collective-permute-start(bf16[12,64,128]{2,1,0:T(8,128)(2,1)S(1)} %get-tuple-element.73), channel_id=1, source_target_pairs={{0,3},{1,0},{2,1},{3,2},{4,7},{5,4},{6,5},{7,6},{8,11},{9,8},{10,9... | collective-permute-start | bytes 589832 | tf_op jit(solution)/shard_map/ppermute | solution.py:35
  57.8 6.9 %collective-permute-start.14 = (bf16[12,64,128]{2,1,0:T(8,128)(2,1)S(1)}, bf16[12,64,128]{2,1,0:T(8,128)(2,1)S(1)}, u32[]{:S(2)}, u32[]{:S(2)}) collective-permute-start(bf16[12,64,128]{2,1,0:T(8,128)(2,1)S(1)} %get-tuple-element.71), channel_id=1, source_target_pairs={{0,1},{1,2},{2,3},{3,0},{4,5},{5,6},{6,7},{7,4},{8,9},{9,10},{10,1... | collective-permute-start | bytes 589832 | tf_op jit(solution)/shard_map/ppermute | solution.py:35
  65.6 20.4 %all-to-all-start = ((bf16[8,8,24,128]{3,1,2,0:T(8,128)(2,1)}), bf16[8,8,24,128]{3,1,2,0:T(8,128)(2,1)S(1)}, u32[]{:S(2)}, u32[]{:S(2)}) async-start(bf16[8,8,24,128]{3,1,2,0:T(8,128)(2,1)} %fusion), calls=%async_computation | async-start | bytes 786432 | tf_op jit(solution)/shard_map/all_to_all | solution.py:31

commit v5 on v4

--- a/solution.py
+++ b/solution.py
@@ -184,7 +184,7 @@
 
     sum_x, sum_y = tie(sum_x, sum_y)
     tot_x, tot_y = sum_x[:, :, :128], sum_y[:, :64, :]
-    for d in (1, 3, 2):
+    for d in (3, 1, 2):
         tot_x = tot_x + move_y(sum_x[:, :, d * 128 : d * 128 + 128].astype(BF), d).astype(F32)
         tot_y = tot_y + move_x(sum_y[:, d * 64 : d * 64 + 64, :].astype(BF), d).astype(F32)
 

time: 87.1 us -> 86.3 us (level)
    ppermute x9, waiting for transfers between devices: 14.2 us -> 12.7 us  [move_y(): return lax.ppermute(a, 'red', [(y, (y + d) % NY) for y in range(NY)])]
    ppermute x9, starting transfers between devices: 12.9 us -> 11.7 us  [move_x(): lax.ppermute(a, 'pair', [(pair_of(x, z, c), pair_of((x + d) % NX, z, c))...]
  transfers between devices with their start and end apart: 21 -> 21, of which waited for: 10 -> 11; matrix products, arithmetic and copies ran while one was open for 2% -> 2% of each run, Pallas kernels for 16% -> 16%
where the time goes in v5:
time: 86.3 us; the launch traced here: 85.6 us
  starting transfers between devices  32.2 us (37%)
  waiting for transfers between devices  30.5 us (35%)
  Pallas kernels  17.7 us (21%)
  other arithmetic  2.7 us (3%)
  local copies, waits for them, and re-layouts  1.54 us (2%)
  between operations  0.9 us (1%)
    pallas_call x4, Pallas kernels, block(): pl.pallas_call(functools.partial(block_kernel, by_x, acc_at, plain_at, fi...  14.4 us
    ppermute x9, waiting for transfers between devices, move_y(): return lax.ppermute(a, 'red', [(y, (y + d) % NY) for y in range(NY)])  12.7 us
    all_to_all x1, waiting for transfers between devices, trade_z(): return lax.all_to_all(a, 'pair', 0, 0, tiled=True, axis_index_groups=groups)  11.8 us
    ppermute x9, starting transfers between devices, move_x(): lax.ppermute(a, 'pair', [(pair_of(x, z, c), pair_of((x + d) % NX, z, c))...  11.7 us
    ppermute x9, starting transfers between devices, move_y(): return lax.ppermute(a, 'red', [(y, (y + d) % NY) for y in range(NY)])  11.5 us
    all_to_all x1, starting transfers between devices, trade_z(): return lax.all_to_all(a, 'pair', 0, 0, tiled=True, axis_index_groups=groups)  8.49 us
    ppermute x9, waiting for transfers between devices, move_x(): lax.ppermute(a, 'pair', [(pair_of(x, z, c), pair_of((x + d) % NX, z, c))...  6.07 us
    pallas_call x1, Pallas kernels, panels(): pl.pallas_call(panel_kernel, out_shape=tuple((jax.ShapeDtypeStruct(dims,...  3.33 us
  transfers between devices with their start and end apart: 21, of which 11 were waited for; matrix products, arithmetic and copies ran while one was open for 2% of the time, Pallas kernels for 16%

profile of v5, /device:TPU:6, one launch (start us, length us, event | category | flops | bytes accessed | tf_op | source)
XLA Modules:
  0.0 85.6 jit_solution(3862512815881637928)
XLA Ops:
  1.2 0.7 copy-done.1
  1.9 3.3 %panels.1 = (bf16[4,256,256]{2,1,0:T(8,128)(2,1)S(1)}, bf16[1024,512]{1,0:T(8,128)(2,1)S(1)}) custom-call(s32[2,2048]{1,0:T(2,128)S(1)} %bitcast.10, bf16[6016,512]{1,0:T(8,128)(2,1)} %coeffs.1), custom_call_target="tpu_custom_call" | custom-call | flops 300000000 | bytes 4000000 | tf_op jit(solution)/shard_map/panels/pallas_call | solution.py:71
  5.3 3.6 %block_x.2 = (bf16[6,64,512]{2,1,0:T(8,128)(2,1)S(1)}, bf16[6,64,512]{2,1,0:T(8,128)(2,1)S(1)}, f32[6,64,512]{2,1,0:T(8,128)S(1)}, f32[6,64,512]{2,1,0:T(8,128)S(1)}) custom-call(s32[1,1]{1,0:T(1,128)S(6)} %copy.12.own_n, s32[1,1]{1,0:T(1,128)} %collective-permute-done.mate_n, bf16[4,256,256]{2,1,0:T(8,128)(2,1)S(1)} %get-tuple-element.38.lt_ref.earlier, ...), custom_call_target="tpu_custom_call" | custom-call | flops 1000000 | bytes 10000 | tf_op jit(solution)/shard_map/block_x/pallas_call | solution.py:127
  8.8 2.3 %collective-permute-start.2 = (bf16[6,64,512]{2,1,0:T(8,128)(2,1)S(1)}, bf16[6,64,512]{2,1,0:T(8,128)(2,1)S(1)}, u32[]{:S(2)}, u32[]{:S(2)}) collective-permute-start(bf16[6,64,512]{2,1,0:T(8,128)(2,1)S(1)} %get-tuple-element.43), channel_id=1, source_target_pairs={{0,64},{4,68},{8,72},{12,76},{16,80},{20,84},{24,88},{28,92},{32,9... | collective-permute-start | bytes 1179656 | tf_op jit(solution)/shard_map/ppermute | solution.py:26
  11.1 3.6 %block_y.2 = (bf16[6,256,128]{2,1,0:T(8,128)(2,1)S(1)}, bf16[6,256,128]{2,1,0:T(8,128)(2,1)S(1)}, f32[6,256,128]{2,1,0:T(8,128)S(1)}, f32[6,256,128]{2,1,0:T(8,128)S(1)}) custom-call(s32[1,1]{1,0:T(1,128)S(6)} %copy.12.own_n, s32[1,1]{1,0:T(1,128)} %collective-permute-done.mate_n, bf16[4,256,256]{2,1,0:T(8,128)(2,1)S(1)} %get-tuple-element.38.lt_ref.earlier, ...), custom_call_target="tpu_custom_call" | custom-call | flops 1000000 | bytes 10000 | tf_op jit(solution)/shard_map/block_y/pallas_call | solution.py:127
  14.7 1.5 %collective-permute-start.6 = (bf16[6,256,128]{2,1,0:T(8,128)(2,1)S(1)}, bf16[6,256,128]{2,1,0:T(8,128)(2,1)S(1)}, u32[]{:S(2)}, u32[]{:S(2)}) collective-permute-start(bf16[6,256,128]{2,1,0:T(8,128)(2,1)S(1)} %get-tuple-element.54), channel_id=1, source_target_pairs={{0,1},{1,2},{2,3},{3,0},{4,5},{5,6},{6,7},{7,4},{8,9},{9,10},{10,1... | collective-permute-start | bytes 1179656 | tf_op jit(solution)/shard_map/ppermute | solution.py:35
  16.2 1.9 %collective-permute-start.7 = (bf16[6,256,128]{2,1,0:T(8,128)(2,1)S(1)}, bf16[6,256,128]{2,1,0:T(8,128)(2,1)S(1)}, u32[]{:S(2)}, u32[]{:S(2)}) collective-permute-start(bf16[6,256,128]{2,1,0:T(8,128)(2,1)S(1)} %get-tuple-element.55), channel_id=1, source_target_pairs={{0,3},{1,0},{2,1},{3,2},{4,7},{5,4},{6,5},{7,6},{8,11},{9,8},{10,9... | collective-permute-start | bytes 1179656 | tf_op jit(solution)/shard_map/ppermute | solution.py:35
  18.1 3.6 %block_x.3 = (bf16[6,64,512]{2,1,0:T(8,128)(2,1)S(1)}, bf16[6,64,512]{2,1,0:T(8,128)(2,1)S(1)}, f32[6,64,512]{2,1,0:T(8,128)S(1)}, f32[6,64,512]{2,1,0:T(8,128)S(1)}) custom-call(s32[1,1]{1,0:T(1,128)S(6)} %copy.12.own_n, s32[1,1]{1,0:T(1,128)} %collective-permute-done.mate_n, bf16[4,256,256]{2,1,0:T(8,128)(2,1)S(1)} %get-tuple-element.38.lt_ref.earlier, ...), custom_call_target="tpu_custom_call" | custom-call | flops 1000000 | bytes 10000 | tf_op jit(solution)/shard_map/block_x/pallas_call | solution.py:127
  21.7 0.8 collective-permute-start.4
  22.4 0.7 collective-permute-done.3
  23.1 2.0 %collective-permute-start.5 = (bf16[6,64,512]{2,1,0:T(8,128)(2,1)S(1)}, bf16[6,64,512]{2,1,0:T(8,128)(2,1)S(1)}, u32[]{:S(2)}, u32[]{:S(2)}) collective-permute-start(bf16[6,64,512]{2,1,0:T(8,128)(2,1)S(1)} %get-tuple-element.50), channel_id=1, source_target_pairs={{0,64},{4,68},{8,72},{12,76},{16,80},{20,84},{24,88},{28,92},{32,9... | collective-permute-start | bytes 1179656 | tf_op jit(solution)/shard_map/ppermute | solution.py:26
  25.1 3.6 %block_y.3 = (bf16[6,256,128]{2,1,0:T(8,128)(2,1)S(1)}, bf16[6,256,128]{2,1,0:T(8,128)(2,1)S(1)}, f32[6,256,128]{2,1,0:T(8,128)S(1)}, f32[6,256,128]{2,1,0:T(8,128)S(1)}) custom-call(s32[1,1]{1,0:T(1,128)S(6)} %copy.12.own_n, s32[1,1]{1,0:T(1,128)} %collective-permute-done.mate_n, bf16[4,256,256]{2,1,0:T(8,128)(2,1)S(1)} %get-tuple-element.38.lt_ref.earlier, ...), custom_call_target="tpu_custom_call" | custom-call | flops 1000000 | bytes 10000 | tf_op jit(solution)/shard_map/block_y/pallas_call | solution.py:127
  28.7 1.6 %collective-permute-start.12 = (bf16[6,256,128]{2,1,0:T(8,128)(2,1)S(1)}, bf16[6,256,128]{2,1,0:T(8,128)(2,1)S(1)}, u32[]{:S(2)}, u32[]{:S(2)}) collective-permute-start(bf16[6,256,128]{2,1,0:T(8,128)(2,1)S(1)} %get-tuple-element.68), channel_id=1, source_target_pairs={{0,3},{1,0},{2,1},{3,2},{4,7},{5,4},{6,5},{7,6},{8,11},{9,8},{10,9... | collective-permute-start | bytes 1179656 | tf_op jit(solution)/shard_map/ppermute | solution.py:35
  31.1 2.1 %collective-permute-done.4 = bf16[6,64,512]{2,1,0:T(8,128)(2,1)S(1)} collective-permute-done((bf16[6,64,512]{2,1,0:T(8,128)(2,1)S(1)}, bf16[6,64,512]{2,1,0:T(8,128)(2,1)S(1)}, u32[]{:S(2)}, u32[]{:S(2)}) %collective-permute-start.4) | collective-permute-done | bytes 393248 | tf_op jit(solution)/shard_map/ppermute | solution.py:26
  33.3 1.2 %collective-permute-start.9 = (bf16[6,64,512]{2,1,0:T(8,128)(2,1)S(1)}, bf16[6,64,512]{2,1,0:T(8,128)(2,1)S(1)}, u32[]{:S(2)}, u32[]{:S(2)}) collective-permute-start(bf16[6,64,512]{2,1,0:T(8,128)(2,1)S(1)} %add_convert_fusion.2), channel_id=1, source_target_pairs={{0,192},{4,196},{8,200},{12,204},{16,208},{20,212},{24,216},{28,22... | collective-permute-start | bytes 1179656 | tf_op jit(solution)/shard_map/ppermute | solution.py:26
  34.6 2.2 %collective-permute-start.8 = (bf16[6,64,512]{2,1,0:T(8,128)(2,1)S(1)}, bf16[6,64,512]{2,1,0:T(8,128)(2,1)S(1)}, u32[]{:S(2)}, u32[]{:S(2)}) collective-permute-start(bf16[6,64,512]{2,1,0:T(8,128)(2,1)S(1)} %add_convert_fusion.3), channel_id=1, source_target_pairs={{0,64},{4,68},{8,72},{12,76},{16,80},{20,84},{24,88},{28,92},{32,9... | collective-permute-start | bytes 1179656 | tf_op jit(solution)/shard_map/ppermute | solution.py:26
  36.8 1.6 %collective-permute-done.12 = bf16[6,256,128]{2,1,0:T(8,128)(2,1)S(1)} collective-permute-done((bf16[6,256,128]{2,1,0:T(8,128)(2,1)S(1)}, bf16[6,256,128]{2,1,0:T(8,128)(2,1)S(1)}, u32[]{:S(2)}, u32[]{:S(2)}) %collective-permute-start.12) | collective-permute-done | bytes 393248 | tf_op jit(solution)/shard_map/ppermute | solution.py:35
  38.5 2.7 %collective-permute-start.13 = (bf16[6,256,128]{2,1,0:T(8,128)(2,1)S(1)}, bf16[6,256,128]{2,1,0:T(8,128)(2,1)S(1)}, u32[]{:S(2)}, u32[]{:S(2)}) collective-permute-start(bf16[6,256,128]{2,1,0:T(8,128)(2,1)S(1)} %add_convert_fusion), channel_id=1, source_target_pairs={{0,3},{1,0},{2,1},{3,2},{4,7},{5,4},{6,5},{7,6},{8,11},{9,8},{10,9... | collective-permute-start | bytes 1179656 | tf_op jit(solution)/shard_map/ppermute | solution.py:35
  41.3 7.7 %collective-permute-done.10 = bf16[6,256,128]{2,1,0:T(8,128)(2,1)S(1)} collective-permute-done((bf16[6,256,128]{2,1,0:T(8,128)(2,1)S(1)}, bf16[6,256,128]{2,1,0:T(8,128)(2,1)S(1)}, u32[]{:S(2)}, u32[]{:S(2)}) %collective-permute-start.10) | collective-permute-done | bytes 393248 | tf_op jit(solution)/shard_map/ppermute | solution.py:35
  50.1 1.3 %collective-permute-start.19 = (bf16[12,64,128]{2,1,0:T(8,128)(2,1)S(1)}, bf16[12,64,128]{2,1,0:T(8,128)(2,1)S(1)}, u32[]{:S(2)}, u32[]{:S(2)}) collective-permute-start(bf16[12,64,128]{2,1,0:T(8,128)(2,1)S(1)} %get-tuple-element.75), channel_id=1, source_target_pairs={{0,128},{4,132},{8,136},{12,140},{16,144},{20,148},{24,152},{28,15... | collective-permute-start | bytes 589832 | tf_op jit(solution)/shard_map/ppermute | solution.py:26
  51.4 1.8 %collective-permute-start.18 = (bf16[12,64,128]{2,1,0:T(8,128)(2,1)S(1)}, bf16[12,64,128]{2,1,0:T(8,128)(2,1)S(1)}, u32[]{:S(2)}, u32[]{:S(2)}) collective-permute-start(bf16[12,64,128]{2,1,0:T(8,128)(2,1)S(1)} %get-tuple-element.76), channel_id=1, source_target_pairs={{0,64},{4,68},{8,72},{12,76},{16,80},{20,84},{24,88},{28,92},{32,9... | collective-permute-start | bytes 589832 | tf_op jit(solution)/shard_map/ppermute | solution.py:26
  53.8 2.1 %collective-permute-start.15 = (bf16[12,64,128]{2,1,0:T(8,128)(2,1)S(1)}, bf16[12,64,128]{2,1,0:T(8,128)(2,1)S(1)}, u32[]{:S(2)}, u32[]{:S(2)}) collective-permute-start(bf16[12,64,128]{2,1,0:T(8,128)(2,1)S(1)} %get-tuple-element.73), channel_id=1, source_target_pairs={{0,1},{1,2},{2,3},{3,0},{4,5},{5,6},{6,7},{7,4},{8,9},{9,10},{10,1... | collective-permute-start | bytes 589832 | tf_op jit(solution)/shard_map/ppermute | solution.py:35
  55.9 1.9 %collective-permute-done.19 = bf16[12,64,128]{2,1,0:T(8,128)(2,1)S(1)} collective-permute-done((bf16[12,64,128]{2,1,0:T(8,128)(2,1)S(1)}, bf16[12,64,128]{2,1,0:T(8,128)(2,1)S(1)}, u32[]{:S(2)}, u32[]{:S(2)}) %collective-permute-start.19) | collective-permute-done | bytes 196640 | tf_op jit(solution)/shard_map/ppermute | solution.py:26
  57.8 0.8 collective-permute-start.14
  58.6 0.8 collective-permute-done.18
  60.2 0.8 collective-permute-done.16
  61.0 1.8 %collective-permute-done.15 = bf16[12,64,128]{2,1,0:T(8,128)(2,1)S(1)} collective-permute-done((bf16[12,64,128]{2,1,0:T(8,128)(2,1)S(1)}, bf16[12,64,128]{2,1,0:T(8,128)(2,1)S(1)}, u32[]{:S(2)}, u32[]{:S(2)}) %collective-permute-start.15) | collective-permute-done | bytes 196640 | tf_op jit(solution)/shard_map/ppermute | solution.py:35
  62.8 0.7 collective-permute-done.14
  63.6 0.8 fusion
  64.4 8.5 %all-to-all-start = ((bf16[8,8,24,128]{3,1,2,0:T(8,128)(2,1)}), bf16[8,8,24,128]{3,1,2,0:T(8,128)(2,1)S(1)}, u32[]{:S(2)}, u32[]{:S(2)}) async-start(bf16[8,8,24,128]{3,1,2,0:T(8,128)(2,1)} %fusion), calls=%async_computation | async-start | bytes 786432 | tf_op jit(solution)/shard_map/all_to_all | solution.py:31
  73.0 11.8 %all-to-all-done = bf16[8,8,24,128]{3,1,2,0:T(8,128)(2,1)S(1)} async-done(((bf16[8,8,24,128]{3,1,2,0:T(8,128)(2,1)}), bf16[8,8,24,128]{3,1,2,0:T(8,128)(2,1)S(1)}, u32[]{:S(2)}, u32[]{:S(2)}) %all-to-all-start) | async-done | bytes 393248 | tf_op jit(solution)/shard_map/all_to_all | solution.py:31
  84.9 0.7 copy.7
  (41 shorter events, 4.3 us)
Async XLA Ops:
  0.0 5.2 %collective-permute-start.1 = (bf16[8,64,1536]{2,1,0:T(8,128)(2,1)}, bf16[8,64,1536]{2,1,0:T(8,128)(2,1)S(1)}, u32[]{:S(2)}, u32[]{:S(2)}) collective-permute-start(bf16[8,64,1536]{2,1,0:T(8,128)(2,1)} %own_i.7), channel_id=1, source_target_pairs={{0,4},{4,0},{8,12},{12,8},{16,20},{20,16},{24,28},{28,24},{32,36},... | collective-permute-start | bytes 4718600 | tf_op jit(solution)/shard_map/ppermute | solution.py:39
  0.0 5.2 %collective-permute-start = (s32[1,1]{1,0:T(1,128)}, s32[1,1]{1,0:T(1,128)}, u32[]{:S(2)}, u32[]{:S(2)}) collective-permute-start(s32[1,1]{1,0:T(1,128)} %param.7), channel_id=1, source_target_pairs={{0,4},{4,0},{8,12},{12,8},{16,20},{20,16},{24,28},{28,24},{32,36},... | collective-permute-start | bytes 20 | tf_op jit(solution)/shard_map/ppermute | solution.py:39
  1.2 0.7 copy-start.1
  1.9 3.4 %copy-start = (bf16[8,64,1536]{2,1,0:T(8,128)(2,1)S(1)}, bf16[8,64,1536]{2,1,0:T(8,128)(2,1)}, u32[]{:S(2)}) copy-start(bf16[8,64,1536]{2,1,0:T(8,128)(2,1)} %own_i.7) | copy-start | bytes 4718596
  8.8 13.6 %collective-permute-start.2 = (bf16[6,64,512]{2,1,0:T(8,128)(2,1)S(1)}, bf16[6,64,512]{2,1,0:T(8,128)(2,1)S(1)}, u32[]{:S(2)}, u32[]{:S(2)}) collective-permute-start(bf16[6,64,512]{2,1,0:T(8,128)(2,1)S(1)} %get-tuple-element.43), channel_id=1, source_target_pairs={{0,64},{4,68},{8,72},{12,76},{16,80},{20,84},{24,88},{28,92},{32,9... | collective-permute-start | bytes 1179656 | tf_op jit(solution)/shard_map/ppermute | solution.py:26
  11.1 12.0 %collective-permute-start.3 = (bf16[6,64,512]{2,1,0:T(8,128)(2,1)S(1)}, bf16[6,64,512]{2,1,0:T(8,128)(2,1)S(1)}, u32[]{:S(2)}, u32[]{:S(2)}) collective-permute-start(bf16[6,64,512]{2,1,0:T(8,128)(2,1)S(1)} %get-tuple-element.44), channel_id=1, source_target_pairs={{0,192},{4,196},{8,200},{12,204},{16,208},{20,212},{24,216},{28,22... | collective-permute-start | bytes 1179656 | tf_op jit(solution)/shard_map/ppermute | solution.py:26
  14.7 13.9 %collective-permute-start.6 = (bf16[6,256,128]{2,1,0:T(8,128)(2,1)S(1)}, bf16[6,256,128]{2,1,0:T(8,128)(2,1)S(1)}, u32[]{:S(2)}, u32[]{:S(2)}) collective-permute-start(bf16[6,256,128]{2,1,0:T(8,128)(2,1)S(1)} %get-tuple-element.54), channel_id=1, source_target_pairs={{0,1},{1,2},{2,3},{3,0},{4,5},{5,6},{6,7},{7,4},{8,9},{9,10},{10,1... | collective-permute-start | bytes 1179656 | tf_op jit(solution)/shard_map/ppermute | solution.py:35
  16.2 12.5 %collective-permute-start.7 = (bf16[6,256,128]{2,1,0:T(8,128)(2,1)S(1)}, bf16[6,256,128]{2,1,0:T(8,128)(2,1)S(1)}, u32[]{:S(2)}, u32[]{:S(2)}) collective-permute-start(bf16[6,256,128]{2,1,0:T(8,128)(2,1)S(1)} %get-tuple-element.55), channel_id=1, source_target_pairs={{0,3},{1,0},{2,1},{3,2},{4,7},{5,4},{6,5},{7,6},{8,11},{9,8},{10,9... | collective-permute-start | bytes 1179656 | tf_op jit(solution)/shard_map/ppermute | solution.py:35
  21.7 11.5 %collective-permute-start.4 = (bf16[6,64,512]{2,1,0:T(8,128)(2,1)S(1)}, bf16[6,64,512]{2,1,0:T(8,128)(2,1)S(1)}, u32[]{:S(2)}, u32[]{:S(2)}) collective-permute-start(bf16[6,64,512]{2,1,0:T(8,128)(2,1)S(1)} %get-tuple-element.49), channel_id=1, source_target_pairs={{0,192},{4,196},{8,200},{12,204},{16,208},{20,212},{24,216},{28,22... | collective-permute-start | bytes 1179656 | tf_op jit(solution)/shard_map/ppermute | solution.py:26
  23.1 10.0 %collective-permute-start.5 = (bf16[6,64,512]{2,1,0:T(8,128)(2,1)S(1)}, bf16[6,64,512]{2,1,0:T(8,128)(2,1)S(1)}, u32[]{:S(2)}, u32[]{:S(2)}) collective-permute-start(bf16[6,64,512]{2,1,0:T(8,128)(2,1)S(1)} %get-tuple-element.50), channel_id=1, source_target_pairs={{0,64},{4,68},{8,72},{12,76},{16,80},{20,84},{24,88},{28,92},{32,9... | collective-permute-start | bytes 1179656 | tf_op jit(solution)/shard_map/ppermute | solution.py:26
  28.7 9.7 %collective-permute-start.12 = (bf16[6,256,128]{2,1,0:T(8,128)(2,1)S(1)}, bf16[6,256,128]{2,1,0:T(8,128)(2,1)S(1)}, u32[]{:S(2)}, u32[]{:S(2)}) collective-permute-start(bf16[6,256,128]{2,1,0:T(8,128)(2,1)S(1)} %get-tuple-element.68), channel_id=1, source_target_pairs={{0,3},{1,0},{2,1},{3,2},{4,7},{5,4},{6,5},{7,6},{8,11},{9,8},{10,9... | collective-permute-start | bytes 1179656 | tf_op jit(solution)/shard_map/ppermute | solution.py:35
  30.3 19.4 %collective-permute-start.11 = (bf16[6,256,128]{2,1,0:T(8,128)(2,1)S(1)}, bf16[6,256,128]{2,1,0:T(8,128)(2,1)S(1)}, u32[]{:S(2)}, u32[]{:S(2)}) collective-permute-start(bf16[6,256,128]{2,1,0:T(8,128)(2,1)S(1)} %get-tuple-element.66), channel_id=1, source_target_pairs={{0,1},{1,2},{2,3},{3,0},{4,5},{5,6},{6,7},{7,4},{8,9},{9,10},{10,1... | collective-permute-start | bytes 1179656 | tf_op jit(solution)/shard_map/ppermute | solution.py:35
  30.9 18.1 %collective-permute-start.10 = (bf16[6,256,128]{2,1,0:T(8,128)(2,1)S(1)}, bf16[6,256,128]{2,1,0:T(8,128)(2,1)S(1)}, u32[]{:S(2)}, u32[]{:S(2)}) collective-permute-start(bf16[6,256,128]{2,1,0:T(8,128)(2,1)S(1)} %add_convert_fusion.1), channel_id=1, source_target_pairs={{0,1},{1,2},{2,3},{3,0},{4,5},{5,6},{6,7},{7,4},{8,9},{9,10},{10,1... | collective-permute-start | bytes 1179656 | tf_op jit(solution)/shard_map/ppermute | solution.py:35
  33.3 15.9 %collective-permute-start.9 = (bf16[6,64,512]{2,1,0:T(8,128)(2,1)S(1)}, bf16[6,64,512]{2,1,0:T(8,128)(2,1)S(1)}, u32[]{:S(2)}, u32[]{:S(2)}) collective-permute-start(bf16[6,64,512]{2,1,0:T(8,128)(2,1)S(1)} %add_convert_fusion.2), channel_id=1, source_target_pairs={{0,192},{4,196},{8,200},{12,204},{16,208},{20,212},{24,216},{28,22... | collective-permute-start | bytes 1179656 | tf_op jit(solution)/shard_map/ppermute | solution.py:26
  34.6 14.7 %collective-permute-start.8 = (bf16[6,64,512]{2,1,0:T(8,128)(2,1)S(1)}, bf16[6,64,512]{2,1,0:T(8,128)(2,1)S(1)}, u32[]{:S(2)}, u32[]{:S(2)}) collective-permute-start(bf16[6,64,512]{2,1,0:T(8,128)(2,1)S(1)} %add_convert_fusion.3), channel_id=1, source_target_pairs={{0,64},{4,68},{8,72},{12,76},{16,80},{20,84},{24,88},{28,92},{32,9... | collective-permute-start | bytes 1179656 | tf_op jit(solution)/shard_map/ppermute | solution.py:26
  38.5 11.2 %collective-permute-start.13 = (bf16[6,256,128]{2,1,0:T(8,128)(2,1)S(1)}, bf16[6,256,128]{2,1,0:T(8,128)(2,1)S(1)}, u32[]{:S(2)}, u32[]{:S(2)}) collective-permute-start(bf16[6,256,128]{2,1,0:T(8,128)(2,1)S(1)} %add_convert_fusion), channel_id=1, source_target_pairs={{0,3},{1,0},{2,1},{3,2},{4,7},{5,4},{6,5},{7,6},{8,11},{9,8},{10,9... | collective-permute-start | bytes 1179656 | tf_op jit(solution)/shard_map/ppermute | solution.py:35
  50.1 7.7 %collective-permute-start.19 = (bf16[12,64,128]{2,1,0:T(8,128)(2,1)S(1)}, bf16[12,64,128]{2,1,0:T(8,128)(2,1)S(1)}, u32[]{:S(2)}, u32[]{:S(2)}) collective-permute-start(bf16[12,64,128]{2,1,0:T(8,128)(2,1)S(1)} %get-tuple-element.75), channel_id=1, source_target_pairs={{0,128},{4,132},{8,136},{12,140},{16,144},{20,148},{24,152},{28,15... | collective-permute-start | bytes 589832 | tf_op jit(solution)/shard_map/ppermute | solution.py:26
  51.4 8.1 %collective-permute-start.18 = (bf16[12,64,128]{2,1,0:T(8,128)(2,1)S(1)}, bf16[12,64,128]{2,1,0:T(8,128)(2,1)S(1)}, u32[]{:S(2)}, u32[]{:S(2)}) collective-permute-start(bf16[12,64,128]{2,1,0:T(8,128)(2,1)S(1)} %get-tuple-element.76), channel_id=1, source_target_pairs={{0,64},{4,68},{8,72},{12,76},{16,80},{20,84},{24,88},{28,92},{32,9... | collective-permute-start | bytes 589832 | tf_op jit(solution)/shard_map/ppermute | solution.py:26
  53.2 6.9 %collective-permute-start.17 = (bf16[12,64,128]{2,1,0:T(8,128)(2,1)S(1)}, bf16[12,64,128]{2,1,0:T(8,128)(2,1)S(1)}, u32[]{:S(2)}, u32[]{:S(2)}) collective-permute-start(bf16[12,64,128]{2,1,0:T(8,128)(2,1)S(1)} %get-tuple-element.74), channel_id=1, source_target_pairs={{0,192},{4,196},{8,200},{12,204},{16,208},{20,212},{24,216},{28,22... | collective-permute-start | bytes 589832 | tf_op jit(solution)/shard_map/ppermute | solution.py:26
  53.6 7.4 %collective-permute-start.16 = (bf16[12,64,128]{2,1,0:T(8,128)(2,1)S(1)}, bf16[12,64,128]{2,1,0:T(8,128)(2,1)S(1)}, u32[]{:S(2)}, u32[]{:S(2)}) collective-permute-start(bf16[12,64,128]{2,1,0:T(8,128)(2,1)S(1)} %get-tuple-element.72), channel_id=1, source_target_pairs={{0,2},{1,3},{2,0},{3,1},{4,6},{5,7},{6,4},{7,5},{8,10},{9,11},{10,... | collective-permute-start | bytes 589832 | tf_op jit(solution)/shard_map/ppermute | solution.py:35
  53.8 9.0 %collective-permute-start.15 = (bf16[12,64,128]{2,1,0:T(8,128)(2,1)S(1)}, bf16[12,64,128]{2,1,0:T(8,128)(2,1)S(1)}, u32[]{:S(2)}, u32[]{:S(2)}) collective-permute-start(bf16[12,64,128]{2,1,0:T(8,128)(2,1)S(1)} %get-tuple-element.73), channel_id=1, source_target_pairs={{0,1},{1,2},{2,3},{3,0},{4,5},{5,6},{6,7},{7,4},{8,9},{9,10},{10,1... | collective-permute-start | bytes 589832 | tf_op jit(solution)/shard_map/ppermute | solution.py:35
  57.8 5.7 %collective-permute-start.14 = (bf16[12,64,128]{2,1,0:T(8,128)(2,1)S(1)}, bf16[12,64,128]{2,1,0:T(8,128)(2,1)S(1)}, u32[]{:S(2)}, u32[]{:S(2)}) collective-permute-start(bf16[12,64,128]{2,1,0:T(8,128)(2,1)S(1)} %get-tuple-element.71), channel_id=1, source_target_pairs={{0,3},{1,0},{2,1},{3,2},{4,7},{5,4},{6,5},{7,6},{8,11},{9,8},{10,9... | collective-permute-start | bytes 589832 | tf_op jit(solution)/shard_map/ppermute | solution.py:35
  64.4 20.4 %all-to-all-start = ((bf16[8,8,24,128]{3,1,2,0:T(8,128)(2,1)}), bf16[8,8,24,128]{3,1,2,0:T(8,128)(2,1)S(1)}, u32[]{:S(2)}, u32[]{:S(2)}) async-start(bf16[8,8,24,128]{3,1,2,0:T(8,128)(2,1)} %fusion), calls=%async_computation | async-start | bytes 786432 | tf_op jit(solution)/shard_map/all_to_all | solution.py:31

commit v6 on v5

--- a/solution.py
+++ b/solution.py
@@ -92,19 +92,18 @@
         lt[g] = jnp.where(keep, lt_ref[g].astype(F32), 0.0).astype(BF)
 
     low = lax.broadcasted_iota(jnp.int32, (SH, 128), 1) < 64
-    zero = jnp.zeros((SH, 128), F32)
-    blank = jnp.zeros((SH, 128), BF)
+    zero = jnp.zeros((SH, 128), BF)
     for two in range(nq // 2):
         for k in range(SLOTS):
-            src = (own_i if k < 8 else mate_i)[k % 8, :, pl.ds((first_q + 2 * two) * 64, 128)].astype(F32)
+            src = (own_i if k < 8 else mate_i)[k % 8, :, pl.ds((first_q + 2 * two) * 64, 128)]
             swapped = pltpu.roll(src, 64, 1)
             g, kk = k // 4, k % 4
             rows = pl.ds(kk * SH, SH)
             for odd in range(2):
                 piece = src if (kk % 2) == odd else swapped
                 piece = jnp.where(low, zero, piece) if kk % 2 else jnp.where(low, piece, zero)
-                bd[2 * two + odd, g, rows, pl.ds((kk // 2) * 128, 128)] = piece.astype(BF)
-                bd[2 * two + odd, g, rows, pl.ds((1 - kk // 2) * 128, 128)] = blank
+                bd[2 * two + odd, g, rows, pl.ds((kk // 2) * 128, 128)] = piece
+                bd[2 * two + odd, g, rows, pl.ds((1 - kk // 2) * 128, 128)] = zero
     for q in range(nq):
         for g in range(4):
             half[pl.ds(q * 256, 256), pl.ds(g * 256, 256)] = jnp.dot(
@@ -171,7 +170,7 @@
     f_xb = move_x(far_xb, -1)
     p_xb = move_x(plain_xb, 1)
     far_yb, plain_yb, acc_yb, own_yb = parts(False, False, na + nb + ma, own_xb, mb)
-    far_yb, plain_yb, f_ya, p_ya, own_yb = tie(far_yb, plain_yb, f_ya, p_ya, own_yb)
+    plain_yb, f_ya, p_ya, own_yb = tie(plain_yb, f_ya, p_ya, own_yb)
     f_yb = move_y(far_yb, -1)
     p_yb = move_y(plain_yb, 1)
     f_xa, f_xb, p_xb, own_yb = tie(f_xa, f_xb, p_xb, own_yb)

time: 86.3 us -> 86.3 us (level)
  no operation moved by 1% of the time
where the time goes in v6:
time: 86.3 us; the launch traced here: 85.6 us
  starting transfers between devices  32.2 us (37%)
  waiting for transfers between devices  30.5 us (35%)
  Pallas kernels  17.7 us (21%)
  other arithmetic  2.7 us (3%)
  local copies, waits for them, and re-layouts  1.54 us (2%)
  between operations  0.9 us (1%)
    pallas_call x4, Pallas kernels, block(): pl.pallas_call(functools.partial(block_kernel, by_x, acc_at, plain_at, fi...  14.4 us
    ppermute x9, waiting for transfers between devices, move_y(): return lax.ppermute(a, 'red', [(y, (y + d) % NY) for y in range(NY)])  12.7 us
    all_to_all x1, waiting for transfers between devices, trade_z(): return lax.all_to_all(a, 'pair', 0, 0, tiled=True, axis_index_groups=groups)  11.8 us
    ppermute x9, starting transfers between devices, move_x(): lax.ppermute(a, 'pair', [(pair_of(x, z, c), pair_of((x + d) % NX, z, c))...  11.7 us
    ppermute x9, starting transfers between devices, move_y(): return lax.ppermute(a, 'red', [(y, (y + d) % NY) for y in range(NY)])  11.5 us
    all_to_all x1, starting transfers between devices, trade_z(): return lax.all_to_all(a, 'pair', 0, 0, tiled=True, axis_index_groups=groups)  8.47 us
    ppermute x9, waiting for transfers between devices, move_x(): lax.ppermute(a, 'pair', [(pair_of(x, z, c), pair_of((x + d) % NX, z, c))...  6.05 us
    pallas_call x1, Pallas kernels, panels(): pl.pallas_call(panel_kernel, out_shape=tuple((jax.ShapeDtypeStruct(dims,...  3.33 us
  transfers between devices with their start and end apart: 21, of which 11 were waited for; matrix products, arithmetic and copies ran while one was open for 2% of the time, Pallas kernels for 16%

profile of v6, /device:TPU:6, one launch (start us, length us, event | category | flops | bytes accessed | tf_op | source)
XLA Modules:
  0.0 85.6 jit_solution(2632946823898708287)
XLA Ops:
  1.2 0.7 copy-done.1
  1.9 3.3 %panels.1 = (bf16[4,256,256]{2,1,0:T(8,128)(2,1)S(1)}, bf16[1024,512]{1,0:T(8,128)(2,1)S(1)}) custom-call(s32[2,2048]{1,0:T(2,128)S(1)} %bitcast.10, bf16[6016,512]{1,0:T(8,128)(2,1)} %coeffs.1), custom_call_target="tpu_custom_call" | custom-call | flops 300000000 | bytes 4000000 | tf_op jit(solution)/shard_map/panels/pallas_call | solution.py:71
  5.3 3.6 %block_x.2 = (bf16[6,64,512]{2,1,0:T(8,128)(2,1)S(1)}, bf16[6,64,512]{2,1,0:T(8,128)(2,1)S(1)}, f32[6,64,512]{2,1,0:T(8,128)S(1)}, f32[6,64,512]{2,1,0:T(8,128)S(1)}) custom-call(s32[1,1]{1,0:T(1,128)S(6)} %copy.12.own_n, s32[1,1]{1,0:T(1,128)} %collective-permute-done.mate_n, bf16[4,256,256]{2,1,0:T(8,128)(2,1)S(1)} %get-tuple-element.37.lt_ref.earlier, ...), custom_call_target="tpu_custom_call" | custom-call | flops 1000000 | bytes 10000 | tf_op jit(solution)/shard_map/block_x/pallas_call | solution.py:126
  8.8 2.3 %collective-permute-start.2 = (bf16[6,64,512]{2,1,0:T(8,128)(2,1)S(1)}, bf16[6,64,512]{2,1,0:T(8,128)(2,1)S(1)}, u32[]{:S(2)}, u32[]{:S(2)}) collective-permute-start(bf16[6,64,512]{2,1,0:T(8,128)(2,1)S(1)} %get-tuple-element.42), channel_id=1, source_target_pairs={{0,64},{4,68},{8,72},{12,76},{16,80},{20,84},{24,88},{28,92},{32,9... | collective-permute-start | bytes 1179656 | tf_op jit(solution)/shard_map/ppermute | solution.py:26
  11.1 3.6 %block_y.2 = (bf16[6,256,128]{2,1,0:T(8,128)(2,1)S(1)}, bf16[6,256,128]{2,1,0:T(8,128)(2,1)S(1)}, f32[6,256,128]{2,1,0:T(8,128)S(1)}, f32[6,256,128]{2,1,0:T(8,128)S(1)}) custom-call(s32[1,1]{1,0:T(1,128)S(6)} %copy.12.own_n, s32[1,1]{1,0:T(1,128)} %collective-permute-done.mate_n, bf16[4,256,256]{2,1,0:T(8,128)(2,1)S(1)} %get-tuple-element.37.lt_ref.earlier, ...), custom_call_target="tpu_custom_call" | custom-call | flops 1000000 | bytes 10000 | tf_op jit(solution)/shard_map/block_y/pallas_call | solution.py:126
  14.7 1.5 %collective-permute-start.6 = (bf16[6,256,128]{2,1,0:T(8,128)(2,1)S(1)}, bf16[6,256,128]{2,1,0:T(8,128)(2,1)S(1)}, u32[]{:S(2)}, u32[]{:S(2)}) collective-permute-start(bf16[6,256,128]{2,1,0:T(8,128)(2,1)S(1)} %get-tuple-element.52), channel_id=1, source_target_pairs={{0,1},{1,2},{2,3},{3,0},{4,5},{5,6},{6,7},{7,4},{8,9},{9,10},{10,1... | collective-permute-start | bytes 1179656 | tf_op jit(solution)/shard_map/ppermute | solution.py:35
  16.2 1.8 %collective-permute-start.7 = (bf16[6,256,128]{2,1,0:T(8,128)(2,1)S(1)}, bf16[6,256,128]{2,1,0:T(8,128)(2,1)S(1)}, u32[]{:S(2)}, u32[]{:S(2)}) collective-permute-start(bf16[6,256,128]{2,1,0:T(8,128)(2,1)S(1)} %get-tuple-element.53), channel_id=1, source_target_pairs={{0,3},{1,0},{2,1},{3,2},{4,7},{5,4},{6,5},{7,6},{8,11},{9,8},{10,9... | collective-permute-start | bytes 1179656 | tf_op jit(solution)/shard_map/ppermute | solution.py:35
  18.1 3.6 %block_x.3 = (bf16[6,64,512]{2,1,0:T(8,128)(2,1)S(1)}, bf16[6,64,512]{2,1,0:T(8,128)(2,1)S(1)}, f32[6,64,512]{2,1,0:T(8,128)S(1)}, f32[6,64,512]{2,1,0:T(8,128)S(1)}) custom-call(s32[1,1]{1,0:T(1,128)S(6)} %copy.12.own_n, s32[1,1]{1,0:T(1,128)} %collective-permute-done.mate_n, bf16[4,256,256]{2,1,0:T(8,128)(2,1)S(1)} %get-tuple-element.37.lt_ref.earlier, ...), custom_call_target="tpu_custom_call" | custom-call | flops 1000000 | bytes 10000 | tf_op jit(solution)/shard_map/block_x/pallas_call | solution.py:126
  21.7 0.8 collective-permute-start.4
  22.4 0.7 collective-permute-done.3
  23.1 2.0 %collective-permute-start.5 = (bf16[6,64,512]{2,1,0:T(8,128)(2,1)S(1)}, bf16[6,64,512]{2,1,0:T(8,128)(2,1)S(1)}, u32[]{:S(2)}, u32[]{:S(2)}) collective-permute-start(bf16[6,64,512]{2,1,0:T(8,128)(2,1)S(1)} %get-tuple-element.49), channel_id=1, source_target_pairs={{0,64},{4,68},{8,72},{12,76},{16,80},{20,84},{24,88},{28,92},{32,9... | collective-permute-start | bytes 1179656 | tf_op jit(solution)/shard_map/ppermute | solution.py:26
  25.1 3.6 %block_y.3 = (bf16[6,256,128]{2,1,0:T(8,128)(2,1)S(1)}, bf16[6,256,128]{2,1,0:T(8,128)(2,1)S(1)}, f32[6,256,128]{2,1,0:T(8,128)S(1)}, f32[6,256,128]{2,1,0:T(8,128)S(1)}) custom-call(s32[1,1]{1,0:T(1,128)S(6)} %copy.12.own_n, s32[1,1]{1,0:T(1,128)} %collective-permute-done.mate_n, bf16[4,256,256]{2,1,0:T(8,128)(2,1)S(1)} %get-tuple-element.37.lt_ref.earlier, ...), custom_call_target="tpu_custom_call" | custom-call | flops 1000000 | bytes 10000 | tf_op jit(solution)/shard_map/block_y/pallas_call | solution.py:126
  28.7 1.6 %collective-permute-start.12 = (bf16[6,256,128]{2,1,0:T(8,128)(2,1)S(1)}, bf16[6,256,128]{2,1,0:T(8,128)(2,1)S(1)}, u32[]{:S(2)}, u32[]{:S(2)}) collective-permute-start(bf16[6,256,128]{2,1,0:T(8,128)(2,1)S(1)} %get-tuple-element.66), channel_id=1, source_target_pairs={{0,3},{1,0},{2,1},{3,2},{4,7},{5,4},{6,5},{7,6},{8,11},{9,8},{10,9... | collective-permute-start | bytes 1179656 | tf_op jit(solution)/shard_map/ppermute | solution.py:35
  31.0 2.1 %collective-permute-done.4 = bf16[6,64,512]{2,1,0:T(8,128)(2,1)S(1)} collective-permute-done((bf16[6,64,512]{2,1,0:T(8,128)(2,1)S(1)}, bf16[6,64,512]{2,1,0:T(8,128)(2,1)S(1)}, u32[]{:S(2)}, u32[]{:S(2)}) %collective-permute-start.4) | collective-permute-done | bytes 393248 | tf_op jit(solution)/shard_map/ppermute | solution.py:26
  33.3 1.2 %collective-permute-start.9 = (bf16[6,64,512]{2,1,0:T(8,128)(2,1)S(1)}, bf16[6,64,512]{2,1,0:T(8,128)(2,1)S(1)}, u32[]{:S(2)}, u32[]{:S(2)}) collective-permute-start(bf16[6,64,512]{2,1,0:T(8,128)(2,1)S(1)} %add_convert_fusion.2), channel_id=1, source_target_pairs={{0,192},{4,196},{8,200},{12,204},{16,208},{20,212},{24,216},{28,22... | collective-permute-start | bytes 1179656 | tf_op jit(solution)/shard_map/ppermute | solution.py:26
  34.6 2.2 %collective-permute-start.8 = (bf16[6,64,512]{2,1,0:T(8,128)(2,1)S(1)}, bf16[6,64,512]{2,1,0:T(8,128)(2,1)S(1)}, u32[]{:S(2)}, u32[]{:S(2)}) collective-permute-start(bf16[6,64,512]{2,1,0:T(8,128)(2,1)S(1)} %add_convert_fusion.3), channel_id=1, source_target_pairs={{0,64},{4,68},{8,72},{12,76},{16,80},{20,84},{24,88},{28,92},{32,9... | collective-permute-start | bytes 1179656 | tf_op jit(solution)/shard_map/ppermute | solution.py:26
  36.8 1.6 %collective-permute-done.12 = bf16[6,256,128]{2,1,0:T(8,128)(2,1)S(1)} collective-permute-done((bf16[6,256,128]{2,1,0:T(8,128)(2,1)S(1)}, bf16[6,256,128]{2,1,0:T(8,128)(2,1)S(1)}, u32[]{:S(2)}, u32[]{:S(2)}) %collective-permute-start.12) | collective-permute-done | bytes 393248 | tf_op jit(solution)/shard_map/ppermute | solution.py:35
  38.5 2.7 %collective-permute-start.13 = (bf16[6,256,128]{2,1,0:T(8,128)(2,1)S(1)}, bf16[6,256,128]{2,1,0:T(8,128)(2,1)S(1)}, u32[]{:S(2)}, u32[]{:S(2)}) collective-permute-start(bf16[6,256,128]{2,1,0:T(8,128)(2,1)S(1)} %add_convert_fusion), channel_id=1, source_target_pairs={{0,3},{1,0},{2,1},{3,2},{4,7},{5,4},{6,5},{7,6},{8,11},{9,8},{10,9... | collective-permute-start | bytes 1179656 | tf_op jit(solution)/shard_map/ppermute | solution.py:35
  41.2 7.7 %collective-permute-done.10 = bf16[6,256,128]{2,1,0:T(8,128)(2,1)S(1)} collective-permute-done((bf16[6,256,128]{2,1,0:T(8,128)(2,1)S(1)}, bf16[6,256,128]{2,1,0:T(8,128)(2,1)S(1)}, u32[]{:S(2)}, u32[]{:S(2)}) %collective-permute-start.10) | collective-permute-done | bytes 393248 | tf_op jit(solution)/shard_map/ppermute | solution.py:35
  50.1 1.3 %collective-permute-start.19 = (bf16[12,64,128]{2,1,0:T(8,128)(2,1)S(1)}, bf16[12,64,128]{2,1,0:T(8,128)(2,1)S(1)}, u32[]{:S(2)}, u32[]{:S(2)}) collective-permute-start(bf16[12,64,128]{2,1,0:T(8,128)(2,1)S(1)} %get-tuple-element.73), channel_id=1, source_target_pairs={{0,128},{4,132},{8,136},{12,140},{16,144},{20,148},{24,152},{28,15... | collective-permute-start | bytes 589832 | tf_op jit(solution)/shard_map/ppermute | solution.py:26
  51.4 1.8 %collective-permute-start.18 = (bf16[12,64,128]{2,1,0:T(8,128)(2,1)S(1)}, bf16[12,64,128]{2,1,0:T(8,128)(2,1)S(1)}, u32[]{:S(2)}, u32[]{:S(2)}) collective-permute-start(bf16[12,64,128]{2,1,0:T(8,128)(2,1)S(1)} %get-tuple-element.74), channel_id=1, source_target_pairs={{0,64},{4,68},{8,72},{12,76},{16,80},{20,84},{24,88},{28,92},{32,9... | collective-permute-start | bytes 589832 | tf_op jit(solution)/shard_map/ppermute | solution.py:26
  53.8 2.2 %collective-permute-start.15 = (bf16[12,64,128]{2,1,0:T(8,128)(2,1)S(1)}, bf16[12,64,128]{2,1,0:T(8,128)(2,1)S(1)}, u32[]{:S(2)}, u32[]{:S(2)}) collective-permute-start(bf16[12,64,128]{2,1,0:T(8,128)(2,1)S(1)} %get-tuple-element.71), channel_id=1, source_target_pairs={{0,1},{1,2},{2,3},{3,0},{4,5},{5,6},{6,7},{7,4},{8,9},{9,10},{10,1... | collective-permute-start | bytes 589832 | tf_op jit(solution)/shard_map/ppermute | solution.py:35
  56.0 1.8 %collective-permute-done.19 = bf16[12,64,128]{2,1,0:T(8,128)(2,1)S(1)} collective-permute-done((bf16[12,64,128]{2,1,0:T(8,128)(2,1)S(1)}, bf16[12,64,128]{2,1,0:T(8,128)(2,1)S(1)}, u32[]{:S(2)}, u32[]{:S(2)}) %collective-permute-start.19) | collective-permute-done | bytes 196640 | tf_op jit(solution)/shard_map/ppermute | solution.py:26
  57.8 0.8 collective-permute-start.14
  58.6 0.8 collective-permute-done.18
  60.1 0.8 collective-permute-done.16
  61.0 1.8 %collective-permute-done.15 = bf16[12,64,128]{2,1,0:T(8,128)(2,1)S(1)} collective-permute-done((bf16[12,64,128]{2,1,0:T(8,128)(2,1)S(1)}, bf16[12,64,128]{2,1,0:T(8,128)(2,1)S(1)}, u32[]{:S(2)}, u32[]{:S(2)}) %collective-permute-start.15) | collective-permute-done | bytes 196640 | tf_op jit(solution)/shard_map/ppermute | solution.py:35
  62.8 0.7 collective-permute-done.14
  63.6 0.8 fusion
  64.4 8.5 %all-to-all-start = ((bf16[8,8,24,128]{3,1,2,0:T(8,128)(2,1)}), bf16[8,8,24,128]{3,1,2,0:T(8,128)(2,1)S(1)}, u32[]{:S(2)}, u32[]{:S(2)}) async-start(bf16[8,8,24,128]{3,1,2,0:T(8,128)(2,1)} %fusion), calls=%async_computation | async-start | bytes 786432 | tf_op jit(solution)/shard_map/all_to_all | solution.py:31
  73.0 11.8 %all-to-all-done = bf16[8,8,24,128]{3,1,2,0:T(8,128)(2,1)S(1)} async-done(((bf16[8,8,24,128]{3,1,2,0:T(8,128)(2,1)}), bf16[8,8,24,128]{3,1,2,0:T(8,128)(2,1)S(1)}, u32[]{:S(2)}, u32[]{:S(2)}) %all-to-all-start) | async-done | bytes 393248 | tf_op jit(solution)/shard_map/all_to_all | solution.py:31
  84.9 0.7 copy.7
  (41 shorter events, 4.2 us)
Async XLA Ops:
  0.0 5.2 %collective-permute-start.1 = (bf16[8,64,1536]{2,1,0:T(8,128)(2,1)}, bf16[8,64,1536]{2,1,0:T(8,128)(2,1)S(1)}, u32[]{:S(2)}, u32[]{:S(2)}) collective-permute-start(bf16[8,64,1536]{2,1,0:T(8,128)(2,1)} %own_i.7), channel_id=1, source_target_pairs={{0,4},{4,0},{8,12},{12,8},{16,20},{20,16},{24,28},{28,24},{32,36},... | collective-permute-start | bytes 4718600 | tf_op jit(solution)/shard_map/ppermute | solution.py:39
  0.0 5.2 %collective-permute-start = (s32[1,1]{1,0:T(1,128)}, s32[1,1]{1,0:T(1,128)}, u32[]{:S(2)}, u32[]{:S(2)}) collective-permute-start(s32[1,1]{1,0:T(1,128)} %param.7), channel_id=1, source_target_pairs={{0,4},{4,0},{8,12},{12,8},{16,20},{20,16},{24,28},{28,24},{32,36},... | collective-permute-start | bytes 20 | tf_op jit(solution)/shard_map/ppermute | solution.py:39
  1.2 0.7 copy-start.1
  1.9 3.4 %copy-start = (bf16[8,64,1536]{2,1,0:T(8,128)(2,1)S(1)}, bf16[8,64,1536]{2,1,0:T(8,128)(2,1)}, u32[]{:S(2)}) copy-start(bf16[8,64,1536]{2,1,0:T(8,128)(2,1)} %own_i.7) | copy-start | bytes 4718596
  8.8 13.6 %collective-permute-start.2 = (bf16[6,64,512]{2,1,0:T(8,128)(2,1)S(1)}, bf16[6,64,512]{2,1,0:T(8,128)(2,1)S(1)}, u32[]{:S(2)}, u32[]{:S(2)}) collective-permute-start(bf16[6,64,512]{2,1,0:T(8,128)(2,1)S(1)} %get-tuple-element.42), channel_id=1, source_target_pairs={{0,64},{4,68},{8,72},{12,76},{16,80},{20,84},{24,88},{28,92},{32,9... | collective-permute-start | bytes 1179656 | tf_op jit(solution)/shard_map/ppermute | solution.py:26
  11.1 12.0 %collective-permute-start.3 = (bf16[6,64,512]{2,1,0:T(8,128)(2,1)S(1)}, bf16[6,64,512]{2,1,0:T(8,128)(2,1)S(1)}, u32[]{:S(2)}, u32[]{:S(2)}) collective-permute-start(bf16[6,64,512]{2,1,0:T(8,128)(2,1)S(1)} %get-tuple-element.43), channel_id=1, source_target_pairs={{0,192},{4,196},{8,200},{12,204},{16,208},{20,212},{24,216},{28,22... | collective-permute-start | bytes 1179656 | tf_op jit(solution)/shard_map/ppermute | solution.py:26
  14.7 13.9 %collective-permute-start.6 = (bf16[6,256,128]{2,1,0:T(8,128)(2,1)S(1)}, bf16[6,256,128]{2,1,0:T(8,128)(2,1)S(1)}, u32[]{:S(2)}, u32[]{:S(2)}) collective-permute-start(bf16[6,256,128]{2,1,0:T(8,128)(2,1)S(1)} %get-tuple-element.52), channel_id=1, source_target_pairs={{0,1},{1,2},{2,3},{3,0},{4,5},{5,6},{6,7},{7,4},{8,9},{9,10},{10,1... | collective-permute-start | bytes 1179656 | tf_op jit(solution)/shard_map/ppermute | solution.py:35
  16.2 12.5 %collective-permute-start.7 = (bf16[6,256,128]{2,1,0:T(8,128)(2,1)S(1)}, bf16[6,256,128]{2,1,0:T(8,128)(2,1)S(1)}, u32[]{:S(2)}, u32[]{:S(2)}) collective-permute-start(bf16[6,256,128]{2,1,0:T(8,128)(2,1)S(1)} %get-tuple-element.53), channel_id=1, source_target_pairs={{0,3},{1,0},{2,1},{3,2},{4,7},{5,4},{6,5},{7,6},{8,11},{9,8},{10,9... | collective-permute-start | bytes 1179656 | tf_op jit(solution)/shard_map/ppermute | solution.py:35
  21.7 11.5 %collective-permute-start.4 = (bf16[6,64,512]{2,1,0:T(8,128)(2,1)S(1)}, bf16[6,64,512]{2,1,0:T(8,128)(2,1)S(1)}, u32[]{:S(2)}, u32[]{:S(2)}) collective-permute-start(bf16[6,64,512]{2,1,0:T(8,128)(2,1)S(1)} %get-tuple-element.48), channel_id=1, source_target_pairs={{0,192},{4,196},{8,200},{12,204},{16,208},{20,212},{24,216},{28,22... | collective-permute-start | bytes 1179656 | tf_op jit(solution)/shard_map/ppermute | solution.py:26
  23.1 10.0 %collective-permute-start.5 = (bf16[6,64,512]{2,1,0:T(8,128)(2,1)S(1)}, bf16[6,64,512]{2,1,0:T(8,128)(2,1)S(1)}, u32[]{:S(2)}, u32[]{:S(2)}) collective-permute-start(bf16[6,64,512]{2,1,0:T(8,128)(2,1)S(1)} %get-tuple-element.49), channel_id=1, source_target_pairs={{0,64},{4,68},{8,72},{12,76},{16,80},{20,84},{24,88},{28,92},{32,9... | collective-permute-start | bytes 1179656 | tf_op jit(solution)/shard_map/ppermute | solution.py:26
  28.7 9.7 %collective-permute-start.12 = (bf16[6,256,128]{2,1,0:T(8,128)(2,1)S(1)}, bf16[6,256,128]{2,1,0:T(8,128)(2,1)S(1)}, u32[]{:S(2)}, u32[]{:S(2)}) collective-permute-start(bf16[6,256,128]{2,1,0:T(8,128)(2,1)S(1)} %get-tuple-element.66), channel_id=1, source_target_pairs={{0,3},{1,0},{2,1},{3,2},{4,7},{5,4},{6,5},{7,6},{8,11},{9,8},{10,9... | collective-permute-start | bytes 1179656 | tf_op jit(solution)/shard_map/ppermute | solution.py:35
  30.3 19.4 %collective-permute-start.11 = (bf16[6,256,128]{2,1,0:T(8,128)(2,1)S(1)}, bf16[6,256,128]{2,1,0:T(8,128)(2,1)S(1)}, u32[]{:S(2)}, u32[]{:S(2)}) collective-permute-start(bf16[6,256,128]{2,1,0:T(8,128)(2,1)S(1)} %get-tuple-element.64), channel_id=1, source_target_pairs={{0,1},{1,2},{2,3},{3,0},{4,5},{5,6},{6,7},{7,4},{8,9},{9,10},{10,1... | collective-permute-start | bytes 1179656 | tf_op jit(solution)/shard_map/ppermute | solution.py:35
  30.9 18.1 %collective-permute-start.10 = (bf16[6,256,128]{2,1,0:T(8,128)(2,1)S(1)}, bf16[6,256,128]{2,1,0:T(8,128)(2,1)S(1)}, u32[]{:S(2)}, u32[]{:S(2)}) collective-permute-start(bf16[6,256,128]{2,1,0:T(8,128)(2,1)S(1)} %add_convert_fusion.1), channel_id=1, source_target_pairs={{0,1},{1,2},{2,3},{3,0},{4,5},{5,6},{6,7},{7,4},{8,9},{9,10},{10,1... | collective-permute-start | bytes 1179656 | tf_op jit(solution)/shard_map/ppermute | solution.py:35
  33.3 15.8 %collective-permute-start.9 = (bf16[6,64,512]{2,1,0:T(8,128)(2,1)S(1)}, bf16[6,64,512]{2,1,0:T(8,128)(2,1)S(1)}, u32[]{:S(2)}, u32[]{:S(2)}) collective-permute-start(bf16[6,64,512]{2,1,0:T(8,128)(2,1)S(1)} %add_convert_fusion.2), channel_id=1, source_target_pairs={{0,192},{4,196},{8,200},{12,204},{16,208},{20,212},{24,216},{28,22... | collective-permute-start | bytes 1179656 | tf_op jit(solution)/shard_map/ppermute | solution.py:26
  34.6 14.7 %collective-permute-start.8 = (bf16[6,64,512]{2,1,0:T(8,128)(2,1)S(1)}, bf16[6,64,512]{2,1,0:T(8,128)(2,1)S(1)}, u32[]{:S(2)}, u32[]{:S(2)}) collective-permute-start(bf16[6,64,512]{2,1,0:T(8,128)(2,1)S(1)} %add_convert_fusion.3), channel_id=1, source_target_pairs={{0,64},{4,68},{8,72},{12,76},{16,80},{20,84},{24,88},{28,92},{32,9... | collective-permute-start | bytes 1179656 | tf_op jit(solution)/shard_map/ppermute | solution.py:26
  38.5 11.2 %collective-permute-start.13 = (bf16[6,256,128]{2,1,0:T(8,128)(2,1)S(1)}, bf16[6,256,128]{2,1,0:T(8,128)(2,1)S(1)}, u32[]{:S(2)}, u32[]{:S(2)}) collective-permute-start(bf16[6,256,128]{2,1,0:T(8,128)(2,1)S(1)} %add_convert_fusion), channel_id=1, source_target_pairs={{0,3},{1,0},{2,1},{3,2},{4,7},{5,4},{6,5},{7,6},{8,11},{9,8},{10,9... | collective-permute-start | bytes 1179656 | tf_op jit(solution)/shard_map/ppermute | solution.py:35
  50.1 7.7 %collective-permute-start.19 = (bf16[12,64,128]{2,1,0:T(8,128)(2,1)S(1)}, bf16[12,64,128]{2,1,0:T(8,128)(2,1)S(1)}, u32[]{:S(2)}, u32[]{:S(2)}) collective-permute-start(bf16[12,64,128]{2,1,0:T(8,128)(2,1)S(1)} %get-tuple-element.73), channel_id=1, source_target_pairs={{0,128},{4,132},{8,136},{12,140},{16,144},{20,148},{24,152},{28,15... | collective-permute-start | bytes 589832 | tf_op jit(solution)/shard_map/ppermute | solution.py:26
  51.4 8.1 %collective-permute-start.18 = (bf16[12,64,128]{2,1,0:T(8,128)(2,1)S(1)}, bf16[12,64,128]{2,1,0:T(8,128)(2,1)S(1)}, u32[]{:S(2)}, u32[]{:S(2)}) collective-permute-start(bf16[12,64,128]{2,1,0:T(8,128)(2,1)S(1)} %get-tuple-element.74), channel_id=1, source_target_pairs={{0,64},{4,68},{8,72},{12,76},{16,80},{20,84},{24,88},{28,92},{32,9... | collective-permute-start | bytes 589832 | tf_op jit(solution)/shard_map/ppermute | solution.py:26
  53.2 6.9 %collective-permute-start.17 = (bf16[12,64,128]{2,1,0:T(8,128)(2,1)S(1)}, bf16[12,64,128]{2,1,0:T(8,128)(2,1)S(1)}, u32[]{:S(2)}, u32[]{:S(2)}) collective-permute-start(bf16[12,64,128]{2,1,0:T(8,128)(2,1)S(1)} %get-tuple-element.72), channel_id=1, source_target_pairs={{0,192},{4,196},{8,200},{12,204},{16,208},{20,212},{24,216},{28,22... | collective-permute-start | bytes 589832 | tf_op jit(solution)/shard_map/ppermute | solution.py:26
  53.6 7.4 %collective-permute-start.16 = (bf16[12,64,128]{2,1,0:T(8,128)(2,1)S(1)}, bf16[12,64,128]{2,1,0:T(8,128)(2,1)S(1)}, u32[]{:S(2)}, u32[]{:S(2)}) collective-permute-start(bf16[12,64,128]{2,1,0:T(8,128)(2,1)S(1)} %get-tuple-element.70), channel_id=1, source_target_pairs={{0,2},{1,3},{2,0},{3,1},{4,6},{5,7},{6,4},{7,5},{8,10},{9,11},{10,... | collective-permute-start | bytes 589832 | tf_op jit(solution)/shard_map/ppermute | solution.py:35
  53.8 9.0 %collective-permute-start.15 = (bf16[12,64,128]{2,1,0:T(8,128)(2,1)S(1)}, bf16[12,64,128]{2,1,0:T(8,128)(2,1)S(1)}, u32[]{:S(2)}, u32[]{:S(2)}) collective-permute-start(bf16[12,64,128]{2,1,0:T(8,128)(2,1)S(1)} %get-tuple-element.71), channel_id=1, source_target_pairs={{0,1},{1,2},{2,3},{3,0},{4,5},{5,6},{6,7},{7,4},{8,9},{9,10},{10,1... | collective-permute-start | bytes 589832 | tf_op jit(solution)/shard_map/ppermute | solution.py:35
  57.8 5.7 %collective-permute-start.14 = (bf16[12,64,128]{2,1,0:T(8,128)(2,1)S(1)}, bf16[12,64,128]{2,1,0:T(8,128)(2,1)S(1)}, u32[]{:S(2)}, u32[]{:S(2)}) collective-permute-start(bf16[12,64,128]{2,1,0:T(8,128)(2,1)S(1)} %get-tuple-element.69), channel_id=1, source_target_pairs={{0,3},{1,0},{2,1},{3,2},{4,7},{5,4},{6,5},{7,6},{8,11},{9,8},{10,9... | collective-permute-start | bytes 589832 | tf_op jit(solution)/shard_map/ppermute | solution.py:35
  64.4 20.4 %all-to-all-start = ((bf16[8,8,24,128]{3,1,2,0:T(8,128)(2,1)}), bf16[8,8,24,128]{3,1,2,0:T(8,128)(2,1)S(1)}, u32[]{:S(2)}, u32[]{:S(2)}) async-start(bf16[8,8,24,128]{3,1,2,0:T(8,128)(2,1)} %fusion), calls=%async_computation | async-start | bytes 786432 | tf_op jit(solution)/shard_map/all_to_all | solution.py:31
